TPU v7x, 32 devices: a whole 2x2x4 slice. The times are simulated.
32 devices in a mesh: obj: 4 (over y, x), seq: 8 (over z, core).
Axes of the slice: x: 2, y: 2, z: 4, core: 2. Of those that a mesh axis runs over, the one named last changes fastest.
Arguments:
- tokens: bfloat16 [8, 1536, 1024], P('obj', 'seq'), may hold values from -6 to 6
- camera: float32 [8, 16], P('obj'), may hold values from -4 to 4
- patches: bfloat16 [8, 1024, 768], P('obj', 'seq'), may hold values from -6 to 6
- patch_count: int32 [8], P('obj'), may hold values from 256 to 1024, as said below
- patch_index: int32 [8, 1024], P('obj', 'seq'), may hold values from 0 to 4095
- cotangent: bfloat16 [8, 1536, 1024], P('obj', 'seq'), may hold values from -6 to 6
- camera_weight: float32 [16, 2048], P(None, ('obj', 'seq')), may hold values from -0.75 to 0.75
- self_weight: float32 [1024, 3072], P(('obj', 'seq')), may hold values from -0.1875 to 0.1875
- self_output: float32 [1024, 1024], P(('obj', 'seq')), may hold values from -4 to 4
- mid_gain: float32 [1024], P(('obj', 'seq')), may hold values from 0.25 to 1.75
- mid_bias: float32 [1024], P(('obj', 'seq')), may hold values from -3 to 3
- patch_weight: float32 [768, 1024], P(('obj', 'seq')), may hold values from -0.21875 to 0.21875
- view_table: float32 [4, 1024], P(None, ('obj', 'seq')), may hold values from -5 to 5
- cross_query: float32 [1024, 1024], P(('obj', 'seq')), may hold values from -0.1875 to 0.1875
- cross_memory: float32 [1024, 2048], P(('obj', 'seq')), may hold values from -0.125 to 0.125
- cross_output: float32 [1024, 1024], P(('obj', 'seq')), may hold values from -2.5 to 2.5
- last_gain: float32 [1024], P(('obj', 'seq')), may hold values from 0.25 to 1.75
- last_bias: float32 [1024], P(('obj', 'seq')), may hold values from -3 to 3
- up_weight: float32 [1024, 4096], P(('obj', 'seq')), may hold values from -0.1875 to 0.1875
- up_bias: float32 [4096], P(('obj', 'seq')), may hold values from -3 to 3
- down_weight: float32 [4096, 1024], P(('obj', 'seq')), may hold values from -0.125 to 0.125
- down_bias: float32 [1024], P(('obj', 'seq')), may hold values from -3 to 3
Outputs:
- result: bfloat16 [8, 1536, 1024], P('obj', 'seq')
- token_grad: bfloat16 [8, 1536, 1024], P('obj', 'seq')
- patch_grad: bfloat16 [8, 1024, 768], P('obj', 'seq')
- camera_weight_grad: float32 [16, 2048], P(None, ('obj', 'seq'))
- self_weight_grad: float32 [1024, 3072], P(('obj', 'seq'))
- self_output_grad: float32 [1024, 1024], P(('obj', 'seq'))
- mid_gain_grad: float32 [1024], P(('obj', 'seq'))
- mid_bias_grad: float32 [1024], P(('obj', 'seq'))
- patch_weight_grad: float32 [768, 1024], P(('obj', 'seq'))
- view_table_grad: float32 [4, 1024], P(None, ('obj', 'seq'))
- cross_query_grad: float32 [1024, 1024], P(('obj', 'seq'))
- cross_memory_grad: float32 [1024, 2048], P(('obj', 'seq'))
- cross_output_grad: float32 [1024, 1024], P(('obj', 'seq'))
- last_gain_grad: float32 [1024], P(('obj', 'seq'))
- last_bias_grad: float32 [1024], P(('obj', 'seq'))
- up_weight_grad: float32 [1024, 4096], P(('obj', 'seq'))
- up_bias_grad: float32 [4096], P(('obj', 'seq'))
- down_weight_grad: float32 [4096, 1024], P(('obj', 'seq'))
- down_bias_grad: float32 [1024], P(('obj', 'seq'))
Inputs may be any that keep to these rules, and one draw needn't show every extreme that they name: Slots j < patch_count of an object hold live patches, the rest padding. In every aligned group of 2 objects one object has all 1024 slots live. A slot's view is patch_index // 1024.
All inputs are finite; a program needn't handle non-finite values.
Results may differ from a plain program's by a relative error of at most 0.023.
Values may be sent and summed in bfloat16 or wider, within the bound.
No kernel may reach another device: no remote copies, remote signals or barrier semaphores. Data moves between devices by JAX's collectives and lax.ppermute only.
A program may use at most 384 MiB of HBM per device.

v0:
```python
from functools import partial

import jax
import jax.numpy as jnp
from jax import lax
from jax.sharding import PartitionSpec as P

HEADS = 16
HEAD_DIM = 64
VIEWS = 4
VIEW_PATCHES = 1024


epsilon = 1e-05


def normalize(values):
    center = values - jnp.mean(values, -1, keepdims=True)
    spread = jnp.mean(center * center, -1, keepdims=True)
    return center * lax.rsqrt(spread + epsilon)


def modulated(values, modulation):
    width = values.shape[-1]
    return normalize(values) * (1.0 + modulation[:, None, :width]) + modulation[:, None, width:]


def affine_norm(values, gain, shift):
    return normalize(values) * gain + shift


def head_slice(matrix, start):
    part = matrix[:, :, start * HEAD_DIM : (start + 2) * HEAD_DIM]
    return part.reshape(matrix.shape[0], matrix.shape[1], 2, HEAD_DIM)


def head_scores(head_query, head_keys, mask):
    factor = HEAD_DIM ** (-0.5)
    raw = (
        jnp.einsum("onhd,omhd->ohnm", head_query, head_keys, preferred_element_type=jnp.float32)
        * factor
    )
    if mask is not None:
        raw = jnp.where(mask[:, None, None, :], raw, -1e30)
    top = jnp.max(raw, -1, keepdims=True)
    total = jnp.sum(jnp.exp(raw - top), -1, keepdims=True)
    return (raw, top, total)


def head_probs(head_query, head_keys, mask):
    raw, top, total = head_scores(head_query, head_keys, mask)
    return jnp.exp(raw - top) / total


def attend_forward(query, keys, values, mask):
    pieces = []
    for start in range(0, HEADS, 2):
        probs = head_probs(head_slice(query, start), head_slice(keys, start), mask).astype(
            jnp.bfloat16
        )
        mixed = jnp.einsum(
            "ohnm,omhd->onhd", probs, head_slice(values, start), preferred_element_type=jnp.float32
        )
        pieces.append(mixed.reshape(mixed.shape[0], mixed.shape[1], 2 * HEAD_DIM))
    return jnp.concatenate(pieces, -1)


def attend_backward(query, keys, values, mask, out_grad):
    factor = HEAD_DIM ** (-0.5)
    query_parts = []
    key_parts = []
    value_parts = []
    for start in range(0, HEADS, 2):
        head_query = head_slice(query, start)
        head_keys = head_slice(keys, start)
        head_values = head_slice(values, start)
        head_grad = head_slice(out_grad, start)
        probs = head_probs(head_query, head_keys, mask)
        prob_grad = jnp.einsum(
            "onhd,omhd->ohnm", head_grad, head_values, preferred_element_type=jnp.float32
        )
        delta = jnp.sum(probs * prob_grad, -1, keepdims=True)
        score_grad = (probs * (prob_grad - delta)).astype(jnp.bfloat16)
        query_grad = (
            jnp.einsum("ohnm,omhd->onhd", score_grad, head_keys, preferred_element_type=jnp.float32)
            * factor
        )
        key_grad = (
            jnp.einsum(
                "ohnm,onhd->omhd", score_grad, head_query, preferred_element_type=jnp.float32
            )
            * factor
        )
        value_grad = jnp.einsum(
            "ohnm,onhd->omhd",
            probs.astype(jnp.bfloat16),
            head_grad,
            preferred_element_type=jnp.float32,
        )
        query_parts.append(
            query_grad.reshape(query_grad.shape[0], query_grad.shape[1], 2 * HEAD_DIM)
        )
        key_parts.append(key_grad.reshape(key_grad.shape[0], key_grad.shape[1], 2 * HEAD_DIM))
        value_parts.append(
            value_grad.reshape(value_grad.shape[0], value_grad.shape[1], 2 * HEAD_DIM)
        )
    pair_grad = jnp.concatenate(
        [jnp.concatenate(key_parts, -1), jnp.concatenate(value_parts, -1)], -1
    )
    return (jnp.concatenate(query_parts, -1), pair_grad)


def forward(tokens, camera, patches, patch_count, patch_index, shards):
    (
        camera_weight,
        self_weight,
        self_output,
        mid_gain,
        mid_bias,
        patch_weight,
        view_table,
        cross_query,
        cross_memory,
        cross_output,
        last_gain,
        last_bias,
        up_weight,
        up_bias,
        down_weight,
        down_bias,
    ) = tuple((shard.astype(jnp.bfloat16) for shard in shards))
    (
        camera_weight,
        self_weight,
        self_output,
        mid_gain,
        mid_bias,
        patch_weight,
        view_table,
        cross_query,
        cross_memory,
        cross_output,
        last_gain,
        last_bias,
        up_weight,
        up_bias,
        down_weight,
        down_bias,
    ) = (
        lax.all_gather(camera_weight, ("obj", "seq"), axis=1, tiled=True),
        lax.all_gather(self_weight, ("obj", "seq"), axis=0, tiled=True),
        lax.all_gather(self_output, ("obj", "seq"), axis=0, tiled=True),
        lax.all_gather(mid_gain, ("obj", "seq"), axis=0, tiled=True),
        lax.all_gather(mid_bias, ("obj", "seq"), axis=0, tiled=True),
        lax.all_gather(patch_weight, ("obj", "seq"), axis=0, tiled=True),
        lax.all_gather(view_table, ("obj", "seq"), axis=1, tiled=True),
        lax.all_gather(cross_query, ("obj", "seq"), axis=0, tiled=True),
        lax.all_gather(cross_memory, ("obj", "seq"), axis=0, tiled=True),
        lax.all_gather(cross_output, ("obj", "seq"), axis=0, tiled=True),
        lax.all_gather(last_gain, ("obj", "seq"), axis=0, tiled=True),
        lax.all_gather(last_bias, ("obj", "seq"), axis=0, tiled=True),
        lax.all_gather(up_weight, ("obj", "seq"), axis=0, tiled=True),
        lax.all_gather(up_bias, ("obj", "seq"), axis=0, tiled=True),
        lax.all_gather(down_weight, ("obj", "seq"), axis=0, tiled=True),
        lax.all_gather(down_bias, ("obj", "seq"), axis=0, tiled=True),
    )
    width = self_output.shape[0]
    inputs = tokens.astype(jnp.float32)
    modulation = jnp.dot(camera, camera_weight.astype(jnp.float32), precision=lax.Precision.HIGHEST)
    hidden = modulated(inputs, modulation).astype(jnp.bfloat16)
    queries = jnp.einsum(
        "ond,de->one", hidden, self_weight[:, :width], preferred_element_type=jnp.float32
    ).astype(jnp.bfloat16)
    local_pairs = jnp.einsum(
        "ond,de->one", hidden, self_weight[:, width:], preferred_element_type=jnp.float32
    ).astype(jnp.bfloat16)
    self_pairs = lax.all_gather(local_pairs, "seq", axis=1, tiled=True)
    views = patch_index // VIEW_PATCHES
    view_hot = (views[:, :, None] == jnp.arange(VIEWS)[None, None, :]).astype(jnp.float32)
    embedded = (
        jnp.einsum("opc,cd->opd", patches, patch_weight, preferred_element_type=jnp.float32)
        + jnp.einsum(
            "opv,vd->opd", view_hot, view_table.astype(jnp.float32), precision=lax.Precision.HIGHEST
        )
    ).astype(jnp.bfloat16)
    memory = jnp.einsum(
        "opd,de->ope", embedded, cross_memory, preferred_element_type=jnp.float32
    ).astype(jnp.bfloat16)
    cross_pairs = lax.all_gather(memory, "seq", axis=1, tiled=True)
    attended = attend_forward(
        queries, self_pairs[:, :, :width], self_pairs[:, :, width:], None
    ).astype(jnp.bfloat16)
    second = inputs + jnp.einsum(
        "ond,de->one", attended, self_output, preferred_element_type=jnp.float32
    )
    normed = affine_norm(second, mid_gain.astype(jnp.float32), mid_bias.astype(jnp.float32)).astype(
        jnp.bfloat16
    )
    asked = jnp.einsum(
        "ond,de->one", normed, cross_query, preferred_element_type=jnp.float32
    ).astype(jnp.bfloat16)
    live = jnp.arange(cross_pairs.shape[1])[None, :] < patch_count[:, None]
    crossed = attend_forward(
        asked, cross_pairs[:, :, :width], cross_pairs[:, :, width:], live
    ).astype(jnp.bfloat16)
    third = second + jnp.einsum(
        "ond,de->one", crossed, cross_output, preferred_element_type=jnp.float32
    )
    final = affine_norm(third, last_gain.astype(jnp.float32), last_bias.astype(jnp.float32)).astype(
        jnp.bfloat16
    )
    upper = jnp.einsum(
        "ond,df->onf", final, up_weight, preferred_element_type=jnp.float32
    ) + up_bias.astype(jnp.float32)
    active = jax.nn.gelu(upper, approximate=False).astype(jnp.bfloat16)
    result = third + (
        jnp.einsum("onf,fd->ond", active, down_weight, preferred_element_type=jnp.float32)
        + down_bias.astype(jnp.float32)
    )
    weights = (
        camera_weight,
        self_weight,
        self_output,
        mid_gain,
        mid_bias,
        patch_weight,
        view_table,
        cross_query,
        cross_memory,
        cross_output,
        last_gain,
        last_bias,
        up_weight,
        up_bias,
        down_weight,
        down_bias,
    )
    saved = dict(
        inputs=inputs,
        modulation=modulation,
        hidden=hidden,
        queries=queries,
        self_pairs=self_pairs,
        attended=attended,
        second=second,
        normed=normed,
        asked=asked,
        live=live,
        cross_pairs=cross_pairs,
        crossed=crossed,
        third=third,
        final=final,
        upper=upper,
        active=active,
        embedded=embedded,
        view_hot=view_hot,
        weights=weights,
    )
    return (result, saved)


def on_device(
    tokens,
    camera,
    patches,
    patch_count,
    patch_index,
    cotangent,
    camera_weight,
    self_weight,
    self_output,
    mid_gain,
    mid_bias,
    patch_weight,
    view_table,
    cross_query,
    cross_memory,
    cross_output,
    last_gain,
    last_bias,
    up_weight,
    up_bias,
    down_weight,
    down_bias,
):
    shards = (
        camera_weight,
        self_weight,
        self_output,
        mid_gain,
        mid_bias,
        patch_weight,
        view_table,
        cross_query,
        cross_memory,
        cross_output,
        last_gain,
        last_bias,
        up_weight,
        up_bias,
        down_weight,
        down_bias,
    )
    result, saved = forward(tokens, camera, patches, patch_count, patch_index, shards)
    tokens_again, camera_again, patches_again, count_again, index_again, shards_again = (
        lax.optimization_barrier((tokens, camera, patches, patch_count, patch_index, shards))
    )
    unused, saved = forward(
        tokens_again, camera_again, patches_again, count_again, index_again, shards_again
    )
    (
        full_camera,
        full_self,
        full_self_out,
        full_mid_gain,
        full_mid_bias,
        full_patch,
        full_view,
        full_query,
        full_memory,
        full_cross_out,
        full_last_gain,
        full_last_bias,
        full_up,
        full_up_bias,
        full_down,
        full_down_bias,
    ) = saved["weights"]
    width = full_self_out.shape[0]
    grad_out = cotangent.astype(jnp.float32)
    down_bias_grad = jnp.sum(cotangent.astype(jnp.float32), axis=(0, 1))
    down_weight_grad = jnp.einsum(
        "onf,ond->fd", saved["active"], cotangent, preferred_element_type=jnp.float32
    )
    active_grad = jnp.einsum(
        "ond,fd->onf", cotangent, full_down, preferred_element_type=jnp.float32
    )
    unused_gelu, gelu_pull = jax.vjp(partial(jax.nn.gelu, approximate=False), saved["upper"])
    upper_grad = gelu_pull(active_grad)[0].astype(jnp.bfloat16)
    up_bias_grad = jnp.sum(upper_grad.astype(jnp.float32), axis=(0, 1))
    up_weight_grad = jnp.einsum(
        "ond,onf->df", saved["final"], upper_grad, preferred_element_type=jnp.float32
    )
    final_grad = jnp.einsum("onf,df->ond", upper_grad, full_up, preferred_element_type=jnp.float32)
    unused_last, last_pull = jax.vjp(
        affine_norm,
        saved["third"],
        full_last_gain.astype(jnp.float32),
        full_last_bias.astype(jnp.float32),
    )
    third_part, last_gain_grad, last_bias_grad = last_pull(final_grad)
    third_grad = grad_out + third_part
    third_low = third_grad.astype(jnp.bfloat16)
    cross_output_grad = jnp.einsum(
        "ond,one->de", saved["crossed"], third_low, preferred_element_type=jnp.float32
    )
    crossed_grad = jnp.einsum(
        "one,de->ond", third_low, full_cross_out, preferred_element_type=jnp.float32
    ).astype(jnp.bfloat16)
    cross_pairs = saved["cross_pairs"]
    asked_grad, memory_terms = attend_backward(
        saved["asked"],
        cross_pairs[:, :, :width],
        cross_pairs[:, :, width:],
        saved["live"],
        crossed_grad,
    )
    memory_grad = lax.psum_scatter(
        memory_terms.astype(jnp.bfloat16), "seq", scatter_dimension=1, tiled=True
    )
    asked_low = asked_grad.astype(jnp.bfloat16)
    cross_query_grad = jnp.einsum(
        "ond,one->de", saved["normed"], asked_low, preferred_element_type=jnp.float32
    )
    normed_grad = jnp.einsum(
        "one,de->ond", asked_low, full_query, preferred_element_type=jnp.float32
    )
    cross_memory_grad = jnp.einsum(
        "opd,ope->de", saved["embedded"], memory_grad, preferred_element_type=jnp.float32
    )
    embedded_grad = jnp.einsum(
        "ope,de->opd", memory_grad, full_memory, preferred_element_type=jnp.float32
    ).astype(jnp.bfloat16)
    patch_weight_grad = jnp.einsum(
        "opc,opd->cd", patches, embedded_grad, preferred_element_type=jnp.float32
    )
    view_table_grad = jnp.einsum(
        "opv,opd->vd",
        saved["view_hot"],
        embedded_grad.astype(jnp.float32),
        precision=lax.Precision.HIGHEST,
    )
    patch_grad = jnp.einsum(
        "opd,cd->opc", embedded_grad, full_patch, preferred_element_type=jnp.float32
    ).astype(jnp.bfloat16)
    unused_mid, mid_pull = jax.vjp(
        affine_norm,
        saved["second"],
        full_mid_gain.astype(jnp.float32),
        full_mid_bias.astype(jnp.float32),
    )
    second_part, mid_gain_grad, mid_bias_grad = mid_pull(normed_grad)
    second_grad = third_grad + second_part
    second_low = second_grad.astype(jnp.bfloat16)
    self_output_grad = jnp.einsum(
        "ond,one->de", saved["attended"], second_low, preferred_element_type=jnp.float32
    )
    attended_grad = jnp.einsum(
        "one,de->ond", second_low, full_self_out, preferred_element_type=jnp.float32
    ).astype(jnp.bfloat16)
    self_pairs = saved["self_pairs"]
    query_grad, pair_terms = attend_backward(
        saved["queries"], self_pairs[:, :, :width], self_pairs[:, :, width:], None, attended_grad
    )
    pair_grad = lax.psum_scatter(
        pair_terms.astype(jnp.bfloat16), "seq", scatter_dimension=1, tiled=True
    )
    triple_grad = jnp.concatenate([query_grad.astype(jnp.bfloat16), pair_grad], -1)
    self_weight_grad = jnp.einsum(
        "ond,one->de", saved["hidden"], triple_grad, preferred_element_type=jnp.float32
    )
    hidden_grad = jnp.einsum(
        "one,de->ond", triple_grad, full_self, preferred_element_type=jnp.float32
    )
    unused_first, first_pull = jax.vjp(modulated, saved["inputs"], saved["modulation"])
    inputs_part, modulation_grad = first_pull(hidden_grad)
    camera_weight_grad = jnp.dot(camera.T, modulation_grad, precision=lax.Precision.HIGHEST)
    token_grad = (second_grad + inputs_part).astype(jnp.bfloat16)
    (
        camera_weight_grad,
        self_weight_grad,
        self_output_grad,
        mid_gain_grad,
        mid_bias_grad,
        patch_weight_grad,
        view_table_grad,
        cross_query_grad,
        cross_memory_grad,
        cross_output_grad,
        last_gain_grad,
        last_bias_grad,
        up_weight_grad,
        up_bias_grad,
        down_weight_grad,
        down_bias_grad,
    ) = (
        lax.psum_scatter(camera_weight_grad, ("obj", "seq"), scatter_dimension=1, tiled=True),
        lax.psum_scatter(self_weight_grad, ("obj", "seq"), scatter_dimension=0, tiled=True),
        lax.psum_scatter(self_output_grad, ("obj", "seq"), scatter_dimension=0, tiled=True),
        lax.psum_scatter(mid_gain_grad, ("obj", "seq"), scatter_dimension=0, tiled=True),
        lax.psum_scatter(mid_bias_grad, ("obj", "seq"), scatter_dimension=0, tiled=True),
        lax.psum_scatter(patch_weight_grad, ("obj", "seq"), scatter_dimension=0, tiled=True),
        lax.psum_scatter(view_table_grad, ("obj", "seq"), scatter_dimension=1, tiled=True),
        lax.psum_scatter(cross_query_grad, ("obj", "seq"), scatter_dimension=0, tiled=True),
        lax.psum_scatter(cross_memory_grad, ("obj", "seq"), scatter_dimension=0, tiled=True),
        lax.psum_scatter(cross_output_grad, ("obj", "seq"), scatter_dimension=0, tiled=True),
        lax.psum_scatter(last_gain_grad, ("obj", "seq"), scatter_dimension=0, tiled=True),
        lax.psum_scatter(last_bias_grad, ("obj", "seq"), scatter_dimension=0, tiled=True),
        lax.psum_scatter(up_weight_grad, ("obj", "seq"), scatter_dimension=0, tiled=True),
        lax.psum_scatter(up_bias_grad, ("obj", "seq"), scatter_dimension=0, tiled=True),
        lax.psum_scatter(down_weight_grad, ("obj", "seq"), scatter_dimension=0, tiled=True),
        lax.psum_scatter(down_bias_grad, ("obj", "seq"), scatter_dimension=0, tiled=True),
    )
    return (
        result.astype(jnp.bfloat16),
        token_grad,
        patch_grad,
        camera_weight_grad,
        self_weight_grad,
        self_output_grad,
        mid_gain_grad,
        mid_bias_grad,
        patch_weight_grad,
        view_table_grad,
        cross_query_grad,
        cross_memory_grad,
        cross_output_grad,
        last_gain_grad,
        last_bias_grad,
        up_weight_grad,
        up_bias_grad,
        down_weight_grad,
        down_bias_grad,
    )


def solution(mesh):
    in_specs = (
        P("obj", "seq", None),
        P("obj", None),
        P("obj", "seq", None),
        P("obj"),
        P("obj", "seq"),
        P("obj", "seq", None),
        P(None, ("obj", "seq")),
        P(("obj", "seq"), None),
        P(("obj", "seq"), None),
        P(("obj", "seq")),
        P(("obj", "seq")),
        P(("obj", "seq"), None),
        P(None, ("obj", "seq")),
        P(("obj", "seq"), None),
        P(("obj", "seq"), None),
        P(("obj", "seq"), None),
        P(("obj", "seq")),
        P(("obj", "seq")),
        P(("obj", "seq"), None),
        P(("obj", "seq")),
        P(("obj", "seq"), None),
        P(("obj", "seq")),
    )
    out_specs = (
        P("obj", "seq", None),
        P("obj", "seq", None),
        P("obj", "seq", None),
        P(None, ("obj", "seq")),
        P(("obj", "seq"), None),
        P(("obj", "seq"), None),
        P(("obj", "seq")),
        P(("obj", "seq")),
        P(("obj", "seq"), None),
        P(None, ("obj", "seq")),
        P(("obj", "seq"), None),
        P(("obj", "seq"), None),
        P(("obj", "seq"), None),
        P(("obj", "seq")),
        P(("obj", "seq")),
        P(("obj", "seq"), None),
        P(("obj", "seq")),
        P(("obj", "seq"), None),
        P(("obj", "seq")),
    )
    return jax.shard_map(
        on_device, mesh=mesh, in_specs=in_specs, out_specs=out_specs, check_vma=False
    )
```

profile of v0, /device:TPU:0, one launch (start us, length us, event | category | flops | bytes accessed | tf_op | source)
XLA Modules:
  0.0 3217.0 jit_solution(3161194726997001109)
XLA Ops:
  13.0 43.3 %all-gather.4 = bf16[32,32,4]{1,2,0:T(4,128)(2,1)S(1)} all-gather(bf16[1,32,4]{1,2,0:T(4,128)(2,1)S(1)} %convert_bitcast_fusion.2), channel_id=1, replica_groups=mesh['obj'=4,'seq'=8] {'obj','seq'}, dimensions={0}, use_global_device_ids=true | all-gather | bytes 8448 | tf_op jit(solution)/shard_map/all_gather | solution.py:156
  57.1 12.3 all-gather.53.cloned.1.call-done
  71.9 62.2 %all-gather.55.cloned.1.call-done = bf16[1024,2048]{1,0:T(8,128)(2,1)} async-done(((bf16[32,2048]{1,0:T(8,128)(2,1)}), bf16[1024,2048]{1,0:T(8,128)(2,1)}) %all-gather.55.cloned.1.call-update) | async-done | bytes 4194320 | tf_op jit(solution)/shard_map/all_gather | solution.py:158
  138.6 40.0 %all-gather.3 = bf16[32,64,16]{1,2,0:T(8,128)(2,1)S(1)} all-gather(bf16[1,64,16]{1,2,0:T(8,128)(2,1)S(1)} %convert_bitcast_fusion), channel_id=1, replica_groups=mesh['obj'=4,'seq'=8] {'obj','seq'}, dimensions={0}, use_global_device_ids=true | all-gather | bytes 67584 | tf_op jit(solution)/shard_map/all_gather | solution.py:150
  180.2 25.8 all-gather.47.cloned.1.call-done
  219.7 44.2 %all-reduce.18 = (bf16[1024]{0:T(1024)(128)(2,1)}, bf16[1024]{0:T(1024)(128)(2,1)}, bf16[1024]{0:T(1024)(128)(2,1)}, bf16[1024]{0:T(1024)(128)(2,1)}, bf16[1024]...) all-reduce(bf16[1024]{0:T(1024)(128)(2,1)S(1)} %dynamic-update-slic, ...), channel_id=1, replica_groups=mesh['obj'=4,'seq'=8] {'obj','seq'}, use_global_device_ids=true, to_apply=%add.3 | all-reduce | flops 9216 | bytes 36864
  264.6 39.5 %all-gather.5 = bf16[32,1,128]{2,1,0:T(2,128)(2,1)S(1)} all-gather(bf16[1,1,128]{2,1,0:T(2,128)(2,1)S(1)} %convert_bitcast_fusion.4), channel_id=1, replica_groups=mesh['obj'=4,'seq'=8] {'obj','seq'}, dimensions={0}, use_global_device_ids=true | all-gather | bytes 8448 | tf_op jit(solution)/shard_map/all_gather | solution.py:163
  349.7 56.2 %all-gather.49.cloned.1.call-done = bf16[2,1536,2048]{2,1,0:T(8,128)(2,1)} async-done(((bf16[2,192,2048]{2,1,0:T(8,128)(2,1)}), bf16[2,1536,2048]{2,1,0:T(8,128)(2,1)}) %all-gather.49.cloned.1.call-update) | async-done | bytes 12582928 | tf_op jit(solution)/shard_map/all_gather | solution.py:177
  618.1 42.1 %all-gather.63.cloned.1.call-done = bf16[1024,4096]{1,0:T(8,128)(2,1)} async-done(((bf16[32,4096]{1,0:T(8,128)(2,1)}), bf16[1024,4096]{1,0:T(8,128)(2,1)}) %all-gather.63.cloned.1.call-update) | async-done | bytes 8388624 | tf_op jit(solution)/shard_map/all_gather | solution.py:162
  671.8 14.6 fusion.45
  686.4 53.2 %all-gather.65.cloned.1.call-done = bf16[4096,1024]{1,0:T(8,128)(2,1)} async-done(((bf16[128,1024]{1,0:T(8,128)(2,1)}), bf16[4096,1024]{1,0:T(8,128)(2,1)}) %all-gather.65.cloned.1.call-update) | async-done | bytes 8388624 | tf_op jit(solution)/shard_map/all_gather | solution.py:164
  739.6 13.5 convert_reduce_fusion
  1061.0 40.1 %all-gather.1 = bf16[32,32,4]{1,2,0:T(4,128)(2,1)S(1)} all-gather(bf16[1,32,4]{1,2,0:T(4,128)(2,1)S(1)} %convert_bitcast_fusion.3), channel_id=1, replica_groups=mesh['obj'=4,'seq'=8] {'obj','seq'}, dimensions={0}, use_global_device_ids=true | all-gather | bytes 8448 | tf_op jit(solution)/shard_map/all_gather | solution.py:156
  1108.4 39.5 %all-gather = bf16[32,64,16]{1,2,0:T(8,128)(2,1)S(1)} all-gather(bf16[1,64,16]{1,2,0:T(8,128)(2,1)S(1)} %convert_bitcast_fusion.1), channel_id=1, replica_groups=mesh['obj'=4,'seq'=8] {'obj','seq'}, dimensions={0}, use_global_device_ids=true | all-gather | bytes 67584 | tf_op jit(solution)/shard_map/all_gather | solution.py:150
  1252.2 10.3 convolution_bitcast_fusion.1
  1263.6 12.9 convolution_bitcast_fusion
  1278.4 38.4 %all-gather.2 = bf16[32,1,128]{2,1,0:T(2,128)(2,1)S(1)} all-gather(bf16[1,1,128]{2,1,0:T(2,128)(2,1)S(1)} %convert_bitcast_fusion.5), channel_id=1, replica_groups=mesh['obj'=4,'seq'=8] {'obj','seq'}, dimensions={0}, use_global_device_ids=true | all-gather | bytes 8448 | tf_op jit(solution)/shard_map/all_gather | solution.py:163
  1364.2 25.1 all-gather.29.cloned.1.call-done
  1595.3 40.8 %all-reduce.17 = (f32[1024]{0:T(1024)S(1)}, f32[1024]{0:T(1024)S(1)}, f32[1024]{0:T(1024)S(1)}, f32[1024]{0:T(1024)S(1)}, f32[4096]{0:T(1024)S(1)}, /*index=5*/f32[1024]{0:T(1024)S(1)}) all-reduce(f32[1024]{0:T(1024)S(1)} %copy-done.209, f32[1024]{0:T(1024)S(1)} %copy-done.271, ...), channel_id=7, replica_groups=mesh['obj'=4,'seq'=8] {'obj','seq'}, use_global_device_ids=true, to_apply=%region_106.107.clone | all-reduce | flops 9216 | bytes 73728
  1651.3 13.4 fusion.263
  1664.7 57.9 %all-gather.45.cloned.1.call-done = bf16[4096,1024]{1,0:T(8,128)(2,1)} async-done(((bf16[128,1024]{1,0:T(8,128)(2,1)}), bf16[4096,1024]{1,0:T(8,128)(2,1)}) %all-gather.45.cloned.1.call-update) | async-done | bytes 8388624 | tf_op jit(solution)/shard_map/all_gather | solution.py:164
  1722.6 20.7 add_convert_fusion.3
  1744.7 112.6 %reduce-scatter.41.cloned.1.call-done = f32[32,4]{1,0:T(8,128)} async-done(((f32[1024,4]{1,0:T(8,128)}), f32[32,4]{1,0:T(8,128)}) %reduce-scatter.41.cloned.1.call-update) | async-done | bytes 528
  1861.5 129.3 %reduce-scatter.37.cloned.1.call-done = f32[64,16]{1,0:T(8,128)} async-done(((f32[2048,16]{1,0:T(8,128)}), f32[64,16]{1,0:T(8,128)}) %reduce-scatter.37.cloned.1.call-update) | async-done | bytes 4112
  1992.2 140.4 %reduce-scatter.25.cloned.1.call-done = f32[32,1024]{1,0:T(8,128)} async-done(((f32[1024,1024]{1,0:T(8,128)}), f32[32,1024]{1,0:T(8,128)}) %reduce-scatter.25.cloned.1.call-update) | async-done | bytes 131088 | tf_op jit(solution)/shard_map/reduce_scatter | solution.py:449
  2132.6 142.3 %reduce-scatter.27.cloned.1.call-done = f32[32,1024]{1,0:T(8,128)} async-done(((f32[1024,1024]{1,0:T(8,128)}), f32[32,1024]{1,0:T(8,128)}) %reduce-scatter.27.cloned.1.call-update) | async-done | bytes 131088 | tf_op jit(solution)/shard_map/reduce_scatter | solution.py:454
  2274.9 142.2 %reduce-scatter.31.cloned.1.call-done = f32[32,1024]{1,0:T(8,128)} async-done(((f32[1024,1024]{1,0:T(8,128)}), f32[32,1024]{1,0:T(8,128)}) %reduce-scatter.31.cloned.1.call-update) | async-done | bytes 131088 | tf_op jit(solution)/shard_map/reduce_scatter | solution.py:456
  2417.1 104.5 %reduce-scatter.39.cloned.1.call-done = f32[24,1024]{1,0:T(8,128)} async-done(((f32[768,1024]{1,0:T(8,128)}), f32[24,1024]{1,0:T(8,128)}) %reduce-scatter.39.cloned.1.call-update) | async-done | bytes 98320
  2521.6 154.0 %reduce-scatter.29.cloned.1.call-done = f32[32,2048]{1,0:T(8,128)} async-done(((f32[1024,2048]{1,0:T(8,128)}), f32[32,2048]{1,0:T(8,128)}) %reduce-scatter.29.cloned.1.call-update) | async-done | bytes 262160 | tf_op jit(solution)/shard_map/reduce_scatter | solution.py:455
  2675.6 187.1 %reduce-scatter.33.cloned.1.call-done = f32[32,4096]{1,0:T(8,128)} async-done(((f32[1024,4096]{1,0:T(8,128)}), f32[32,4096]{1,0:T(8,128)}) %reduce-scatter.33.cloned.1.call-update) | async-done | bytes 524304 | tf_op jit(solution)/shard_map/reduce_scatter | solution.py:459
  2862.7 187.3 %reduce-scatter.35.cloned.1.call-done = f32[128,1024]{1,0:T(8,128)} async-done(((f32[4096,1024]{1,0:T(8,128)}), f32[128,1024]{1,0:T(8,128)}) %reduce-scatter.35.cloned.1.call-update) | async-done | bytes 524304 | tf_op jit(solution)/shard_map/reduce_scatter | solution.py:461
  3050.0 160.1 %reduce-scatter.23.cloned.1.call-done = f32[32,3072]{1,0:T(8,128)} async-done(((f32[1024,3072]{1,0:T(8,128)}), f32[32,3072]{1,0:T(8,128)}) %reduce-scatter.23.cloned.1.call-update) | async-done | bytes 393232 | tf_op jit(solution)/shard_map/reduce_scatter | solution.py:448
  (1296 shorter events, 993.6 us)
Async XLA Ops:
  7.2 62.2 %all-gather.53.cloned.1.call-start = ((), (), s32[]{:S(2)}) async-start(), calls=%async_computation.25 | async-start | bytes 1622016 | tf_op jit(solution)/shard_map/all_gather | solution.py:155
  8.8 125.2 %all-gather.55.cloned.1.call-start = ((), (), s32[]{:S(2)}) async-start(), calls=%async_computation.26 | async-start | bytes 4325376 | tf_op jit(solution)/shard_map/all_gather | solution.py:158
  10.5 195.4 %all-gather.47.cloned.1.call-start = ((), (), s32[]{:S(2)}) async-start(), calls=%async_computation.22 | async-start | bytes 6488064 | tf_op jit(solution)/shard_map/all_gather | solution.py:151
  12.3 302.0 %all-gather.57.cloned.1.call-start = ((), (), s32[]{:S(2)}) async-start(), calls=%async_computation.27 | async-start | bytes 9437184 | tf_op jit(solution)/shard_map/all_gather | solution.py:189
  138.5 267.3 %all-gather.49.cloned.1.call-start = ((), (), s32[]{:S(2)}) async-start(), calls=%async_computation.23 | async-start | bytes 14155776 | tf_op jit(solution)/shard_map/all_gather | solution.py:177
  211.5 323.3 %all-gather.51.cloned.1.call-start = ((), (), s32[]{:S(2)}) async-start(), calls=%async_computation.24 | async-start | bytes 2162688 | tf_op jit(solution)/shard_map/all_gather | solution.py:152
  212.2 325.9 %all-gather.59.cloned.1.call-start = ((), (), s32[]{:S(2)}) async-start(), calls=%async_computation.28 | async-start | bytes 2162688 | tf_op jit(solution)/shard_map/all_gather | solution.py:157
  212.9 400.7 %all-gather.61.cloned.1.call-start = ((), (), s32[]{:S(2)}) async-start(), calls=%async_computation.29 | async-start | bytes 2162688 | tf_op jit(solution)/shard_map/all_gather | solution.py:159
  213.7 446.5 %all-gather.63.cloned.1.call-start = ((), (), s32[]{:S(2)}) async-start(), calls=%async_computation.30 | async-start | bytes 8650752 | tf_op jit(solution)/shard_map/all_gather | solution.py:162
  214.5 525.1 %all-gather.65.cloned.1.call-start = ((), (), s32[]{:S(2)}) async-start(), calls=%async_computation.31 | async-start | bytes 8650752 | tf_op jit(solution)/shard_map/all_gather | solution.py:164
  215.3 885.9 %all-gather.33.cloned.1.call-start = ((), (), s32[]{:S(2)}) async-start(), calls=%async_computation.15 | async-start | bytes 1622016 | tf_op jit(solution)/shard_map/all_gather | solution.py:155
  216.1 887.6 %all-gather.35.cloned.1.call-start = ((), (), s32[]{:S(2)}) async-start(), calls=%async_computation.16 | async-start | bytes 4325376 | tf_op jit(solution)/shard_map/all_gather | solution.py:158
  216.8 932.1 %all-gather.27.cloned.1.call-start = ((), (), s32[]{:S(2)}) async-start(), calls=%async_computation.12 | async-start | bytes 6488064 | tf_op jit(solution)/shard_map/all_gather | solution.py:151
  217.6 987.3 %reduce-scatter.21.cloned.1.call-start = ((), (), s32[]{:S(2)}) async-start(), calls=%async_computation.33 | async-start | bytes 9437184 | tf_op jit(solution)/shard_map/reduce_scatter | solution.py:368
  948.6 261.5 %reduce-scatter.19.cloned.1.call-start = ((), (), s32[]{:S(2)}) async-start(), calls=%async_computation.32 | async-start | bytes 14155776 | tf_op jit(solution)/shard_map/reduce_scatter | solution.py:415
  1060.3 268.5 %all-gather.37.cloned.1.call-start = ((), (), s32[]{:S(2)}) async-start(), calls=%async_computation.17 | async-start | bytes 9437184 | tf_op jit(solution)/shard_map/all_gather | solution.py:189
  1108.3 280.9 %all-gather.29.cloned.1.call-start = ((), (), s32[]{:S(2)}) async-start(), calls=%async_computation.13 | async-start | bytes 14155776 | tf_op jit(solution)/shard_map/all_gather | solution.py:177
  1154.8 354.3 %all-gather.31.cloned.1.call-start = ((), (), s32[]{:S(2)}) async-start(), calls=%async_computation.14 | async-start | bytes 2162688 | tf_op jit(solution)/shard_map/all_gather | solution.py:152
  1156.6 355.6 %all-gather.39.cloned.1.call-start = ((), (), s32[]{:S(2)}) async-start(), calls=%async_computation.18 | async-start | bytes 2162688 | tf_op jit(solution)/shard_map/all_gather | solution.py:157
  1158.2 488.9 %all-gather.41.cloned.1.call-start = ((), (), s32[]{:S(2)}) async-start(), calls=%async_computation.19 | async-start | bytes 2162688 | tf_op jit(solution)/shard_map/all_gather | solution.py:159
  1159.8 491.5 %all-gather.43.cloned.1.call-start = ((), (), s32[]{:S(2)}) async-start(), calls=%async_computation.20 | async-start | bytes 8650752 | tf_op jit(solution)/shard_map/all_gather | solution.py:162
  1161.7 560.9 %all-gather.45.cloned.1.call-start = ((), (), s32[]{:S(2)}) async-start(), calls=%async_computation.21 | async-start | bytes 8650752 | tf_op jit(solution)/shard_map/all_gather | solution.py:164
  1163.5 693.8 %reduce-scatter.41.cloned.1.call-start = ((), (), s32[]{:S(2)}) async-start(), calls=%async_computation.43 | async-start | bytes 540672
  1210.0 780.8 %reduce-scatter.37.cloned.1.call-start = ((), (), s32[]{:S(2)}) async-start(), calls=%async_computation.41 | async-start | bytes 1081344
  1223.0 909.6 %reduce-scatter.25.cloned.1.call-start = ((), (), s32[]{:S(2)}) async-start(), calls=%async_computation.35 | async-start | bytes 4325376 | tf_op jit(solution)/shard_map/reduce_scatter | solution.py:449
  1227.5 1047.4 %reduce-scatter.27.cloned.1.call-start = ((), (), s32[]{:S(2)}) async-start(), calls=%async_computation.36 | async-start | bytes 4325376 | tf_op jit(solution)/shard_map/reduce_scatter | solution.py:454
  1233.6 1183.6 %reduce-scatter.31.cloned.1.call-start = ((), (), s32[]{:S(2)}) async-start(), calls=%async_computation.38 | async-start | bytes 4325376 | tf_op jit(solution)/shard_map/reduce_scatter | solution.py:456
  1238.3 1283.3 %reduce-scatter.39.cloned.1.call-start = ((), (), s32[]{:S(2)}) async-start(), calls=%async_computation.42 | async-start | bytes 3244032
  1244.8 1430.8 %reduce-scatter.29.cloned.1.call-start = ((), (), s32[]{:S(2)}) async-start(), calls=%async_computation.37 | async-start | bytes 8650752 | tf_op jit(solution)/shard_map/reduce_scatter | solution.py:455
  1250.8 1611.9 %reduce-scatter.33.cloned.1.call-start = ((), (), s32[]{:S(2)}) async-start(), calls=%async_computation.39 | async-start | bytes 17301504 | tf_op jit(solution)/shard_map/reduce_scatter | solution.py:459
  1262.5 1787.5 %reduce-scatter.35.cloned.1.call-start = ((), (), s32[]{:S(2)}) async-start(), calls=%async_computation.40 | async-start | bytes 17301504 | tf_op jit(solution)/shard_map/reduce_scatter | solution.py:461
  1276.6 1933.4 %reduce-scatter.23.cloned.1.call-start = ((), (), s32[]{:S(2)}) async-start(), calls=%async_computation.34 | async-start | bytes 12976128 | tf_op jit(solution)/shard_map/reduce_scatter | solution.py:448
  (316 other events, 5934.8 us)
Sparse Core Ops, SparseCore 0:
  11.6 57.7 all-gather.52
  73.0 60.9 all-gather.54
  137.6 68.2 all-gather.46
  207.4 81.6 all-gather.56
  290.5 115.2 all-gather.48
  408.7 54.6 all-gather.50
  466.4 55.3 all-gather.58
  524.7 55.3 all-gather.60
  583.7 76.4 all-gather.62
  663.5 75.9 all-gather.64
  742.6 53.6 all-gather.32
  799.8 61.0 all-gather.34
  864.4 67.9 all-gather.26
  948.7 88.3 reduce-scatter.20
  1060.5 130.0 reduce-scatter.18
  1192.0 80.3 all-gather.36
  1273.8 115.3 all-gather.28
  1392.1 54.7 all-gather.30
  1449.9 55.3 all-gather.38
  1508.1 55.4 all-gather.40
  1566.6 76.4 all-gather.42
  1646.6 75.9 all-gather.44
  1724.8 132.4 reduce-scatter.40
  1859.5 131.2 reduce-scatter.36
  1993.6 138.8 reduce-scatter.24
  2135.3 139.5 reduce-scatter.26
  2277.6 139.4 reduce-scatter.30
  2423.1 98.4 reduce-scatter.38
  2524.5 151.0 reduce-scatter.28
  2678.3 184.3 reduce-scatter.32
  2865.6 184.3 reduce-scatter.34
  3056.6 153.4 reduce-scatter.22
where the time goes:
time: 3230 us; the launch traced here: 3220 us
  waiting for transfers between devices  1800 us (56%)
  matrix products  572 us (18%)
  local copies, waits for them, and re-layouts  443 us (14%)
  blocking collectives  326 us (10%)
  other arithmetic  61.8 us (2%)
    unnamed x35, waiting for transfers between devices  347 us
    slice x122, local copies, waits for them, and re-layouts, head_slice(): part = matrix[:, :, start * HEAD_DIM:(start + 2) * HEAD_DIM]  197 us
    reduce_scatter x1, waiting for transfers between devices, on_device(): lax.psum_scatter(down_weight_grad, ('obj', 'seq'), scatter_dimension=0, t...  187 us
    reduce_scatter x1, waiting for transfers between devices, on_device(): lax.psum_scatter(up_weight_grad, ('obj', 'seq'), scatter_dimension=0, til...  187 us
    reduce_scatter x1, waiting for transfers between devices, on_device(): lax.psum_scatter(self_weight_grad, ('obj', 'seq'), scatter_dimension=0, t...  160 us
    reduce_scatter x1, waiting for transfers between devices, on_device(): lax.psum_scatter(cross_memory_grad, ('obj', 'seq'), scatter_dimension=0,...  154 us
    reduce_scatter x1, waiting for transfers between devices, on_device(): lax.psum_scatter(cross_query_grad, ('obj', 'seq'), scatter_dimension=0, t...  142 us
    reduce_scatter x1, waiting for transfers between devices, on_device(): lax.psum_scatter(cross_output_grad, ('obj', 'seq'), scatter_dimension=0,...  142 us
  transfers between devices with their start and end apart: 32, of which 18 were waited for; matrix products, arithmetic and copies ran while one was open for 32% of the time, Pallas kernels for 0%

commit v1 on v0

v1 whole, which is shorter than its diff:
```python
from functools import partial

import jax
import jax.numpy as jnp
from jax import lax
from jax.experimental import pallas as pl
from jax.experimental.pallas import tpu as pltpu
from jax.sharding import PartitionSpec as P

HEAD_DIM = 64
PAIR = 2 * HEAD_DIM
VIEWS = 4
VIEW_PATCHES = 1024
BOTH = ("obj", "seq")
SMALL = 16

epsilon = 1e-05
f32 = jnp.float32
bf16 = jnp.bfloat16
NN = (((1,), (0,)), ((), ()))
NT = (((1,), (1,)), ((), ()))
TN = (((0,), (0,)), ((), ()))


def dot(left, right, dims=NN):
    return lax.dot_general(left, right, dims, preferred_element_type=f32)


def params(megabytes=56):
    return pltpu.CompilerParams(vmem_limit_bytes=megabytes * 2**20)


def norm_parts(values):
    center = values - jnp.mean(values, -1, keepdims=True)
    spread = jnp.mean(center * center, -1, keepdims=True)
    scale = lax.rsqrt(spread + epsilon)
    return center * scale, scale


def norm_back(unit, scale, grad):
    return scale * (
        grad - jnp.mean(grad, -1, keepdims=True) - unit * jnp.mean(grad * unit, -1, keepdims=True)
    )


def attend_kernel(count, masked, *refs):
    q_ref, kv = refs[0], refs[1 : 1 + count]
    bias = refs[1 + count] if masked else None
    o_ref, lse_ref = refs[-2:]
    query = q_ref[...]
    keys = jnp.concatenate([r[:, :PAIR] for r in kv], 0)
    values = jnp.concatenate([r[:, PAIR:] for r in kv], 0)
    low = lax.broadcasted_iota(jnp.int32, query.shape, 1) < HEAD_DIM
    outs, lses = [], []
    for head in range(2):
        mine = low if head == 0 else ~low
        score = dot(jnp.where(mine, query, jnp.zeros_like(query)), keys, NT)
        if masked:
            score = score + bias[...]
        top = jnp.max(score, 1, keepdims=True)
        lifted = jnp.exp(score - top)
        total = jnp.sum(lifted, 1, keepdims=True)
        outs.append(dot(lifted.astype(bf16), values) * (1.0 / total))
        lses.append(top + jnp.log(total))
    o_ref[...] = jnp.where(low, outs[0], outs[1]).astype(bf16)
    lse_ref[...] = jnp.where(low, lses[0], lses[1])[None]


def attend(query, kvs, bias):
    rows, width = query.shape
    count, slots, pairs = len(kvs), kvs[0].shape[0], width // PAIR
    row = pl.BlockSpec((rows, PAIR), lambda i: (0, i))
    slot = pl.BlockSpec((slots, 2 * PAIR), lambda i: (0, i))
    masked = bias is not None
    total = count * slots
    return pl.pallas_call(
        partial(attend_kernel, count, masked),
        grid=(pairs,),
        in_specs=[row] + [slot] * count + [pl.BlockSpec((1, total), lambda i: (0, 0))] * masked,
        out_specs=[row, pl.BlockSpec((1, rows, PAIR), lambda i: (i, 0, 0))],
        out_shape=[
            jax.ShapeDtypeStruct((rows, width), bf16),
            jax.ShapeDtypeStruct((pairs, rows, PAIR), f32),
        ],
        compiler_params=params(),
        name="attend",
        cost_estimate=pl.CostEstimate(
            flops=16 * rows * total * width,
            bytes_accessed=4 * width * (rows + total),
            transcendentals=2 * pairs * rows * total,
        ),
    )(query, *kvs, *([bias] if masked else []))


def attend_back_kernel(count, masked, *refs):
    q_ref, kv = refs[0], refs[1 : 1 + count]
    o_ref, do_ref, lse_ref = refs[1 + count : 4 + count]
    bias = refs[4 + count] if masked else None
    dq_ref, dkv = refs[-1 - count], refs[-count:]
    query, grad = q_ref[...], do_ref[...]
    slots = kv[0].shape[0]
    keys = jnp.concatenate([r[:, :PAIR] for r in kv], 0)
    values = jnp.concatenate([r[:, PAIR:] for r in kv], 0)
    low = lax.broadcasted_iota(jnp.int32, query.shape, 1) < HEAD_DIM
    lse = lse_ref[0]
    product = o_ref[...].astype(f32) * grad.astype(f32)
    dk = dv = 0.0
    dqs = []
    for head in range(2):
        mine = low if head == 0 else ~low
        head_query = jnp.where(mine, query, jnp.zeros_like(query))
        head_grad = jnp.where(mine, grad, jnp.zeros_like(grad))
        score = dot(head_query, keys, NT)
        if masked:
            score = score + bias[...]
        probs = jnp.exp(score - lse[:, HEAD_DIM * head : HEAD_DIM * head + 1])
        delta = jnp.sum(jnp.where(mine, product, 0.0), 1, keepdims=True)
        score_grad = (probs * (dot(head_grad, values, NT) - delta)).astype(bf16)
        dk = dk + dot(jnp.transpose(head_query), score_grad)
        dv = dv + dot(jnp.transpose(head_grad), probs.astype(bf16))
        dqs.append(dot(score_grad, keys))
    dq_ref[...] = (jnp.where(low, dqs[0], dqs[1]) * HEAD_DIM**-0.5).astype(bf16)
    dk, dv = jnp.transpose(dk), jnp.transpose(dv)
    for j in range(count):
        dkv[j][:, :PAIR] = dk[j * slots : (j + 1) * slots].astype(bf16)
        dkv[j][:, PAIR:] = dv[j * slots : (j + 1) * slots].astype(bf16)


def attend_back(query, kvs, out, grad, lse, bias):
    rows, width = query.shape
    count, slots, pairs = len(kvs), kvs[0].shape[0], width // PAIR
    row = pl.BlockSpec((rows, PAIR), lambda i: (0, i))
    slot = pl.BlockSpec((slots, 2 * PAIR), lambda i: (0, i))
    masked = bias is not None
    total = count * slots
    result = pl.pallas_call(
        partial(attend_back_kernel, count, masked),
        grid=(pairs,),
        in_specs=[row]
        + [slot] * count
        + [row, row, pl.BlockSpec((1, rows, PAIR), lambda i: (i, 0, 0))]
        + [pl.BlockSpec((1, total), lambda i: (0, 0))] * masked,
        out_specs=[row] + [slot] * count,
        out_shape=[jax.ShapeDtypeStruct((rows, width), bf16)]
        + [jax.ShapeDtypeStruct((slots, 2 * width), bf16)] * count,
        compiler_params=params(),
        name="attend_back",
        cost_estimate=pl.CostEstimate(
            flops=40 * rows * total * width,
            bytes_accessed=8 * width * (rows + total),
            transcendentals=2 * pairs * rows * total,
        ),
    )(query, *kvs, out, grad, lse, *([bias] if masked else []))
    return result[0], result[1:]


def block_kernel(core_ref, third_ref, cot_ref, gain_ref, shift_ref, dbias_ref, ubias_ref, up_ref, down_ref,
                 result_ref, tgrad_ref, upkeep_ref, upsend_ref, dnkeep_ref, dnsend_ref, vec_ref, ubgrad_ref,
                 unit_s, final_s, final_t, out_s, fgrad_s, scale_s, wide_s, tall_s):
    step = pl.program_id(0)
    core = core_ref[0]

    @pl.when(step == 0)
    def _():
        unit, scale = norm_parts(third_ref[...])
        unit_s[...] = unit
        scale_s[...] = scale
        final = (unit * gain_ref[...] + shift_ref[...]).astype(bf16)
        final_s[...] = final
        final_t[...] = jnp.transpose(final)
        out_s[...] = jnp.zeros_like(out_s)
        fgrad_s[...] = jnp.zeros_like(fgrad_s)

    cot = cot_ref[...]
    up = up_ref[...].reshape(-1, up_ref.shape[-1])
    down = down_ref[...].reshape(-1, down_ref.shape[-1])
    upper = dot(final_s[...], up) + ubias_ref[...]
    cdf = 0.5 * (1.0 + lax.erf(upper * (0.5**0.5)))
    active = (upper * cdf).astype(bf16)
    slope = cdf + upper * (jnp.exp(-0.5 * upper * upper) * 0.3989422804014327)
    ugrad = (slope * dot(cot, down, NT)).astype(bf16)
    out_s[...] += dot(active, down)
    fgrad_s[...] += dot(ugrad, up, NT)
    ubgrad_ref[...] = jnp.sum(ugrad.astype(f32), 0, keepdims=True)
    wide_s[...] = dot(final_t[...], ugrad).astype(bf16).reshape(wide_s.shape)
    upkeep_ref[...] = wide_s[:, core]
    upsend_ref[...] = wide_s[:, 1 - core]
    tall_s[...] = dot(jnp.transpose(active), cot).astype(bf16).reshape(tall_s.shape)
    dnkeep_ref[...] = tall_s[:, core]
    dnsend_ref[...] = tall_s[:, 1 - core]

    @pl.when(step == pl.num_programs(0) - 1)
    def _():
        result_ref[...] = (third_ref[...] + (out_s[...] + dbias_ref[...])).astype(bf16)
        unit, fgrad, cotf = unit_s[...], fgrad_s[...], cot.astype(f32)
        tgrad_ref[...] = cotf + norm_back(unit, scale_s[...], fgrad * gain_ref[...])
        vec_ref[...] = jnp.zeros_like(vec_ref)
        vec_ref[0:1, :] = jnp.sum(fgrad * unit, 0, keepdims=True)
        vec_ref[1:2, :] = jnp.sum(fgrad, 0, keepdims=True)
        vec_ref[2:3, :] = jnp.sum(cotf, 0, keepdims=True)


def feed_forward(core, third, cot, gain, shift, down_bias, up_bias, packed, up_row, down_row, shard):
    rows, width = third.shape
    parts = packed.shape[0]
    hidden = up_bias.shape[1]
    tile = 512
    per = width // tile
    tall = hidden // parts
    spread = tile // tall
    steps = hidden // tile
    whole = lambda shape: pl.BlockSpec(shape, lambda j, c: (0,) * len(shape))
    wide_map = lambda base: (lambda j, c: (0, base + j // per, j % per))
    half = parts // 2
    return pl.pallas_call(
        block_kernel,
        grid_spec=pltpu.PrefetchScalarGridSpec(
            num_scalar_prefetch=1,
            grid=(steps,),
            in_specs=[
                whole((rows, width)),
                whole((rows, width)),
                whole((1, width)),
                whole((1, width)),
                whole((1, width)),
                pl.BlockSpec((1, tile), lambda j, c: (0, j)),
                pl.BlockSpec((parts, shard, tile), wide_map(up_row // shard)),
                pl.BlockSpec((spread, tall, width), lambda j, c: (j, down_row // tall, 0)),
            ],
            out_specs=[
                whole((rows, width)),
                whole((rows, width)),
                pl.BlockSpec((half, shard, tile), wide_map(0)),
                pl.BlockSpec((half, shard, tile), wide_map(0)),
                pl.BlockSpec((spread // 2, tall, width), lambda j, c: (j, 0, 0)),
                pl.BlockSpec((spread // 2, tall, width), lambda j, c: (j, 0, 0)),
                whole((8, width)),
                pl.BlockSpec((1, tile), lambda j, c: (0, j)),
            ],
            scratch_shapes=[
                pltpu.VMEM((rows, width), f32),
                pltpu.VMEM((rows, width), bf16),
                pltpu.VMEM((width, rows), bf16),
                pltpu.VMEM((rows, width), f32),
                pltpu.VMEM((rows, width), f32),
                pltpu.VMEM((rows, 1), f32),
                pltpu.VMEM((half, 2, shard, tile), bf16),
                pltpu.VMEM((spread // 2, 2, tall, width), bf16),
            ],
        ),
        out_shape=[
            jax.ShapeDtypeStruct((rows, width), bf16),
            jax.ShapeDtypeStruct((rows, width), f32),
            jax.ShapeDtypeStruct((half, tall, width), bf16),
            jax.ShapeDtypeStruct((half, tall, width), bf16),
            jax.ShapeDtypeStruct((half, tall, width), bf16),
            jax.ShapeDtypeStruct((half, tall, width), bf16),
            jax.ShapeDtypeStruct((8, width), f32),
            jax.ShapeDtypeStruct((1, hidden), f32),
        ],
        compiler_params=params(),
        name="feed_forward",
        cost_estimate=pl.CostEstimate(
            flops=12 * rows * width * hidden,
            bytes_accessed=8 * width * hidden + 12 * rows * width,
            transcendentals=2 * rows * hidden,
        ),
    )(core, third, cot, gain, shift, down_bias, up_bias, packed, packed)


class Grid:
    def __init__(self, mesh):
        self.obj, self.seq = mesh.shape["obj"], mesh.shape["seq"]
        self.all = self.obj * self.seq
        self.me = lax.axis_index("obj") * self.seq + lax.axis_index("seq")
        self.group = [m for m in (1 << k for k in range(20)) if m < self.seq // 2]
        self.far = self.seq // 2

    def swap(self, value, mask):
        return lax.ppermute(value, BOTH, [(i, i ^ mask) for i in range(self.all)])

    def bit(self, mask):
        return (self.me // mask) % 2

    def orders(self):
        low = [m for m in self.group[1:]] + [self.far]
        high = [m for m in (1 << k for k in range(20)) if self.seq <= m < self.all]
        return high[::-1] + low, high + low

    def gather_group(self, value):
        found = {0: value}
        for mask in self.group[1:][::-1] + self.group[:1]:
            found.update({d ^ mask: self.swap(v, mask) for d, v in list(found.items())})
        return [found[d] for d in range(self.seq // 2)]

    def sum_group(self, terms):
        terms = {d: [t] for d, t in enumerate(terms)}
        for mask in self.group[:1] + self.group[1:]:
            for d in [d for d in terms if d & mask]:
                moved = self.swap(add(terms.pop(d)), mask)
                terms[d ^ mask].append(moved)
        return add(terms[0])

    def scatter(self, keep, send, order):
        masks = [1 << k for k in range(20) if 1 < 1 << k < self.all][::-1]
        terms = [keep, self.swap(send, 1)]
        terms = [t.reshape((2,) * len(masks) + t.shape[1:]) for t in terms]
        for mask in order:
            axis = masks.index(mask)
            masks.remove(mask)
            bit = self.bit(mask)
            pick = lambda t, which: lax.dynamic_index_in_dim(t, which, axis, keepdims=False)
            moved = self.swap(add([pick(t, 1 - bit) for t in terms]), mask)
            terms = [pick(t, bit) for t in terms] + [moved]
        return sum(t.astype(f32) for t in terms)


def add(terms):
    if len(terms) == 1:
        return terms[0]
    return sum(t.astype(f32) for t in terms).astype(bf16)


def split_pairs(matrix):
    rows, width = matrix.shape
    return matrix.reshape(rows, 2, width // (2 * PAIR), PAIR).transpose(0, 2, 1, 3).reshape(rows, width)


def join_pairs(matrix):
    rows, width = matrix.shape
    return matrix.reshape(rows, width // (2 * PAIR), 2, PAIR).transpose(0, 2, 1, 3).reshape(rows, width)


def stack_columns(matrix, width):
    rows = matrix.shape[0]
    return matrix.reshape(rows, -1, width).transpose(1, 0, 2).reshape(-1, width)


def unstack_columns(matrix, rows):
    width = matrix.shape[1]
    return matrix.reshape(-1, rows, width).transpose(1, 0, 2).reshape(rows, -1)


def pad_rows(matrix, rows):
    return jnp.pad(matrix, ((0, rows - matrix.shape[0]), (0, 0)))


def on_device(
    mesh,
    tokens,
    camera,
    patches,
    patch_count,
    patch_index,
    cotangent,
    camera_weight,
    self_weight,
    self_output,
    mid_gain,
    mid_bias,
    patch_weight,
    view_table,
    cross_query,
    cross_memory,
    cross_output,
    last_gain,
    last_bias,
    up_weight,
    up_bias,
    down_weight,
    down_bias,
):
    grid = Grid(mesh)
    parts = grid.all
    width = self_output.shape[1]
    low = lambda v: v.astype(bf16)
    factor = HEAD_DIM**-0.5
    core = grid.bit(1)
    half = grid.bit(grid.far)

    def compact(value):
        mine = lax.dynamic_index_in_dim(value, half, 0, keepdims=False)
        other = lax.dynamic_index_in_dim(value, 1 - half, 0, keepdims=False)
        return jnp.concatenate([mine, grid.swap(other, grid.far)], 0)

    def spread(value):
        rows = value.shape[0] // 2
        mine, other = value[:rows], grid.swap(value[rows:], grid.far)
        return jnp.where(half == 0, jnp.stack([mine, other]), jnp.stack([other, mine]))

    shard = self_output.shape[0]
    queries_width = width
    self_mixed = jnp.concatenate(
        [low(self_weight[:, :width]), split_pairs(low(self_weight[:, width:]))], 1
    )
    small = jnp.concatenate(
        [
            low(camera_weight).reshape(-1),
            low(view_table).reshape(-1),
            low(mid_gain),
            low(mid_bias),
            low(last_gain),
            low(last_bias),
            low(down_bias),
            low(up_bias),
        ]
    )
    small_sizes = [
        camera_weight.size,
        view_table.size,
        shard,
        shard,
        shard,
        shard,
        shard,
        up_bias.size,
    ]
    small_rows = jnp.pad(small, (0, SMALL * width - small.size)).reshape(SMALL, width)
    first = jnp.concatenate([stack_columns(self_mixed, width), small_rows], 0)
    patch_rows = patch_weight.shape[0]
    patch_room = -(-patch_rows // 16) * 16
    tall = down_weight.shape[0]
    blocks = [
        stack_columns(low(up_weight), width),
        low(down_weight),
        low(self_output),
        low(cross_query),
        low(cross_output),
        stack_columns(split_pairs(low(cross_memory)), width),
        pad_rows(low(patch_weight), patch_room),
    ]
    starts = [0]
    for block in blocks:
        starts.append(starts[-1] + block.shape[0])
    second_pack = jnp.concatenate(blocks, 0)
    first = lax.all_gather(first, BOTH, axis=0, tiled=False)
    first_done, second_pack = lax.optimization_barrier((first, second_pack))
    first = first_done
    packed = lax.all_gather(second_pack, BOTH, axis=0, tiled=False)

    def square(source, start, rows):
        return source[:, start : start + rows].reshape(parts * rows, width)

    def columns(source, start, rows, count):
        return jnp.concatenate(
            [square(source, start + q * rows, rows) for q in range(count)], 1
        )

    full_q = square(first, 0, shard)
    full_kv = columns(first, shard, shard, 2)
    tiny = first[:, 3 * shard :].reshape(parts, -1)
    pieces = []
    at = 0
    for size in small_sizes:
        pieces.append(tiny[:, at : at + size].astype(f32))
        at += size
    full_camera = pieces[0].reshape(parts, 16, -1).transpose(1, 0, 2).reshape(16, -1)
    full_view = pieces[1].reshape(parts, VIEWS, -1).transpose(1, 0, 2).reshape(VIEWS, -1)
    g_mid, b_mid, g_last, b_last, b_down, b_up = (p.reshape(1, -1) for p in pieces[2:])
    full_out = square(packed, starts[2], shard)
    full_cq = square(packed, starts[3], shard)
    full_co = square(packed, starts[4], shard)
    full_mem = columns(packed, starts[5], shard, 2)
    full_patch = packed[:, starts[6] : starts[6] + patch_rows].reshape(-1, width)

    x = compact(tokens).astype(f32)
    cot = compact(cotangent)
    feats = compact(patches)
    views = compact(patch_index) // VIEW_PATCHES
    camera_mine = lax.dynamic_index_in_dim(camera, half, 0, keepdims=False)
    live = lax.dynamic_index_in_dim(patch_count, half, 0, keepdims=False)
    modulation = jnp.sum(camera_mine[:, None] * full_camera, 0)
    scale1, shift1 = 1.0 + modulation[None, :width], modulation[None, width:]
    unit1, rstd1 = norm_parts(x)
    hidden = low(unit1 * scale1 + shift1)
    query = low(low(dot(hidden, full_q)).astype(f32) * factor)
    kv = low(dot(hidden, full_kv))
    kvs = grid.gather_group(kv)

    view_hot = (views[:, None] == jnp.arange(VIEWS)[None, :]).astype(f32)
    view_part = sum(view_hot[:, v : v + 1] * full_view[v : v + 1] for v in range(VIEWS))
    embedded = low(dot(feats, full_patch) + view_part)
    memory = low(dot(embedded, full_mem))
    mems = grid.gather_group(memory)
    place = lax.axis_index("seq")
    chunk = patches.shape[1]
    lane = jnp.arange(chunk)
    slots = jnp.concatenate(
        [
            chunk * (place ^ d ^ far) + lane
            for d in range(grid.seq // 2)
            for far in (0, grid.far)
        ]
    )
    bias = jnp.where(slots < live, 0.0, -1e30).astype(f32).reshape(1, -1)

    attended, lse1 = attend(query, kvs, None)
    second = x + dot(attended, full_out)
    unit2, rstd2 = norm_parts(second)
    normed = low(unit2 * g_mid + b_mid)
    asked = low(low(dot(normed, full_cq)).astype(f32) * factor)
    crossed, lse2 = attend(asked, mems, bias)
    third = second + dot(crossed, full_co)
    (
        result,
        third_grad,
        up_keep,
        up_send,
        down_keep,
        down_send,
        last_vectors,
        up_bias_grad,
    ) = feed_forward(
        core.reshape(1).astype(jnp.int32),
        third,
        cot,
        g_last,
        b_last,
        b_down,
        b_up,
        packed,
        starts[0],
        starts[1],
        shard,
    )
    order_a, order_b = grid.orders()
    up_grad = grid.scatter(up_keep, up_send, order_a)
    down_grad = grid.scatter(down_keep, down_send, order_b)

    def scatter_rows(grads, order):
        joined = jnp.concatenate(grads, 1)
        joined = joined.reshape(parts // 2, 2, *joined.shape[1:])
        keep = lax.dynamic_index_in_dim(joined, core, 1, keepdims=False)
        send = lax.dynamic_index_in_dim(joined, 1 - core, 1, keepdims=False)
        return grid.scatter(keep, send, order)

    def by_owner(grad, columns=1):
        grad = low(grad).reshape(parts, -1, grad.shape[1])
        return [grad[:, :, q * width : (q + 1) * width] for q in range(columns)]

    third_low = low(third_grad)
    co_grad = dot(crossed, third_low, TN)
    crossed_grad = low(dot(third_low, full_co, NT))
    asked_grad, mem_terms = attend_back(asked, mems, crossed, crossed_grad, lse2, bias)
    memory_grad = grid.sum_group(mem_terms)
    cq_grad = dot(normed, asked_grad, TN)
    normed_grad = dot(asked_grad, full_cq, NT)
    second_grad = third_grad + norm_back(unit2, rstd2, normed_grad * g_mid)
    mid_gain_grad = jnp.sum(normed_grad * unit2, 0)
    mid_bias_grad = jnp.sum(normed_grad, 0)
    second_low = low(second_grad)
    so_grad = dot(attended, second_low, TN)
    attended_grad = low(dot(second_low, full_out, NT))
    query_grad, pair_terms = attend_back(query, kvs, attended, attended_grad, lse1, None)
    mem_w_grad = dot(embedded, memory_grad, TN)
    embedded_grad = low(dot(memory_grad, full_mem, NT))
    patch_w_grad = dot(feats, embedded_grad, TN)
    view_grad = jnp.stack(
        [jnp.sum(view_hot[:, v : v + 1] * embedded_grad.astype(f32), 0) for v in range(VIEWS)]
    )
    patch_grad = low(dot(embedded_grad, full_patch, NT))
    cross_sum = scatter_rows(by_owner(co_grad) + by_owner(cq_grad), order_a)
    mem_sum = scatter_rows(
        by_owner(mem_w_grad, 2)
        + [jnp.pad(by_owner(patch_w_grad)[0], ((0, 0), (0, patch_room - patch_rows), (0, 0)))],
        order_b,
    )
    pair_grad = grid.sum_group(pair_terms)
    q_w_grad = dot(hidden, query_grad, TN)
    kv_w_grad = dot(hidden, pair_grad, TN)
    hidden_grad = dot(query_grad, full_q, NT) + dot(pair_grad, full_kv, NT)
    modulation_grad = jnp.concatenate(
        [jnp.sum(hidden_grad * unit1, 0), jnp.sum(hidden_grad, 0)]
    )
    camera_grad = camera_mine[:, None] * modulation_grad[None]
    token_grad = low(second_grad + norm_back(unit1, rstd1, hidden_grad * scale1))
    small_grad = jnp.concatenate(
        [
            camera_grad.reshape(16, parts, -1).transpose(1, 0, 2).reshape(parts, -1),
            view_grad.reshape(VIEWS, parts, -1).transpose(1, 0, 2).reshape(parts, -1),
            mid_gain_grad.reshape(parts, -1),
            mid_bias_grad.reshape(parts, -1),
            last_vectors[0].reshape(parts, -1),
            last_vectors[1].reshape(parts, -1),
            last_vectors[2].reshape(parts, -1),
            up_bias_grad.reshape(parts, -1),
        ],
        1,
    )
    small_grad = jnp.pad(small_grad, ((0, 0), (0, SMALL * width - small_grad.shape[1])))
    small_grad = low(small_grad).reshape(parts, SMALL, width)
    self_sum_a = scatter_rows(by_owner(so_grad) + by_owner(q_w_grad), order_a)
    self_sum_b = scatter_rows(by_owner(kv_w_grad, 2) + [small_grad], order_b)

    tiny = self_sum_b[2 * shard :].reshape(-1)
    pieces = []
    at = 0
    for size in small_sizes:
        pieces.append(tiny[at : at + size])
        at += size
    kv_own = join_pairs(unstack_columns(self_sum_b[: 2 * shard], shard))
    return (
        spread(result),
        spread(token_grad),
        spread(patch_grad),
        pieces[0].reshape(camera_weight.shape),
        jnp.concatenate([self_sum_a[shard:], kv_own], 1),
        self_sum_a[:shard],
        pieces[2],
        pieces[3],
        mem_sum[2 * shard : 2 * shard + patch_rows],
        pieces[1].reshape(view_table.shape),
        cross_sum[shard:],
        join_pairs(unstack_columns(mem_sum[: 2 * shard], shard)),
        cross_sum[:shard],
        pieces[4],
        pieces[5],
        unstack_columns(up_grad, shard),
        pieces[7],
        down_grad,
        pieces[6],
    )


def solution(mesh):
    rows, flat, lanes = P(BOTH, None), P(BOTH), P(None, BOTH)
    sequence = P("obj", "seq", None)
    in_specs = (
        sequence,
        P("obj", None),
        sequence,
        P("obj"),
        P("obj", "seq"),
        sequence,
        lanes,
        rows,
        rows,
        flat,
        flat,
        rows,
        lanes,
        rows,
        rows,
        rows,
        flat,
        flat,
        rows,
        flat,
        rows,
        flat,
    )
    out_specs = (
        sequence,
        sequence,
        sequence,
        lanes,
        rows,
        rows,
        flat,
        flat,
        rows,
        lanes,
        rows,
        rows,
        rows,
        flat,
        flat,
        rows,
        flat,
        rows,
        flat,
    )
    return jax.shard_map(
        partial(on_device, mesh),
        mesh=mesh,
        in_specs=in_specs,
        out_specs=out_specs,
        check_vma=False,
    )
```

time: 3230 us -> 864 us (0.27)
  waiting for transfers between devices: 1800 us -> 481 us
  matrix products: 572 us -> 56.6 us
  local copies, waits for them, and re-layouts: 443 us -> 65.8 us
  blocking collectives: 326 us -> 0 us
  Pallas kernels: 0 us -> 118 us
  starting transfers between devices: 2.23 us -> 44 us
    reduce_scatter x9 -> x0, waiting for transfers between devices: 1110 us -> none  [the longest x1 187 us: on_device(): lax.psum_scatter(down_weight_grad, ('obj', 'seq'), scatter_dimension=0, t...]
    dot_general x135 -> x21, matrix products: 450 us -> 56.6 us  [dot(): return lax.dot_general(left, right, dims, preferred_element_type=f32)]
    unnamed x35 -> x2, waiting for transfers between devices: 347 us -> 0.03 us
    ppermute x0 -> x49, waiting for transfers between devices: none -> 319 us  [swap(): return lax.ppermute(value, BOTH, [(i, i ^ mask) for i in range(self.all)])]
    all_gather x6 -> x0, blocking collectives: 241 us -> none  [the longest x2 83.3 us: forward(): lax.all_gather(view_table, ('obj', 'seq'), axis=1, tiled=True)]
    all_gather x20 -> x2, waiting for transfers between devices: 335 us -> 162 us  [the longest x1 85.5 us: on_device(): packed = lax.all_gather(second_pack, BOTH, axis=0, tiled=False)]
    slice x122 -> x21, local copies, waits for them, and re-layouts: 197 us -> 24.7 us  [the longest x2 11.4 us: square(): return source[:, start:start + rows].reshape(parts * rows, width)]
    sub x32 -> x0, matrix products: 122 us -> none  [head_probs(): return jnp.exp(raw - top) / total]
  transfers between devices with their start and end apart: 32 -> 51, of which waited for: 18 -> 24; matrix products, arithmetic and copies ran while one was open for 32% -> 20% of each run, Pallas kernels for 0% -> 8%
where the time goes in v1:
time: 864 us; the launch traced here: 856 us
  waiting for transfers between devices  481 us (56%)
  Pallas kernels  118 us (14%)
  other arithmetic  74.1 us (9%)
  local copies, waits for them, and re-layouts  65.8 us (8%)
  matrix products  56.6 us (7%)
  starting transfers between devices  44 us (5%)
  between operations  16.1 us (2%)
    ppermute x49, waiting for transfers between devices, swap(): return lax.ppermute(value, BOTH, [(i, i ^ mask) for i in range(self.all)])  319 us
    all_gather x1, waiting for transfers between devices, on_device(): packed = lax.all_gather(second_pack, BOTH, axis=0, tiled=False)  85.5 us
    all_gather x1, waiting for transfers between devices, on_device(): first = lax.all_gather(first, BOTH, axis=0, tiled=False)  76.5 us
    dot_general x21, matrix products, dot(): return lax.dot_general(left, right, dims, preferred_element_type=f32)  56.6 us
    pallas_call x2, Pallas kernels, attend_back(): pl.pallas_call(partial(attend_back_kernel, count, masked), grid=(pairs,),...  49.1 us
    ppermute x49, starting transfers between devices, swap(): return lax.ppermute(value, BOTH, [(i, i ^ mask) for i in range(self.all)])  43.9 us
    convert_element_type x26, other arithmetic, add(): return sum((t.astype(f32) for t in terms)).astype(bf16)  36.5 us
    pallas_call x2, Pallas kernels, attend(): pl.pallas_call(partial(attend_kernel, count, masked), grid=(pairs,), in_s...  36.2 us
  transfers between devices with their start and end apart: 51, of which 24 were waited for; matrix products, arithmetic and copies ran while one was open for 20% of the time, Pallas kernels for 8%

profile of v1, /device:TPU:0, one launch (start us, length us, event | category | flops | bytes accessed | tf_op | source)
XLA Modules:
  0.0 855.8 jit_solution(14654747967380792138)
XLA Ops:
  11.4 76.5 %all-gather.5.cloned.1.call-done = bf16[3584,1024]{1,0:T(8,128)(2,1)} async-done(((bf16[112,1024]{1,0:T(8,128)(2,1)}), bf16[3584,1024]{1,0:T(8,128)(2,1)}) %all-gather.5.cloned.1.call-update) | async-done | bytes 7340048 | tf_op jit(solution)/shard_map/all_gather | solution.py:436
  97.3 50.5 %collective-permute-done = bf16[192,1024]{1,0:T(8,128)(2,1)S(1)} collective-permute-done((bf16[192,1024]{1,0:T(8,128)(2,1)S(1)}, bf16[192,1024]{1,0:T(8,128)(2,1)S(1)}, u32[]{:S(2)}, u32[]{:S(2)}) %collective-permute-start) | collective-permute-done | bytes 393248 | tf_op jit(solution)/shard_map/ppermute | solution.py:280
  151.3 4.0 fusion.82
  160.6 4.4 collective-permute-done.9
  169.1 60.2 %collective-permute-done.2.refs_3_ = bf16[384,2048]{1,0:T(8,128)(2,1)} collective-permute-done((bf16[384,2048]{1,0:T(8,128)(2,1)}, bf16[384,2048]{1,0:T(8,128)(2,1)}, u32[]{:S(2)}, u32[]{:S(2)}) %collective-permute-start.2) | collective-permute-done | bytes 1572896 | tf_op jit(solution)/shard_map/ppermute | solution.py:280
  231.3 85.5 %all-gather.7.cloned.1.call-done = bf16[14336,1024]{1,0:T(8,128)(2,1)} async-done(((bf16[448,1024]{1,0:T(8,128)(2,1)}), bf16[14336,1024]{1,0:T(8,128)(2,1)}) %all-gather.7.cloned.1.call-update) | async-done | bytes 29360144 | tf_op jit(solution)/shard_map/all_gather | solution.py:439
  321.0 7.4 fusion.81
  335.1 21.1 %attend.2 = (bf16[384,1024]{1,0:T(8,128)(2,1)}, f32[8,384,128]{2,1,0:T(8,128)}) custom-call(bf16[384,1024]{1,0:T(8,128)(2,1)} %multiply_convert_fusion.1.refs_0_, bf16[384,2048]{1,0:T(8,128)(2,1)} %convolution_convert_fusion.2.refs_1_, bf16[384,2048]{1,0:T(8,128)(2,1)} %collective-permute-done.1.refs_2_, bf16[384,2048]{1,0:T(8,128)(2,1)} %collective-permute-done.2.refs_3_, ...), custom_call_target="tpu_custom_call" | custom-call | flops 9663676416 | bytes 7864320 | tf_op jit(solution)/shard_map/attend/pallas_call | solution.py:76
  362.4 15.1 %attend.3 = (bf16[384,1024]{1,0:T(8,128)(2,1)}, f32[8,384,128]{2,1,0:T(8,128)}) custom-call(bf16[384,1024]{1,0:T(8,128)(2,1)} %multiply_convert_fusion.refs_0_, bf16[256,2048]{1,0:T(8,128)(2,1)} %fusion.5.refs_1_, bf16[256,2048]{1,0:T(8,128)(2,1)} %copy-done.85, bf16[256,2048]{1,0:T(8,128)(2,1)} %collective-permute-done.7.refs_3_, ...), custom_call_target="tpu_custom_call" | custom-call | flops 6442450944 | bytes 5767168 | tf_op jit(solution)/shard_map/attend/pallas_call | solution.py:76
  380.8 32.6 %feed_forward.1 = (bf16[384,1024]{1,0:T(8,128)(2,1)}, f32[384,1024]{1,0:T(8,128)}, bf16[16,128,1024]{2,1,0:T(8,128)(2,1)}, bf16[16,128,1024]{2,1,0:T(8,128)(2,1)...) custom-call(s32[1]{0:T(128)} %bitcast.core_ref, ...), custom_call_target="tpu_custom_call" | custom-call | flops 19327352832 | bytes 38273024 | tf_op jit(solution)/shard_map/feed_forward/pallas_call | solution.py:215
  413.4 3.5 convolution_convert_fusion.9.refs_6_
  420.1 20.7 %attend_back.2 = (bf16[384,1024]{1,0:T(8,128)(2,1)}, bf16[256,2048]{1,0:T(8,128)(2,1)}, bf16[256,2048]{1,0:T(8,128)(2,1)}, bf16[256,2048]{1,0:T(8,128)(2,1)}, bf16[256,2048]{1,0:T(8,128)(2,1)}) custom-call(bf16[384,1024]{1,0:T(8,128)(2,1)} %multiply_convert_fusion.refs_0_, bf16[256,2048]{1,0:T(8,128)(2,1)} %fusion.5.refs_1_, bf16[256,2048]{1,0:T(8,128)(2,1)} %copy-done.85, ...), custom_call_target="tpu_custom_call" | custom-call | flops 16106127360 | bytes 11534336 | tf_op jit(solution)/shard_map/attend_back/pallas_call | solution.py:136
  447.6 28.5 %attend_back.3 = (bf16[384,1024]{1,0:T(8,128)(2,1)}, bf16[384,2048]{1,0:T(8,128)(2,1)}, bf16[384,2048]{1,0:T(8,128)(2,1)}, bf16[384,2048]{1,0:T(8,128)(2,1)}, bf16[384,2048]{1,0:T(8,128)(2,1)}) custom-call(bf16[384,1024]{1,0:T(8,128)(2,1)} %multiply_convert_fusion.1.refs_0_, bf16[384,2048]{1,0:T(8,128)(2,1)} %convolution_convert_fusion.2.refs_1_, ...), custom_call_target="tpu_custom_call" | custom-call | flops 24159191040 | bytes 15728640 | tf_op jit(solution)/shard_map/attend_back/pallas_call | solution.py:136
  502.5 17.7 %collective-permute-done.17 = bf16[256,2048]{1,0:T(8,128)(2,1)S(1)} collective-permute-done((bf16[256,2048]{1,0:T(8,128)(2,1)S(1)}, bf16[256,2048]{1,0:T(8,128)(2,1)S(1)}, u32[]{:S(2)}, u32[]{:S(2)}) %collective-permute-start.17) | collective-permute-done | bytes 1048608 | tf_op jit(solution)/shard_map/ppermute | solution.py:280
  530.4 4.9 fusion.1
  535.3 3.5 constant_dynamic-slice_fusion
  550.9 9.1 %collective-permute-done.13 = bf16[384,2048]{1,0:T(8,128)(2,1)} collective-permute-done((bf16[384,2048]{1,0:T(8,128)(2,1)S(1)}, bf16[384,2048]{1,0:T(8,128)(2,1)}, u32[]{:S(2)}, u32[]{:S(2)}) %collective-permute-start.13) | collective-permute-done | bytes 1572896 | tf_op jit(solution)/shard_map/ppermute | solution.py:280
  560.1 5.0 fusion.4
  565.2 6.7 convolution_convert_fusion
  575.4 5.1 fusion.84
  592.2 13.9 %collective-permute-done.35 = bf16[2,2,2,64,1024]{4,3,2,1,0:T(8,128)(2,1)} collective-permute-done((bf16[2,2,2,64,1024]{4,3,2,1,0:T(8,128)(2,1)S(1)}, bf16[2,2,2,64,1024]{4,3,2,1,0:T(8,128)(2,1)}, u32[]{:S(2)}, u32[]{:S(2)}) %collective-permute-start.35) | collective-permute-done | bytes 1048608 | tf_op jit(solution)/shard_map/ppermute | solution.py:280
  616.7 3.9 collective-permute-done.18
  621.2 11.0 %collective-permute-done.25 = bf16[2,2,2,64,1024]{4,3,2,1,0:T(8,128)(2,1)S(1)} collective-permute-done((bf16[2,2,2,64,1024]{4,3,2,1,0:T(8,128)(2,1)S(1)}, bf16[2,2,2,64,1024]{4,3,2,1,0:T(8,128)(2,1)S(1)}, u32[]{:S(2)}, u32[]{:S(2)}) %collective-permute-start.25) | collective-permute-done | bytes 1048608 | tf_op jit(solution)/shard_map/ppermute | solution.py:280
  639.4 41.0 %collective-permute-done.36 = bf16[2,2,64,1024]{3,2,0,1:T(8,128)(2,1)S(1)} collective-permute-done((bf16[2,2,64,1024]{3,2,0,1:T(8,128)(2,1)S(1)}, bf16[2,2,64,1024]{3,2,0,1:T(8,128)(2,1)S(1)}, u32[]{:S(2)}, u32[]{:S(2)}) %collective-permute-start.36) | collective-permute-done | bytes 524320 | tf_op jit(solution)/shard_map/ppermute | solution.py:280
  681.0 10.6 %collective-permute-done.26 = bf16[2,2,64,1024]{3,2,0,1:T(8,128)(2,1)S(1)} collective-permute-done((bf16[2,2,64,1024]{3,2,0,1:T(8,128)(2,1)S(1)}, bf16[2,2,64,1024]{3,2,0,1:T(8,128)(2,1)S(1)}, u32[]{:S(2)}, u32[]{:S(2)}) %collective-permute-start.26) | collective-permute-done | bytes 524320 | tf_op jit(solution)/shard_map/ppermute | solution.py:280
  699.8 7.9 collective-permute-done.14
  730.9 22.4 %collective-permute-done.20 = bf16[2,2,2,80,1024]{4,3,2,1,0:T(8,128)(2,1)S(1)} collective-permute-done((bf16[2,2,2,80,1024]{4,3,2,1,0:T(8,128)(2,1)S(1)}, bf16[2,2,2,80,1024]{4,3,2,1,0:T(8,128)(2,1)S(1)}, u32[]{:S(2)}, u32[]{:S(2)}) %collective-permute-start.20) | collective-permute-done | bytes 1310752 | tf_op jit(solution)/shard_map/ppermute | solution.py:280
  755.5 18.2 %collective-permute-done.41 = bf16[2,2,128,1024]{3,2,0,1:T(8,128)(2,1)S(1)} collective-permute-done((bf16[2,2,128,1024]{3,2,0,1:T(8,128)(2,1)S(1)}, bf16[2,2,128,1024]{3,2,0,1:T(8,128)(2,1)S(1)}, u32[]{:S(2)}, u32[]{:S(2)}) %collective-permute-start.41) | collective-permute-done | bytes 1048608 | tf_op jit(solution)/shard_map/ppermute | solution.py:280
  782.8 7.1 collective-permute-done.42
  793.5 13.3 %collective-permute-done.47 = bf16[2,128,1024]{2,1,0:T(8,128)(2,1)S(1)} collective-permute-done((bf16[2,128,1024]{2,1,0:T(8,128)(2,1)S(1)}, bf16[2,128,1024]{2,1,0:T(8,128)(2,1)S(1)}, u32[]{:S(2)}, u32[]{:S(2)}) %collective-permute-start.47) | collective-permute-done | bytes 524320 | tf_op jit(solution)/shard_map/ppermute | solution.py:280
  809.9 10.9 %collective-permute-done.32 = bf16[2,96,1024]{2,1,0:T(8,128)(2,1)S(1)} collective-permute-done((bf16[2,96,1024]{2,1,0:T(8,128)(2,1)S(1)}, bf16[2,96,1024]{2,1,0:T(8,128)(2,1)S(1)}, u32[]{:S(2)}, u32[]{:S(2)}) %collective-permute-start.32) | collective-permute-done | bytes 393248 | tf_op jit(solution)/shard_map/ppermute | solution.py:280
  831.7 8.4 collective-permute-done.33
  (484 shorter events, 209.3 us)
Async XLA Ops:
  7.3 80.6 %all-gather.5.cloned.1.call-start = ((), (), s32[]{:S(2)}) async-start(), calls=%async_computation | async-start | bytes 7569408 | tf_op jit(solution)/shard_map/all_gather | solution.py:436
  10.3 306.4 %all-gather.7.cloned.1.call-start = ((), (), s32[]{:S(2)}) async-start(), calls=%async_computation.1 | async-start | bytes 30277632 | tf_op jit(solution)/shard_map/all_gather | solution.py:439
  88.0 72.5 %collective-permute-start.5 = (s32[128]{0:T(128)S(1)}, s32[128]{0:T(128)S(1)}, u32[]{:S(2)}, u32[]{:S(2)}) collective-permute-start(s32[128]{0:T(128)S(1)} %get-tuple-element.143), channel_id=1, source_target_pairs={{0,4},{1,5},{2,6},{3,7},{4,0},{5,1},{6,2},{7,3},{8,12},{9,13},{10,... | collective-permute-start | bytes 1544 | tf_op jit(solution)/shard_map/ppermute | solution.py:280
  90.6 227.7 %collective-permute-start.4 = (bf16[128,768]{1,0:T(8,128)(2,1)}, bf16[128,768]{1,0:T(8,128)(2,1)}, u32[]{:S(2)}, u32[]{:S(2)}) collective-permute-start(bf16[128,768]{1,0:T(8,128)(2,1)} %get-tuple-element.124), channel_id=1, source_target_pairs={{0,4},{1,5},{2,6},{3,7},{4,0},{5,1},{6,2},{7,3},{8,12},{9,13},{10,... | collective-permute-start | bytes 589832 | tf_op jit(solution)/shard_map/ppermute | solution.py:280
  91.8 56.0 %collective-permute-start = (bf16[192,1024]{1,0:T(8,128)(2,1)S(1)}, bf16[192,1024]{1,0:T(8,128)(2,1)S(1)}, u32[]{:S(2)}, u32[]{:S(2)}) collective-permute-start(bf16[192,1024]{1,0:T(8,128)(2,1)S(1)} %get-tuple-element.120), channel_id=1, source_target_pairs={{0,4},{1,5},{2,6},{3,7},{4,0},{5,1},{6,2},{7,3},{8,12},{9,13},{10,... | collective-permute-start | bytes 1179656 | tf_op jit(solution)/shard_map/ppermute | solution.py:280
  95.6 69.4 %collective-permute-start.9 = (bf16[192,1024]{1,0:T(8,128)(2,1)}, bf16[192,1024]{1,0:T(8,128)(2,1)}, u32[]{:S(2)}, u32[]{:S(2)}) collective-permute-start(bf16[192,1024]{1,0:T(8,128)(2,1)} %get-tuple-element.118), channel_id=1, source_target_pairs={{0,4},{1,5},{2,6},{3,7},{4,0},{5,1},{6,2},{7,3},{8,12},{9,13},{10,... | collective-permute-start | bytes 1179656 | tf_op jit(solution)/shard_map/ppermute | solution.py:280
  158.5 70.8 %collective-permute-start.2 = (bf16[384,2048]{1,0:T(8,128)(2,1)}, bf16[384,2048]{1,0:T(8,128)(2,1)}, u32[]{:S(2)}, u32[]{:S(2)}) collective-permute-start(bf16[384,2048]{1,0:T(8,128)(2,1)} %convolution_convert_fusion.2.refs_1_), channel_id=1, source_target_pairs={{0,2},{1,3},{2,0},{3,1},{4,6},{5,7},{6,4},{7,5},{8,10},{9,11},{10,... | collective-permute-start | bytes 4718600 | tf_op jit(solution)/shard_map/ppermute | solution.py:280
  167.1 166.8 %collective-permute-start.1 = (bf16[384,2048]{1,0:T(8,128)(2,1)}, bf16[384,2048]{1,0:T(8,128)(2,1)}, u32[]{:S(2)}, u32[]{:S(2)}) collective-permute-start(bf16[384,2048]{1,0:T(8,128)(2,1)} %convolution_convert_fusion.2.refs_1_), channel_id=1, source_target_pairs={{0,1},{1,0},{2,3},{3,2},{4,5},{5,4},{6,7},{7,6},{8,9},{9,8},{10,11... | collective-permute-start | bytes 4718600 | tf_op jit(solution)/shard_map/ppermute | solution.py:280
  229.3 104.6 %collective-permute-start.3 = (bf16[384,2048]{1,0:T(8,128)(2,1)}, bf16[384,2048]{1,0:T(8,128)(2,1)S(1)}, u32[]{:S(2)}, u32[]{:S(2)}) collective-permute-start(bf16[384,2048]{1,0:T(8,128)(2,1)} %collective-permute-done.2.refs_3_), channel_id=1, source_target_pairs={{0,1},{1,0},{2,3},{3,2},{4,5},{5,4},{6,7},{7,6},{8,9},{9,8},{10,11... | collective-permute-start | bytes 4718600 | tf_op jit(solution)/shard_map/ppermute | solution.py:280
  419.6 193.8 %collective-permute-start.44 = (bf16[16,128,1024]{2,1,0:T(8,128)(2,1)}, bf16[16,128,1024]{2,1,0:T(8,128)(2,1)}, u32[]{:S(2)}, u32[]{:S(2)}) collective-permute-start(bf16[16,128,1024]{2,1,0:T(8,128)(2,1)} %get-tuple-element.66), channel_id=1, source_target_pairs={{0,1},{1,0},{2,3},{3,2},{4,5},{5,4},{6,7},{7,6},{8,9},{9,8},{10,11... | collective-permute-start | bytes 12582920 | tf_op jit(solution)/shard_map/ppermute | solution.py:280
  419.9 189.3 %collective-permute-start.39 = (bf16[16,128,1024]{2,1,0:T(8,128)(2,1)}, bf16[16,128,1024]{2,1,0:T(8,128)(2,1)}, u32[]{:S(2)}, u32[]{:S(2)}) collective-permute-start(bf16[16,128,1024]{2,1,0:T(8,128)(2,1)} %get-tuple-element.64), channel_id=1, source_target_pairs={{0,1},{1,0},{2,3},{3,2},{4,5},{5,4},{6,7},{7,6},{8,9},{9,8},{10,11... | collective-permute-start | bytes 12582920 | tf_op jit(solution)/shard_map/ppermute | solution.py:280
  440.8 52.1 %collective-permute-start.16 = (bf16[256,2048]{1,0:T(8,128)(2,1)}, bf16[256,2048]{1,0:T(8,128)(2,1)}, u32[]{:S(2)}, u32[]{:S(2)}) collective-permute-start(bf16[256,2048]{1,0:T(8,128)(2,1)} %get-tuple-element.60), channel_id=1, source_target_pairs={{0,1},{1,0},{2,3},{3,2},{4,5},{5,4},{6,7},{7,6},{8,9},{9,8},{10,11... | collective-permute-start | bytes 3145736 | tf_op jit(solution)/shard_map/ppermute | solution.py:280
  441.1 61.0 %collective-permute-start.15 = (bf16[256,2048]{1,0:T(8,128)(2,1)}, bf16[256,2048]{1,0:T(8,128)(2,1)}, u32[]{:S(2)}, u32[]{:S(2)}) collective-permute-start(bf16[256,2048]{1,0:T(8,128)(2,1)} %get-tuple-element.58), channel_id=1, source_target_pairs={{0,1},{1,0},{2,3},{3,2},{4,5},{5,4},{6,7},{7,6},{8,9},{9,8},{10,11... | collective-permute-start | bytes 3145736 | tf_op jit(solution)/shard_map/ppermute | solution.py:280
  499.8 46.5 %collective-permute-start.34 = (bf16[16,64,1024]{2,1,0:T(8,128)(2,1)}, bf16[16,64,1024]{2,1,0:T(8,128)(2,1)}, u32[]{:S(2)}, u32[]{:S(2)}) collective-permute-start(bf16[16,64,1024]{2,1,0:T(8,128)(2,1)} %get-tuple-element.99), channel_id=1, source_target_pairs={{0,1},{1,0},{2,3},{3,2},{4,5},{5,4},{6,7},{7,6},{8,9},{9,8},{10,11... | collective-permute-start | bytes 6291464 | tf_op jit(solution)/shard_map/ppermute | solution.py:280
  502.1 47.4 %collective-permute-start.11 = (bf16[384,2048]{1,0:T(8,128)(2,1)}, bf16[384,2048]{1,0:T(8,128)(2,1)}, u32[]{:S(2)}, u32[]{:S(2)}) collective-permute-start(bf16[384,2048]{1,0:T(8,128)(2,1)} %get-tuple-element.54), channel_id=1, source_target_pairs={{0,1},{1,0},{2,3},{3,2},{4,5},{5,4},{6,7},{7,6},{8,9},{9,8},{10,11... | collective-permute-start | bytes 4718600 | tf_op jit(solution)/shard_map/ppermute | solution.py:280
  520.2 39.9 %collective-permute-start.13 = (bf16[384,2048]{1,0:T(8,128)(2,1)S(1)}, bf16[384,2048]{1,0:T(8,128)(2,1)}, u32[]{:S(2)}, u32[]{:S(2)}) collective-permute-start(bf16[384,2048]{1,0:T(8,128)(2,1)S(1)} %add_convert_fusion.4), channel_id=1, source_target_pairs={{0,2},{1,3},{2,0},{3,1},{4,6},{5,7},{6,4},{7,5},{8,10},{9,11},{10,... | collective-permute-start | bytes 4718600 | tf_op jit(solution)/shard_map/ppermute | solution.py:280
  546.4 42.1 %collective-permute-start.24 = (bf16[16,64,1024]{2,1,0:T(8,128)(2,1)}, bf16[16,64,1024]{2,1,0:T(8,128)(2,1)}, u32[]{:S(2)}, u32[]{:S(2)}) collective-permute-start(bf16[16,64,1024]{2,1,0:T(8,128)(2,1)} %get-tuple-element.103), channel_id=1, source_target_pairs={{0,1},{1,0},{2,3},{3,2},{4,5},{5,4},{6,7},{7,6},{8,9},{9,8},{10,11... | collective-permute-start | bytes 6291464 | tf_op jit(solution)/shard_map/ppermute | solution.py:280
  560.0 74.7 %collective-permute-start.29 = (bf16[16,96,1024]{2,1,0:T(8,128)(2,1)}, bf16[16,96,1024]{2,1,0:T(8,128)(2,1)}, u32[]{:S(2)}, u32[]{:S(2)}) collective-permute-start(bf16[16,96,1024]{2,1,0:T(8,128)(2,1)} %get-tuple-element.95), channel_id=1, source_target_pairs={{0,1},{1,0},{2,3},{3,2},{4,5},{5,4},{6,7},{7,6},{8,9},{9,8},{10,11... | collective-permute-start | bytes 9437192 | tf_op jit(solution)/shard_map/ppermute | solution.py:280
  588.4 106.5 %collective-permute-start.19 = (bf16[16,80,1024]{2,1,0:T(8,128)(2,1)S(1)}, bf16[16,80,1024]{2,1,0:T(8,128)(2,1)S(1)}, u32[]{:S(2)}, u32[]{:S(2)}) collective-permute-start(bf16[16,80,1024]{2,1,0:T(8,128)(2,1)S(1)} %get-tuple-element.97), channel_id=1, source_target_pairs={{0,1},{1,0},{2,3},{3,2},{4,5},{5,4},{6,7},{7,6},{8,9},{9,8},{10,11... | collective-permute-start | bytes 7864328 | tf_op jit(solution)/shard_map/ppermute | solution.py:280
  613.4 102.9 %collective-permute-start.40 = (bf16[2,2,2,128,1024]{4,3,2,1,0:T(8,128)(2,1)S(1)}, bf16[2,2,2,128,1024]{4,3,2,1,0:T(8,128)(2,1)S(1)}, u32[]{:S(2)}, u32[]{:S(2)}) collective-permute-start(bf16[2,2,2,128,1024]{4,3,2,1,0:T(8,128)(2,1)S(1)} %fusion.6), channel_id=1, source_target_pairs={{0,16},{1,17},{2,18},{3,19},{4,20},{5,21},{6,22},{7,23},{8,24},{9,... | collective-permute-start | bytes 6291464 | tf_op jit(solution)/shard_map/ppermute | solution.py:280
  620.5 99.4 %collective-permute-start.45 = (bf16[2,2,2,128,1024]{4,3,2,1,0:T(8,128)(2,1)S(1)}, bf16[2,2,2,128,1024]{4,3,2,1,0:T(8,128)(2,1)S(1)}, u32[]{:S(2)}, u32[]{:S(2)}) collective-permute-start(bf16[2,2,2,128,1024]{4,3,2,1,0:T(8,128)(2,1)S(1)} %fusion.7), channel_id=1, source_target_pairs={{0,8},{1,9},{2,10},{3,11},{4,12},{5,13},{6,14},{7,15},{8,0},{9,1},... | collective-permute-start | bytes 6291464 | tf_op jit(solution)/shard_map/ppermute | solution.py:280
  632.1 48.2 %collective-permute-start.36 = (bf16[2,2,64,1024]{3,2,0,1:T(8,128)(2,1)S(1)}, bf16[2,2,64,1024]{3,2,0,1:T(8,128)(2,1)S(1)}, u32[]{:S(2)}, u32[]{:S(2)}) collective-permute-start(bf16[2,2,64,1024]{3,2,0,1:T(8,128)(2,1)S(1)} %copy.122), channel_id=1, source_target_pairs={{0,8},{1,9},{2,10},{3,11},{4,12},{5,13},{6,14},{7,15},{8,0},{9,1},... | collective-permute-start | bytes 1572872 | tf_op jit(solution)/shard_map/ppermute | solution.py:280
  634.7 56.9 %collective-permute-start.26 = (bf16[2,2,64,1024]{3,2,0,1:T(8,128)(2,1)S(1)}, bf16[2,2,64,1024]{3,2,0,1:T(8,128)(2,1)S(1)}, u32[]{:S(2)}, u32[]{:S(2)}) collective-permute-start(bf16[2,2,64,1024]{3,2,0,1:T(8,128)(2,1)S(1)} %copy.110), channel_id=1, source_target_pairs={{0,8},{1,9},{2,10},{3,11},{4,12},{5,13},{6,14},{7,15},{8,0},{9,1},... | collective-permute-start | bytes 1572872 | tf_op jit(solution)/shard_map/ppermute | solution.py:280
  680.3 47.0 %collective-permute-start.30 = (bf16[2,2,2,96,1024]{4,3,2,1,0:T(8,128)(2,1)S(1)}, bf16[2,2,2,96,1024]{4,3,2,1,0:T(8,128)(2,1)S(1)}, u32[]{:S(2)}, u32[]{:S(2)}) collective-permute-start(bf16[2,2,2,96,1024]{4,3,2,1,0:T(8,128)(2,1)S(1)} %fusion.31), channel_id=1, source_target_pairs={{0,8},{1,9},{2,10},{3,11},{4,12},{5,13},{6,14},{7,15},{8,0},{9,1},... | collective-permute-start | bytes 4718600 | tf_op jit(solution)/shard_map/ppermute | solution.py:280
  709.0 44.3 %collective-permute-start.20 = (bf16[2,2,2,80,1024]{4,3,2,1,0:T(8,128)(2,1)S(1)}, bf16[2,2,2,80,1024]{4,3,2,1,0:T(8,128)(2,1)S(1)}, u32[]{:S(2)}, u32[]{:S(2)}) collective-permute-start(bf16[2,2,2,80,1024]{4,3,2,1,0:T(8,128)(2,1)S(1)} %fusion.33), channel_id=1, source_target_pairs={{0,8},{1,9},{2,10},{3,11},{4,12},{5,13},{6,14},{7,15},{8,0},{9,1},... | collective-permute-start | bytes 3932168 | tf_op jit(solution)/shard_map/ppermute | solution.py:280
  716.3 38.1 %collective-permute-start.28 = (bf16[64,1024]{1,0:T(8,128)(2,1)S(1)}, bf16[64,1024]{1,0:T(8,128)(2,1)S(1)}, u32[]{:S(2)}, u32[]{:S(2)}) collective-permute-start(bf16[64,1024]{1,0:T(8,128)(2,1)S(1)} %fusion.65), channel_id=1, source_target_pairs={{0,4},{1,5},{2,6},{3,7},{4,0},{5,1},{6,2},{7,3},{8,12},{9,13},{10,... | collective-permute-start | bytes 393224 | tf_op jit(solution)/shard_map/ppermute | solution.py:280
  719.9 53.7 %collective-permute-start.41 = (bf16[2,2,128,1024]{3,2,0,1:T(8,128)(2,1)S(1)}, bf16[2,2,128,1024]{3,2,0,1:T(8,128)(2,1)S(1)}, u32[]{:S(2)}, u32[]{:S(2)}) collective-permute-start(bf16[2,2,128,1024]{3,2,0,1:T(8,128)(2,1)S(1)} %copy.127), channel_id=1, source_target_pairs={{0,8},{1,9},{2,10},{3,11},{4,12},{5,13},{6,14},{7,15},{8,0},{9,1},... | collective-permute-start | bytes 3145736 | tf_op jit(solution)/shard_map/ppermute | solution.py:280
  725.5 50.6 %collective-permute-start.46 = (bf16[2,2,128,1024]{3,2,1,0:T(8,128)(2,1)S(1)}, bf16[2,2,128,1024]{3,2,1,0:T(8,128)(2,1)S(1)}, u32[]{:S(2)}, u32[]{:S(2)}) collective-permute-start(bf16[2,2,128,1024]{3,2,1,0:T(8,128)(2,1)S(1)} %fusion.14), channel_id=1, source_target_pairs={{0,16},{1,17},{2,18},{3,19},{4,20},{5,21},{6,22},{7,23},{8,24},{9,... | collective-permute-start | bytes 3145736 | tf_op jit(solution)/shard_map/ppermute | solution.py:280
  728.9 49.7 %collective-permute-start.31 = (bf16[2,2,96,1024]{3,2,0,1:T(8,128)(2,1)S(1)}, bf16[2,2,96,1024]{3,2,0,1:T(8,128)(2,1)S(1)}, u32[]{:S(2)}, u32[]{:S(2)}) collective-permute-start(bf16[2,2,96,1024]{3,2,0,1:T(8,128)(2,1)S(1)} %copy.117), channel_id=1, source_target_pairs={{0,16},{1,17},{2,18},{3,19},{4,20},{5,21},{6,22},{7,23},{8,24},{9,... | collective-permute-start | bytes 2359304 | tf_op jit(solution)/shard_map/ppermute | solution.py:280
  779.8 41.1 %collective-permute-start.32 = (bf16[2,96,1024]{2,1,0:T(8,128)(2,1)S(1)}, bf16[2,96,1024]{2,1,0:T(8,128)(2,1)S(1)}, u32[]{:S(2)}, u32[]{:S(2)}) collective-permute-start(bf16[2,96,1024]{2,1,0:T(8,128)(2,1)S(1)} %fusion.47), channel_id=1, source_target_pairs={{0,2},{1,3},{2,0},{3,1},{4,6},{5,7},{6,4},{7,5},{8,10},{9,11},{10,... | collective-permute-start | bytes 1179656 | tf_op jit(solution)/shard_map/ppermute | solution.py:280
  781.8 43.6 %collective-permute-start.22 = (bf16[2,80,1024]{2,1,0:T(8,128)(2,1)S(1)}, bf16[2,80,1024]{2,1,0:T(8,128)(2,1)S(1)}, u32[]{:S(2)}, u32[]{:S(2)}) collective-permute-start(bf16[2,80,1024]{2,1,0:T(8,128)(2,1)S(1)} %fusion.48), channel_id=1, source_target_pairs={{0,2},{1,3},{2,0},{3,1},{4,6},{5,7},{6,4},{7,5},{8,10},{9,11},{10,... | collective-permute-start | bytes 983048 | tf_op jit(solution)/shard_map/ppermute | solution.py:280
  791.1 35.9 %collective-permute-start.43 = (bf16[128,1024]{1,0:T(8,128)(2,1)S(1)}, bf16[128,1024]{1,0:T(8,128)(2,1)S(1)}, u32[]{:S(2)}, u32[]{:S(2)}) collective-permute-start(bf16[128,1024]{1,0:T(8,128)(2,1)S(1)} %fusion.51), channel_id=1, source_target_pairs={{0,4},{1,5},{2,6},{3,7},{4,0},{5,1},{6,2},{7,3},{8,12},{9,13},{10,... | collective-permute-start | bytes 786440 | tf_op jit(solution)/shard_map/ppermute | solution.py:280
  (115 other events, 3391.3 us)
Sparse Core Ops, SparseCore 0:
  11.6 76.2 all-gather.4
  90.8 225.9 all-gather.6

commit v2 on v1

v2 whole, which is shorter than its diff:
```python
from functools import partial

import jax
import jax.numpy as jnp
from jax import lax
from jax.experimental import pallas as pl
from jax.experimental.pallas import tpu as pltpu
from jax.sharding import PartitionSpec as P

HEAD_DIM = 64
PAIR = 2 * HEAD_DIM
VIEWS = 4
VIEW_PATCHES = 1024
BOTH = ("obj", "ring", "core")
SEQ = ("ring", "core")

epsilon = 1e-05
f32 = jnp.float32
bf16 = jnp.bfloat16
NN = (((1,), (0,)), ((), ()))
NT = (((1,), (1,)), ((), ()))
TN = (((0,), (0,)), ((), ()))


def dot(left, right, dims=NN):
    return lax.dot_general(left, right, dims, preferred_element_type=f32)


def params(megabytes=56):
    return pltpu.CompilerParams(vmem_limit_bytes=megabytes * 2**20)


def norm_parts(values):
    center = values - jnp.mean(values, -1, keepdims=True)
    spread = jnp.mean(center * center, -1, keepdims=True)
    scale = lax.rsqrt(spread + epsilon)
    return center * scale, scale


def norm_back(unit, scale, grad):
    return scale * (
        grad - jnp.mean(grad, -1, keepdims=True) - unit * jnp.mean(grad * unit, -1, keepdims=True)
    )


def attend_kernel(count, masked, *refs):
    q_ref, kv = refs[0], refs[1 : 1 + count]
    bias = refs[1 + count] if masked else None
    o_ref, lse_ref = refs[-2:]
    query = q_ref[...]
    keys = jnp.concatenate([r[:, :PAIR] for r in kv], 0)
    values = jnp.concatenate([r[:, PAIR:] for r in kv], 0)
    low = lax.broadcasted_iota(jnp.int32, query.shape, 1) < HEAD_DIM
    outs, lses = [], []
    for head in range(2):
        mine = low if head == 0 else ~low
        score = dot(jnp.where(mine, query, jnp.zeros_like(query)), keys, NT)
        if masked:
            score = score + bias[...]
        top = jnp.max(score, 1, keepdims=True)
        lifted = jnp.exp(score - top)
        total = jnp.sum(lifted, 1, keepdims=True)
        outs.append(dot(lifted.astype(bf16), values) * (1.0 / total))
        lses.append(top + jnp.log(total))
    o_ref[...] = jnp.where(low, outs[0], outs[1]).astype(bf16)
    lse_ref[...] = jnp.where(low, lses[0], lses[1])[None]


def attend(query, kvs, bias):
    rows, width = query.shape
    count, slots, pairs = len(kvs), kvs[0].shape[0], width // PAIR
    row = pl.BlockSpec((rows, PAIR), lambda i: (0, i))
    slot = pl.BlockSpec((slots, 2 * PAIR), lambda i: (0, i))
    masked = bias is not None
    total = count * slots
    return pl.pallas_call(
        partial(attend_kernel, count, masked),
        grid=(pairs,),
        in_specs=[row] + [slot] * count + [pl.BlockSpec((1, total), lambda i: (0, 0))] * masked,
        out_specs=[row, pl.BlockSpec((1, rows, PAIR), lambda i: (i, 0, 0))],
        out_shape=[
            jax.ShapeDtypeStruct((rows, width), bf16),
            jax.ShapeDtypeStruct((pairs, rows, PAIR), f32),
        ],
        compiler_params=params(),
        name="attend",
        cost_estimate=pl.CostEstimate(
            flops=16 * rows * total * width,
            bytes_accessed=4 * width * (rows + total),
            transcendentals=2 * pairs * rows * total,
        ),
    )(query, *kvs, *([bias] if masked else []))


def attend_back_kernel(count, masked, *refs):
    q_ref, kv = refs[0], refs[1 : 1 + count]
    o_ref, do_ref, lse_ref = refs[1 + count : 4 + count]
    bias = refs[4 + count] if masked else None
    dq_ref, dkv = refs[-1 - count], refs[-count:]
    query, grad = q_ref[...], do_ref[...]
    slots = kv[0].shape[0]
    keys = jnp.concatenate([r[:, :PAIR] for r in kv], 0)
    values = jnp.concatenate([r[:, PAIR:] for r in kv], 0)
    low = lax.broadcasted_iota(jnp.int32, query.shape, 1) < HEAD_DIM
    lse = lse_ref[0]
    product = o_ref[...].astype(f32) * grad.astype(f32)
    dk = dv = 0.0
    dqs = []
    for head in range(2):
        mine = low if head == 0 else ~low
        head_query = jnp.where(mine, query, jnp.zeros_like(query))
        head_grad = jnp.where(mine, grad, jnp.zeros_like(grad))
        score = dot(head_query, keys, NT)
        if masked:
            score = score + bias[...]
        probs = jnp.exp(score - lse[:, HEAD_DIM * head : HEAD_DIM * head + 1])
        delta = jnp.sum(jnp.where(mine, product, 0.0), 1, keepdims=True)
        score_grad = (probs * (dot(head_grad, values, NT) - delta)).astype(bf16)
        dk = dk + dot(jnp.transpose(head_query), score_grad)
        dv = dv + dot(jnp.transpose(head_grad), probs.astype(bf16))
        dqs.append(dot(score_grad, keys))
    dq_ref[...] = (jnp.where(low, dqs[0], dqs[1]) * HEAD_DIM**-0.5).astype(bf16)
    dk, dv = jnp.transpose(dk), jnp.transpose(dv)
    for j in range(count):
        dkv[j][:, :PAIR] = dk[j * slots : (j + 1) * slots].astype(bf16)
        dkv[j][:, PAIR:] = dv[j * slots : (j + 1) * slots].astype(bf16)


def attend_back(query, kvs, out, grad, lse, bias):
    rows, width = query.shape
    count, slots, pairs = len(kvs), kvs[0].shape[0], width // PAIR
    row = pl.BlockSpec((rows, PAIR), lambda i: (0, i))
    slot = pl.BlockSpec((slots, 2 * PAIR), lambda i: (0, i))
    masked = bias is not None
    total = count * slots
    result = pl.pallas_call(
        partial(attend_back_kernel, count, masked),
        grid=(pairs,),
        in_specs=[row]
        + [slot] * count
        + [row, row, pl.BlockSpec((1, rows, PAIR), lambda i: (i, 0, 0))]
        + [pl.BlockSpec((1, total), lambda i: (0, 0))] * masked,
        out_specs=[row] + [slot] * count,
        out_shape=[jax.ShapeDtypeStruct((rows, width), bf16)]
        + [jax.ShapeDtypeStruct((slots, 2 * width), bf16)] * count,
        compiler_params=params(),
        name="attend_back",
        cost_estimate=pl.CostEstimate(
            flops=40 * rows * total * width,
            bytes_accessed=8 * width * (rows + total),
            transcendentals=2 * pairs * rows * total,
        ),
    )(query, *kvs, out, grad, lse, *([bias] if masked else []))
    return result[0], result[1:]


def block_kernel(third_ref, cot_ref, gain_ref, shift_ref, dbias_ref, ubias_ref, up_ref, down_ref,
                 result_ref, tgrad_ref, grads_ref, vec_ref, ubgrad_ref,
                 unit_s, final_s, final_t, out_s, fgrad_s, scale_s, wide_s, tall_s, sems):
    step = pl.program_id(0)
    last = pl.num_programs(0) - 1
    slot = lax.rem(step, 2)
    _, parts, shard, tile = wide_s.shape
    _, spread, tall, width = tall_s.shape
    per = width // tile

    def copies(at, place):
        row = pl.multiple_of((at // per) * shard, shard)
        lane = pl.multiple_of(lax.rem(at, per) * tile, tile)
        return (
            pltpu.make_async_copy(
                wide_s.at[place],
                grads_ref.at[:, pl.ds(row, shard), pl.ds(lane, tile)],
                sems.at[0, place],
            ),
            pltpu.make_async_copy(
                tall_s.at[place],
                grads_ref.at[pl.ds(at * spread, spread), pl.ds(tall, tall), :],
                sems.at[1, place],
            ),
        )

    @pl.when(step == 0)
    def _():
        unit, scale = norm_parts(third_ref[...])
        unit_s[...] = unit
        scale_s[...] = scale
        final = (unit * gain_ref[...] + shift_ref[...]).astype(bf16)
        final_s[...] = final
        final_t[...] = jnp.transpose(final)
        out_s[...] = jnp.zeros_like(out_s)
        fgrad_s[...] = jnp.zeros_like(fgrad_s)

    @pl.when(step >= 2)
    def _():
        for copy in copies(step - 2, slot):
            copy.wait()

    cot = cot_ref[...]
    up = up_ref[...].reshape(-1, up_ref.shape[-1])
    down = down_ref[...].reshape(-1, down_ref.shape[-1])
    upper = dot(final_s[...], up) + ubias_ref[...]
    cdf = 0.5 * (1.0 + lax.erf(upper * (0.5**0.5)))
    active = (upper * cdf).astype(bf16)
    slope = cdf + upper * (jnp.exp(-0.5 * upper * upper) * 0.3989422804014327)
    ugrad = (slope * dot(cot, down, NT)).astype(bf16)
    out_s[...] += dot(active, down)
    fgrad_s[...] += dot(ugrad, up, NT)
    ubgrad_ref[...] = jnp.sum(ugrad.astype(f32), 0, keepdims=True)
    wide_s[slot] = dot(final_t[...], ugrad).astype(bf16).reshape(wide_s.shape[1:])
    tall_s[slot] = dot(jnp.transpose(active), cot).astype(bf16).reshape(tall_s.shape[1:])
    for copy in copies(step, slot):
        copy.start()

    @pl.when(step == last)
    def _():
        result_ref[...] = (third_ref[...] + (out_s[...] + dbias_ref[...])).astype(bf16)
        unit, fgrad, cotf = unit_s[...], fgrad_s[...], cot.astype(f32)
        tgrad_ref[...] = cotf + norm_back(unit, scale_s[...], fgrad * gain_ref[...])
        vec_ref[...] = jnp.zeros_like(vec_ref)
        vec_ref[0:1, :] = jnp.sum(fgrad * unit, 0, keepdims=True)
        vec_ref[1:2, :] = jnp.sum(fgrad, 0, keepdims=True)
        vec_ref[2:3, :] = jnp.sum(cotf, 0, keepdims=True)
        for copy in copies(step - 1, 1 - slot) + copies(step, slot):
            copy.wait()


def feed_forward(third, cot, gain, shift, down_bias, up_bias, packed, shard):
    rows, width = third.shape
    parts = packed.shape[0]
    hidden = up_bias.shape[1]
    tile = 512
    per = width // tile
    tall = hidden // parts
    spread = tile // tall
    steps = hidden // tile
    whole = lambda shape: pl.BlockSpec(shape, lambda j: (0,) * len(shape))
    return pl.pallas_call(
        block_kernel,
        grid=(steps,),
        in_specs=[
            whole((rows, width)),
            whole((rows, width)),
            whole((1, width)),
            whole((1, width)),
            whole((1, width)),
            pl.BlockSpec((1, tile), lambda j: (0, j)),
            pl.BlockSpec((parts, shard, tile), lambda j: (0, j // per, j % per)),
            pl.BlockSpec((spread, tall, width), lambda j: (j, 1, 0)),
        ],
        out_specs=[
            whole((rows, width)),
            whole((rows, width)),
            pl.BlockSpec(memory_space=pl.ANY),
            whole((8, width)),
            pl.BlockSpec((1, tile), lambda j: (0, j)),
        ],
        scratch_shapes=[
            pltpu.VMEM((rows, width), f32),
            pltpu.VMEM((rows, width), bf16),
            pltpu.VMEM((width, rows), bf16),
            pltpu.VMEM((rows, width), f32),
            pltpu.VMEM((rows, width), f32),
            pltpu.VMEM((rows, 1), f32),
            pltpu.VMEM((2, parts, shard, tile), bf16),
            pltpu.VMEM((2, spread, tall, width), bf16),
            pltpu.SemaphoreType.DMA((2, 2)),
        ],
        out_shape=[
            jax.ShapeDtypeStruct((rows, width), bf16),
            jax.ShapeDtypeStruct((rows, width), f32),
            jax.ShapeDtypeStruct((parts, 2 * tall, width), bf16),
            jax.ShapeDtypeStruct((8, width), f32),
            jax.ShapeDtypeStruct((1, hidden), f32),
        ],
        compiler_params=params(),
        name="feed_forward",
        cost_estimate=pl.CostEstimate(
            flops=12 * rows * width * hidden,
            bytes_accessed=8 * width * hidden + 12 * rows * width,
            transcendentals=2 * rows * hidden,
        ),
    )(third, cot, gain, shift, down_bias, up_bias, packed, packed)


def grads_kernel(jobs, core_ref, *refs):
    ins, (keep_ref, send_ref) = refs[:-2], refs[-2:]
    step = pl.program_id(0)
    half, room, width = keep_ref.shape

    def store(block, rows):
        block = block.astype(bf16).reshape(half, 2, rows, width)
        keep_ref[:, :rows] = block[:, 0]
        send_ref[:, :rows] = block[:, 1]

    def swapped(block, rows):
        block = block.astype(bf16).reshape(half, 2, rows, width)
        keep_ref[:, :rows] = block[:, 1]
        send_ref[:, :rows] = block[:, 0]

    for at, (left, right, column) in enumerate(jobs):

        @pl.when(step == at)
        def _():
            rows = ins[left].shape[1] // (2 * half)
            if rows < room:
                keep_ref[...] = jnp.zeros_like(keep_ref)
                send_ref[...] = jnp.zeros_like(send_ref)
            block = dot(ins[left][...], ins[right][:, column * width : (column + 1) * width], TN)

            @pl.when(core_ref[0] == 0)
            def _():
                store(block, rows)

            @pl.when(core_ref[0] == 1)
            def _():
                swapped(block, rows)


def weight_grads(core, arrays, jobs, parts, shard, width):
    count = len(jobs)
    whole = lambda array: pl.BlockSpec(array.shape, lambda j, c: (0, 0))
    out = pl.BlockSpec((parts // 2, shard, width), lambda j, c: (0, j, 0))
    flops = sum(2 * arrays[i].shape[0] * arrays[i].shape[1] * width for i, _, _ in jobs)
    return pl.pallas_call(
        partial(grads_kernel, jobs),
        grid_spec=pltpu.PrefetchScalarGridSpec(
            num_scalar_prefetch=1,
            grid=(count,),
            in_specs=[whole(array) for array in arrays],
            out_specs=[out, out],
        ),
        out_shape=[jax.ShapeDtypeStruct((parts // 2, count * shard, width), bf16)] * 2,
        compiler_params=params(),
        name="weight_grads",
        cost_estimate=pl.CostEstimate(
            flops=flops,
            bytes_accessed=2 * parts * count * shard * width + sum(2 * a.size for a in arrays),
            transcendentals=0,
        ),
    )(core, *arrays)


class Grid:
    def __init__(self, mesh):
        self.obj, self.seq = mesh.shape["obj"], mesh.shape["ring"] * 2
        self.all = self.obj * self.seq
        self.place = lax.axis_index("ring") * 2 + lax.axis_index("core")
        self.me = lax.axis_index("obj") * self.seq + self.place
        self.group = [m for m in (1 << k for k in range(20)) if m < self.seq // 2]
        self.far = self.seq // 2

    def swap(self, value, mask):
        return lax.ppermute(value, BOTH, [(i, i ^ mask) for i in range(self.all)])

    def bit(self, mask):
        return (self.me // mask) % 2

    def gather_group(self, value):
        found = {0: value}
        for mask in self.group[1:][::-1] + self.group[:1]:
            found.update({d ^ mask: self.swap(v, mask) for d, v in list(found.items())})
        return [found[d] for d in range(self.seq // 2)]

    def sum_group(self, terms):
        terms = {d: [t] for d, t in enumerate(terms)}
        for mask in self.group[:1] + self.group[1:]:
            for d in [d for d in terms if d & mask]:
                moved = self.swap(add(terms.pop(d)), mask)
                terms[d ^ mask].append(moved)
        return add(terms[0])

    def scatter(self, keep, send):
        moved = yield self.swap(send, 1)
        total = add([keep, moved]).reshape(self.obj, self.seq // 2, *keep.shape[1:])
        total = yield total
        moved = yield lax.all_to_all(total, "obj", 0, 0, tiled=True)
        total = jnp.sum(moved.astype(f32), 0).astype(bf16)
        moved = yield lax.all_to_all(total, "ring", 0, 0, tiled=True)
        yield jnp.sum(moved.astype(f32), 0)

    def exchange_core(self, terms):
        return [self.swap(t, 1) for t in terms[1::2]]

    def exchange_line(self, terms, moved):
        pairs = [add([t, m]) for t, m in zip(terms[::2], moved)]
        step = len(pairs) // 2
        while step > 1:
            pairs = [add([pairs[k], self.swap(pairs[k + step], 2 * step)]) for k in range(step)]
            step //= 2
        return pairs[0], self.swap(pairs[1], 2)


together = lax.optimization_barrier


def add(terms):
    if len(terms) == 1:
        return terms[0]
    return sum(t.astype(f32) for t in terms).astype(bf16)


def split_pairs(matrix):
    rows, width = matrix.shape
    return matrix.reshape(rows, 2, width // (2 * PAIR), PAIR).transpose(0, 2, 1, 3).reshape(rows, width)


def join_pairs(matrix):
    rows, width = matrix.shape
    return matrix.reshape(rows, width // (2 * PAIR), 2, PAIR).transpose(0, 2, 1, 3).reshape(rows, width)


def stack_columns(matrix, width):
    rows = matrix.shape[0]
    return matrix.reshape(rows, -1, width).transpose(1, 0, 2).reshape(-1, width)


def unstack_columns(matrix, rows):
    width = matrix.shape[1]
    return matrix.reshape(-1, rows, width).transpose(1, 0, 2).reshape(rows, -1)


def pad_rows(matrix, rows):
    return jnp.pad(matrix, ((0, rows - matrix.shape[0]), (0, 0)))


def on_device(
    mesh,
    tokens,
    camera,
    patches,
    patch_count,
    patch_index,
    cotangent,
    camera_weight,
    self_weight,
    self_output,
    mid_gain,
    mid_bias,
    patch_weight,
    view_table,
    cross_query,
    cross_memory,
    cross_output,
    last_gain,
    last_bias,
    up_weight,
    up_bias,
    down_weight,
    down_bias,
):
    grid = Grid(mesh)
    parts = grid.all
    width = self_output.shape[1]
    low = lambda v: v.astype(bf16)
    factor = HEAD_DIM**-0.5
    core = grid.bit(1)
    half = grid.bit(grid.far)

    def compact(value):
        mine = lax.dynamic_index_in_dim(value, half, 0, keepdims=False)
        other = lax.dynamic_index_in_dim(value, 1 - half, 0, keepdims=False)
        return jnp.concatenate([mine, grid.swap(other, grid.far)], 0)

    def spread(value):
        rows = value.shape[0] // 2
        mine, other = value[:rows], grid.swap(value[rows:], grid.far)
        return jnp.where(half == 0, jnp.stack([mine, other]), jnp.stack([other, mine]))

    shard = self_output.shape[0]
    self_mixed = jnp.concatenate(
        [low(self_weight[:, :width]), split_pairs(low(self_weight[:, width:]))], 1
    )
    small = jnp.concatenate(
        [
            low(camera_weight).reshape(-1),
            low(view_table).reshape(-1),
            low(mid_gain),
            low(mid_bias),
            low(last_gain),
            low(last_bias),
            low(down_bias),
            low(up_bias),
        ]
    )
    small_sizes = [
        camera_weight.size,
        view_table.size,
        shard,
        shard,
        shard,
        shard,
        shard,
        up_bias.size,
    ]
    patch_rows = patch_weight.shape[0]
    small_count = -(-small.size // width)
    patch_room = -(-(patch_rows + small_count) // shard) * shard
    small_rows = jnp.pad(small, (0, small_count * width - small.size)).reshape(-1, width)
    first = jnp.concatenate(
        [
            stack_columns(self_mixed, width),
            low(self_output),
            low(cross_query),
            low(cross_output),
            stack_columns(split_pairs(low(cross_memory)), width),
            pad_rows(jnp.concatenate([low(patch_weight), small_rows], 0), patch_room),
        ],
        0,
    )
    tokens_all = jnp.concatenate(grid.gather_group(compact(tokens)), 0)
    feats_all = jnp.concatenate(grid.gather_group(compact(patches)), 0)
    views_all = jnp.concatenate(grid.gather_group(compact(patch_index)), 0) // VIEW_PATCHES
    cot = compact(cotangent)
    first = lax.all_gather(first, BOTH, axis=0, tiled=False)
    ffn_mine = jnp.concatenate([stack_columns(low(up_weight), width), low(down_weight)], 0)
    first, ffn_mine, tokens_all, feats_all, views_all, cot = together(
        (first, ffn_mine, tokens_all, feats_all, views_all, cot)
    )
    packed = lax.all_gather(ffn_mine, BOTH, axis=0, tiled=False)

    def square(start, rows=shard):
        return first[:, start : start + rows].reshape(parts * rows, width)

    def columns(start, count):
        return jnp.concatenate([square(start + q * shard) for q in range(count)], 1)

    full_q = square(0)
    full_kv = columns(shard, 2)
    full_out = square(3 * shard)
    full_cq = square(4 * shard)
    full_co = square(5 * shard)
    full_mem = columns(6 * shard, 2)
    full_patch = square(8 * shard, patch_rows)
    at = 8 * shard + patch_rows
    tiny = first[:, at : at + small_count].reshape(parts, -1)
    pieces = []
    at = 0
    for size in small_sizes:
        pieces.append(tiny[:, at : at + size].astype(f32))
        at += size
    full_camera = pieces[0].reshape(parts, 16, -1).transpose(1, 0, 2).reshape(16, -1)
    full_view = pieces[1].reshape(parts, VIEWS, -1).transpose(1, 0, 2).reshape(VIEWS, -1)
    g_mid, b_mid, g_last, b_last, b_down, b_up = (p.reshape(1, -1) for p in pieces[2:])

    own = tokens_all.shape[0] // (grid.seq // 2)
    slots_own = feats_all.shape[0] // (grid.seq // 2)
    x_all = tokens_all.astype(f32)
    x = x_all[:own]
    camera_mine = lax.dynamic_index_in_dim(camera, half, 0, keepdims=False)
    live = lax.dynamic_index_in_dim(patch_count, half, 0, keepdims=False)
    modulation = jnp.sum(camera_mine[:, None] * full_camera, 0)
    scale1, shift1 = 1.0 + modulation[None, :width], modulation[None, width:]
    unit_all, rstd_all = norm_parts(x_all)
    unit1, rstd1 = unit_all[:own], rstd_all[:own]
    hidden_all = low(unit_all * scale1 + shift1)
    hidden = hidden_all[:own]
    query = low(low(dot(hidden, full_q)).astype(f32) * factor)
    kvs = [low(dot(hidden_all, full_kv))]

    hot_all = (views_all[:, None] == jnp.arange(VIEWS)[None, :]).astype(f32)
    view_part = sum(hot_all[:, v : v + 1] * full_view[v : v + 1] for v in range(VIEWS))
    embedded_all = low(dot(feats_all, full_patch) + view_part)
    mems = [low(dot(embedded_all, full_mem))]
    place = grid.place
    chunk = patches.shape[1]
    lane = jnp.arange(chunk)
    slots = jnp.concatenate(
        [
            chunk * (place ^ d ^ far) + lane
            for d in range(grid.seq // 2)
            for far in (0, grid.far)
        ]
    )
    bias = jnp.where(slots < live, 0.0, -1e30).astype(f32).reshape(1, -1)

    attended, lse1 = attend(query, kvs, None)
    second = x + dot(attended, full_out)
    unit2, rstd2 = norm_parts(second)
    normed = low(unit2 * g_mid + b_mid)
    asked = low(low(dot(normed, full_cq)).astype(f32) * factor)
    crossed, lse2 = attend(asked, mems, bias)
    third = second + dot(crossed, full_co)
    core_now = core.reshape(1).astype(jnp.int32)
    result, third_grad, ffn_grads, last_vectors, up_bias_grad = feed_forward(
        third, cot, g_last, b_last, b_down, b_up, packed, shard
    )
    ffn_grad = lax.psum_scatter(ffn_grads, BOTH, scatter_dimension=0, tiled=True)[0].astype(f32)
    tall = down_weight.shape[0]

    def chunks(terms):
        return jnp.split(terms, grid.seq // 2, 0)

    third_low = low(third_grad)
    crossed_grad = low(dot(third_low, full_co, NT))
    asked_grad, mem_terms = attend_back(asked, mems, crossed, crossed_grad, lse2, bias)
    mem_terms = mem_terms[0]
    normed_grad = dot(asked_grad, full_cq, NT)
    second_grad = third_grad + norm_back(unit2, rstd2, normed_grad * g_mid)
    second_low = low(second_grad)
    attended_grad = low(dot(second_low, full_out, NT))
    embedded_grad = low(dot(mem_terms, full_mem, NT))
    arrays = [
        crossed,
        third_low,
        normed,
        asked_grad,
        attended,
        second_low,
        embedded_all,
        mem_terms,
        feats_all,
        embedded_grad,
    ]
    jobs = ((0, 1, 0), (2, 3, 0), (4, 5, 0), (6, 7, 0), (6, 7, 1), (8, 9, 0))
    keep, send = weight_grads(core_now, arrays, jobs, parts, shard, width)
    rest = grid.scatter(keep, send)
    moved = next(rest)
    patch_terms = chunks(low(dot(embedded_grad, full_patch, NT)))
    patch_moved = grid.exchange_core(patch_terms)
    moved, patch_moved = together((moved, patch_moved))
    moved = rest.send(moved)
    moved, attended_grad = together((moved, attended_grad))

    moved = rest.send(moved)
    patch_mine, patch_moved = grid.exchange_line(patch_terms, patch_moved)
    query_grad, pair_terms = attend_back(query, kvs, attended, attended_grad, lse1, None)
    pair_terms = pair_terms[0]
    patch_moved, query_grad, pair_terms = together((patch_moved, query_grad, pair_terms))

    keep, send = weight_grads(
        core_now,
        [hidden, query_grad, hidden_all, pair_terms],
        ((0, 1, 0), (2, 3, 0), (2, 3, 1)),
        parts,
        shard,
        width,
    )
    own_scatter = grid.scatter(keep, send)
    own_moved = next(own_scatter)
    hidden_terms = chunks(low(dot(pair_terms, full_kv, NT)))
    hidden_moved = grid.exchange_core(hidden_terms)
    own_moved, hidden_moved = together((own_moved, hidden_moved))
    own_moved = own_scatter.send(own_moved)
    hidden_mine, hidden_moved = grid.exchange_line(hidden_terms, hidden_moved)
    hidden_query = dot(query_grad, full_q, NT)
    patch_grad = spread(low(patch_mine.astype(f32) + patch_moved.astype(f32)))
    result = spread(result)
    moved, own_moved, hidden_query, hidden_moved, result, patch_grad = together(
        (moved, own_moved, hidden_query, hidden_moved, result, patch_grad)
    )
    own_moved = own_scatter.send(own_moved)
    view_grad = jnp.stack(
        [jnp.sum(hot_all[:, v : v + 1] * embedded_grad.astype(f32), 0) for v in range(VIEWS)]
    )
    hidden_grad = hidden_query + hidden_mine.astype(f32) + hidden_moved.astype(f32)
    token_grad = low(second_grad + norm_back(unit1, rstd1, hidden_grad * scale1))
    token_grad = spread(token_grad)
    modulation_grad = jnp.concatenate(
        [jnp.sum(hidden_grad * unit1, 0), jnp.sum(hidden_grad, 0)]
    )
    camera_grad = camera_mine[:, None] * modulation_grad[None]
    vectors = jnp.concatenate(
        [
            view_grad,
            jnp.sum(normed_grad * unit2, 0)[None],
            jnp.sum(normed_grad, 0)[None],
            last_vectors[0:3],
        ],
        0,
    )
    small_grad = jnp.concatenate(
        [
            low(camera_grad).reshape(16, parts, -1).transpose(1, 0, 2).reshape(parts, -1),
            low(vectors).reshape(VIEWS + 5, parts, -1).transpose(1, 0, 2).reshape(parts, -1),
            low(up_bias_grad).reshape(parts, -1),
        ],
        1,
    )
    small_grad = jnp.pad(small_grad, ((0, 0), (0, small_count * width - small_grad.shape[1])))
    own_moved, small_grad = together((own_moved, small_grad))
    moved = rest.send(moved)
    small_grad = lax.all_to_all(small_grad.reshape(parts, small_count, width), BOTH, 0, 0, tiled=True)
    tiny = jnp.sum(small_grad.astype(f32), 0).reshape(-1)
    own_moved = own_scatter.send(own_moved)
    rest_sum = rest.send(moved)
    self_sum = own_scatter.send(own_moved)
    pieces = []
    at = 0
    for size in small_sizes:
        pieces.append(tiny[at : at + size])
        at += size
    kv_own = join_pairs(unstack_columns(self_sum[shard : 3 * shard], shard))
    return (
        result,
        token_grad,
        patch_grad,
        pieces[0].reshape(camera_weight.shape),
        jnp.concatenate([self_sum[:shard], kv_own], 1),
        rest_sum[2 * shard : 3 * shard],
        pieces[2],
        pieces[3],
        rest_sum[5 * shard : 5 * shard + patch_rows],
        pieces[1].reshape(view_table.shape),
        rest_sum[shard : 2 * shard],
        join_pairs(unstack_columns(rest_sum[3 * shard : 5 * shard], shard)),
        rest_sum[:shard],
        pieces[4],
        pieces[5],
        unstack_columns(ffn_grad[:tall], shard),
        pieces[7],
        ffn_grad[tall:],
        pieces[6],
    )


def solution(mesh):
    line = mesh.shape["seq"] // 2
    mesh = jax.sharding.Mesh(
        mesh.devices.reshape(mesh.shape["obj"], line, 2), ("obj", "ring", "core")
    )
    rows, flat, lanes = P(BOTH, None), P(BOTH), P(None, BOTH)
    sequence = P("obj", SEQ, None)
    in_specs = (
        sequence,
        P("obj", None),
        sequence,
        P("obj"),
        P("obj", SEQ),
        sequence,
        lanes,
        rows,
        rows,
        flat,
        flat,
        rows,
        lanes,
        rows,
        rows,
        rows,
        flat,
        flat,
        rows,
        flat,
        rows,
        flat,
    )
    out_specs = (
        sequence,
        sequence,
        sequence,
        lanes,
        rows,
        rows,
        flat,
        flat,
        rows,
        lanes,
        rows,
        rows,
        rows,
        flat,
        flat,
        rows,
        flat,
        rows,
        flat,
    )
    return jax.shard_map(
        partial(on_device, mesh),
        mesh=mesh,
        in_specs=in_specs,
        out_specs=out_specs,
        check_vma=False,
    )
```

time: 864 us -> 688 us (0.80)
  waiting for transfers between devices: 481 us -> 297 us
  Pallas kernels: 118 us -> 149 us
  other arithmetic: 74.1 us -> 65.3 us
    ppermute x49 -> x24, waiting for transfers between devices: 319 us -> 178 us  [swap(): return lax.ppermute(value, BOTH, [(i, i ^ mask) for i in range(self.all)])]
    all_gather x1, waiting for transfers between devices: 85.5 us -> 19.6 us  [on_device(): packed = lax.all_gather(ffn_mine, BOTH, axis=0, tiled=False)]
    all_to_all x0 -> x5, waiting for transfers between devices: none -> 54.3 us  [the longest x2 30.9 us: scatter(): moved = (yield lax.all_to_all(total, 'obj', 0, 0, tiled=True))]
    pallas_call x1 -> x3, Pallas kernels: 32.6 us -> 64.4 us  [the longest x2 34.2 us: weight_grads(): pl.pallas_call(partial(grads_kernel, jobs), grid_spec=pltpu.PrefetchScala...]
    all_gather x1, waiting for transfers between devices: 76.5 us -> 45 us  [on_device(): first = lax.all_gather(first, BOTH, axis=0, tiled=False)]
    ppermute x49 -> x24, starting transfers between devices: 43.9 us -> 18.8 us  [swap(): return lax.ppermute(value, BOTH, [(i, i ^ mask) for i in range(self.all)])]
    convert_element_type x26 -> x4, other arithmetic: 36.5 us -> 14.7 us  [add(): return sum((t.astype(f32) for t in terms)).astype(bf16)]
    all_to_all x0 -> x5, starting transfers between devices: none -> 21.5 us  [the longest x2 10.1 us: scatter(): moved = (yield lax.all_to_all(total, 'obj', 0, 0, tiled=True))]
  transfers between devices with their start and end apart: 51 -> 32, of which waited for: 24 -> 13; matrix products, arithmetic and copies ran while one was open for 20% -> 24% of each run, Pallas kernels for 8% -> 17%
where the time goes in v2:
time: 688 us; the launch traced here: 681 us
  waiting for transfers between devices  297 us (43%)
  Pallas kernels  149 us (22%)
  other arithmetic  65.3 us (9%)
  local copies, waits for them, and re-layouts  58.7 us (9%)
  matrix products  55 us (8%)
  starting transfers between devices  40.4 us (6%)
  between operations  15.5 us (2%)
    ppermute x24, waiting for transfers between devices, swap(): return lax.ppermute(value, BOTH, [(i, i ^ mask) for i in range(self.all)])  178 us
    dot_general x14, matrix products, dot(): return lax.dot_general(left, right, dims, preferred_element_type=f32)  55 us
    pallas_call x2, Pallas kernels, attend_back(): pl.pallas_call(partial(attend_back_kernel, count, masked), grid=(pairs,),...  49 us
    all_gather x1, waiting for transfers between devices, on_device(): first = lax.all_gather(first, BOTH, axis=0, tiled=False)  45 us
    pallas_call x2, Pallas kernels, attend(): pl.pallas_call(partial(attend_kernel, count, masked), grid=(pairs,), in_s...  36 us
    pallas_call x2, Pallas kernels, weight_grads(): pl.pallas_call(partial(grads_kernel, jobs), grid_spec=pltpu.PrefetchScala...  34.2 us
    all_to_all x2, waiting for transfers between devices, scatter(): moved = (yield lax.all_to_all(total, 'obj', 0, 0, tiled=True))  30.9 us
    pallas_call x1, Pallas kernels, feed_forward(): pl.pallas_call(block_kernel, grid=(steps,), in_specs=[whole((rows, width)...  30.2 us
  transfers between devices with their start and end apart: 32, of which 13 were waited for; matrix products, arithmetic and copies ran while one was open for 24% of the time, Pallas kernels for 17%

profile of v2, /device:TPU:0, one launch (start us, length us, event | category | flops | bytes accessed | tf_op | source)
XLA Modules:
  0.0 681.2 jit_solution(6426464195789136629)
XLA Ops:
  11.7 4.0 collective-permute-start
  27.1 36.9 %collective-permute-done.8 = s32[128]{0:T(128)S(1)} collective-permute-done((s32[128]{0:T(128)}, s32[128]{0:T(128)S(1)}, u32[]{:S(2)}, u32[]{:S(2)}) %collective-permute-start.8) | collective-permute-done | bytes 544 | tf_op jit(solution)/shard_map/ppermute | solution.py:354
  64.1 3.9 collective-permute-done.10
  74.1 53.6 %collective-permute-done.6 = bf16[256,768]{1,0:T(8,128)(2,1)S(1)} collective-permute-done((bf16[256,768]{1,0:T(8,128)(2,1)S(1)}, bf16[256,768]{1,0:T(8,128)(2,1)S(1)}, u32[]{:S(2)}, u32[]{:S(2)}) %collective-permute-start.6) | collective-permute-done | bytes 393248 | tf_op jit(solution)/shard_map/ppermute | solution.py:354
  131.6 45.0 %all-gather.5.cloned.1.call-done = bf16[9216,1024]{1,0:T(8,128)(2,1)} async-done(((bf16[288,1024]{1,0:T(8,128)(2,1)}), bf16[9216,1024]{1,0:T(8,128)(2,1)}) %all-gather.5.cloned.1.call-update) | async-done | bytes 18874384 | tf_op jit(solution)/shard_map/all_gather | solution.py:515
  193.6 10.3 %fusion.22 = (bf16[32,32,1024]{2,1,0:T(8,128)(2,1)}, bf16[32,32,1024]{2,1,0:T(8,128)(2,1)S(1)}, bf16[32,32,1024]{2,1,0:T(8,128)(2,1)}, bf16[32,32,1024]{2,1,0:T(...) fusion(bf16[32,288,1024]{2,1,0:T(8,128)(2,1)} %bitcast.155), kind=kLoop, calls=%fused_computation.170 | loop fusion | bytes 33554432 | tf_op jit(solution)/shard_map/slice | solution.py:523
  210.6 8.9 %convolution_convert_fusion.refs_1_ = bf16[1536,2048]{1,0:T(8,128)(2,1)} fusion(bf16[1536,1024]{1,0:T(8,128)(2,1)S(1)} %get-tuple-element.137.refs_2_, bf16[1024,1024]{1,0:T(8,128)(2,1)S(1)} %bitcast.159, bf16[1024,1024]{1,0:T(8,128)(2,1)S(1)} %bitcast.161), kind=kOutput, calls=%fused_computation.1 | convolution fusion | flops 6453985280 | bytes 13631488 | tf_op jit(solution)/shard_map/dot_general | solution.py:26
  219.5 20.9 %attend.2 = (bf16[384,1024]{1,0:T(8,128)(2,1)}, f32[8,384,128]{2,1,0:T(8,128)}) custom-call(bf16[384,1024]{1,0:T(8,128)(2,1)} %multiply_convert_fusion.1.refs_0_, bf16[1536,2048]{1,0:T(8,128)(2,1)} %convolution_convert_fusion.refs_1_), custom_call_target="tpu_custom_call" | custom-call | flops 9663676416 | bytes 7864320 | tf_op jit(solution)/shard_map/attend/pallas_call | solution.py:76
  250.9 6.4 convolution_convert_fusion.2.refs_1_
  257.3 15.1 %attend.3 = (bf16[384,1024]{1,0:T(8,128)(2,1)}, f32[8,384,128]{2,1,0:T(8,128)}) custom-call(bf16[384,1024]{1,0:T(8,128)(2,1)} %multiply_convert_fusion.refs_0_, bf16[1024,2048]{1,0:T(8,128)(2,1)} %convolution_convert_fusion.2.refs_1_, f32[1,1024]{1,0:T(1,128)} %compare_select_fusion.refs_2_.refs_5_), custom_call_target="tpu_custom_call" | custom-call | flops 6442450944 | bytes 5767168 | tf_op jit(solution)/shard_map/attend/pallas_call | solution.py:76
  275.7 19.6 %all-gather.7.cloned.1.call-done = bf16[8192,1024]{1,0:T(8,128)(2,1)} async-done(((bf16[256,1024]{1,0:T(8,128)(2,1)}), bf16[8192,1024]{1,0:T(8,128)(2,1)}) %all-gather.7.cloned.1.call-update) | async-done | bytes 16777232 | tf_op jit(solution)/shard_map/all_gather | solution.py:520
  295.3 30.2 %feed_forward.1 = (bf16[384,1024]{1,0:T(8,128)(2,1)}, f32[384,1024]{1,0:T(8,128)}, bf16[32,256,1024]{2,1,0:T(8,128)(2,1)}, f32[8,1024]{1,0:T(8,128)}, f32[1,4096]{1,0:T(1,128)}) custom-call(f32[384,1024]{1,0:T(8,128)} %convolution_add_fusion.third_ref, bf16[384,1024]{1,0:T(8,128)(2,1)} %pad_maximum_fusion.9.cot_ref, f32[1,1024]{1,0:T(1,128)} %reshape.444.gain_ref, ...), custom_call_target="tpu_custom_call" | custom-call | flops 19327352832 | bytes 38273024 | tf_op jit(solution)/shard_map/feed_forward/pallas_call | solution.py:238
  329.5 20.9 %attend_back.2 = (bf16[384,1024]{1,0:T(8,128)(2,1)}, bf16[1024,2048]{1,0:T(8,128)(2,1)}) custom-call(bf16[384,1024]{1,0:T(8,128)(2,1)} %multiply_convert_fusion.refs_0_, bf16[1024,2048]{1,0:T(8,128)(2,1)} %convolution_convert_fusion.2.refs_1_, bf16[384,1024]{1,0:T(8,128)(2,1)} %get-tuple-element.66.refs_2_.refs_0_, ...), custom_call_target="tpu_custom_call" | custom-call | flops 16106127360 | bytes 11534336 | tf_op jit(solution)/shard_map/attend_back/pallas_call | solution.py:136
  356.2 7.0 %fusion.3 = (bf16[1024]{0:T(1024)(128)(2,1)S(1)}, bf16[1024]{0:T(1024)(128)(2,1)}, bf16[1024]{0:T(1024)(128)(2,1)}, bf16[1024]{0:T(1024)(128)(2,1)}, bf16[1024,1024]{1,0:T(8,128)(2,1)}) fusion(f32[1024]{0:T(1024)S(1)} %bitcast.212, f32[1024]{0:T(1024)S(1)} %bitcast.216, f32[1024]{0:T(1024)S(1)} %bitcast.214, f32[1024]{0:T(1024)S(1)} %bitcast.210, ...), kind=kOutput, calls=%fused_computation.14 | convolution fusion | flops 4313837568 | bytes 10510336 | tf_op jit(solution)/shard_map/dot_general | solution.py:26
  363.2 19.5 %weight_grads.2 = (bf16[16,192,1024]{2,1,0:T(8,128)(2,1)}, bf16[16,192,1024]{2,1,0:T(8,128)(2,1)}) custom-call(s32[1]{0:T(128)} %bitcast.core_ref, bf16[384,1024]{1,0:T(8,128)(2,1)} %get-tuple-element.66.refs_2_.refs_0_, bf16[384,1024]{1,0:T(8,128)(2,1)} %copy-done.33, bf16[384,1024]{1,0:T(8,128)(2,1)} %copy-done.32, ...), custom_call_target="tpu_custom_call" | custom-call | flops 8321499136 | bytes 27262976 | tf_op jit(solution)/shard_map/weight_grads/pallas_call | solution.py:325
  390.4 4.2 collective-permute-done.13
  394.6 7.6 %add_convert_fusion = bf16[16,192,1024]{2,1,0:T(8,128)(2,1)} fusion(bf16[16,192,1024]{2,1,0:T(8,128)(2,1)} %collective-permute-done.13, bf16[16,192,1024]{2,1,0:T(8,128)(2,1)S(1)} %copy-done.2), kind=kLoop, calls=%fused_computation | loop fusion | flops 12582912 | bytes 18874368 | tf_op jit(solution)/shard_map/convert_element_type | solution.py:400
  402.2 5.5 all-to-all-start
  409.6 28.1 %attend_back.3 = (bf16[384,1024]{1,0:T(8,128)(2,1)}, bf16[1536,2048]{1,0:T(8,128)(2,1)}) custom-call(bf16[384,1024]{1,0:T(8,128)(2,1)} %multiply_convert_fusion.1.refs_0_, bf16[1536,2048]{1,0:T(8,128)(2,1)} %convolution_convert_fusion.refs_1_, bf16[384,1024]{1,0:T(8,128)(2,1)} %get-tuple-element.63.refs_4_.refs_2_, ...), custom_call_target="tpu_custom_call" | custom-call | flops 24159191040 | bytes 15728640 | tf_op jit(solution)/shard_map/attend_back/pallas_call | solution.py:136
  438.4 14.7 %weight_grads.3 = (bf16[16,96,1024]{2,1,0:T(8,128)(2,1)}, bf16[16,96,1024]{2,1,0:T(8,128)(2,1)}) custom-call(s32[1]{0:T(128)} %bitcast.core_ref, bf16[384,1024]{1,0:T(8,128)(2,1)} %slice.262.refs_0_, bf16[384,1024]{1,0:T(8,128)(2,1)} %get-tuple-element.82.refs_1_, bf16[1536,1024]{1,0:T(8,128)(2,1)} %copy-done.4, bf16[1536,2048]{1,0:T(8,128)(2,1)} %get-tuple-element.83.refs_3_), custom_call_target="tpu_custom_call" | custom-call | flops 7247757312 | bytes 17301504 | tf_op jit(solution)/shard_map/weight_grads/pallas_call | solution.py:325
  455.4 9.1 %convolution_convert_fusion.1 = bf16[1536,1024]{1,0:T(8,128)(2,1)S(1)} fusion(bf16[1536,2048]{1,0:T(8,128)(2,1)} %get-tuple-element.83.refs_3_, bf16[1024,1024]{1,0:T(8,128)(2,1)S(1)} %bitcast.160, bf16[1024,1024]{1,0:T(8,128)(2,1)S(1)} %bitcast.162), kind=kOutput, calls=%fused_computation.18 | convolution fusion | flops 6452412416 | bytes 13631488 | tf_op jit(solution)/shard_map/dot_general | solution.py:26
  466.4 26.5 %collective-permute-done.21 = bf16[192,1024]{1,0:T(8,128)(2,1)} collective-permute-done((bf16[192,1024]{1,0:T(8,128)(2,1)}, bf16[192,1024]{1,0:T(8,128)(2,1)}, u32[]{:S(2)}, u32[]{:S(2)}) %collective-permute-start.21) | collective-permute-done | bytes 393248 | tf_op jit(solution)/shard_map/ppermute | solution.py:354
  502.5 10.6 %collective-permute-done.22 = bf16[128,768]{1,0:T(8,128)(2,1)S(1)} collective-permute-done((bf16[128,768]{1,0:T(8,128)(2,1)S(1)}, bf16[128,768]{1,0:T(8,128)(2,1)S(1)}, u32[]{:S(2)}, u32[]{:S(2)}) %collective-permute-start.22) | collective-permute-done | bytes 196640 | tf_op jit(solution)/shard_map/ppermute | solution.py:354
  513.9 4.5 add_convert_fusion.1
  518.4 22.2 %collective-permute-done.20 = bf16[384,1024]{1,0:T(8,128)(2,1)} collective-permute-done((bf16[384,1024]{1,0:T(8,128)(2,1)S(1)}, bf16[384,1024]{1,0:T(8,128)(2,1)}, u32[]{:S(2)}, u32[]{:S(2)}) %collective-permute-start.20) | collective-permute-done | bytes 786464 | tf_op jit(solution)/shard_map/ppermute | solution.py:354
  540.6 4.6 all-to-all-start.1
  546.1 6.1 reduce_sum.224
  552.2 30.9 %all-to-all-done.1 = bf16[4,4,96,1024]{3,2,1,0:T(8,128)(2,1)S(1)} async-done(((bf16[4,4,96,1024]{3,2,1,0:T(8,128)(2,1)}), bf16[4,4,96,1024]{3,2,1,0:T(8,128)(2,1)S(1)}, u32[]{:S(2)}, u32[]{:S(2)}) %all-to-all-start.1) | async-done | bytes 3145760 | tf_op jit(solution)/shard_map/all_to_all | solution.py:377
  583.1 4.4 all-to-all-start.4
  590.2 5.1 multiply_reduce_fusion.2
  602.8 21.5 %all-to-all-done.4 = bf16[4,192,1024]{2,1,0:T(8,128)(2,1)} async-done(((bf16[4,192,1024]{2,1,0:T(8,128)(2,1)}), bf16[4,192,1024]{2,1,0:T(8,128)(2,1)}, u32[]{:S(2)}, u32[]{:S(2)}) %all-to-all-start.4) | async-done | bytes 1572896 | tf_op jit(solution)/shard_map/all_to_all | solution.py:379
  639.5 20.2 %collective-permute-done.23 = bf16[192,1024]{1,0:T(8,128)(2,1)} collective-permute-done((bf16[192,1024]{1,0:T(8,128)(2,1)}, bf16[192,1024]{1,0:T(8,128)(2,1)}, u32[]{:S(2)}, u32[]{:S(2)}) %collective-permute-start.23) | collective-permute-done | bytes 393248 | tf_op jit(solution)/shard_map/ppermute | solution.py:354
  (395 shorter events, 138.0 us)
Async XLA Ops:
  7.2 169.4 %all-gather.5.cloned.1.call-start = ((), (), s32[]{:S(2)}) async-start(), calls=%async_computation.7 | async-start | bytes 19464192 | tf_op jit(solution)/shard_map/all_gather | solution.py:515
  10.9 284.4 %all-gather.7.cloned.1.call-start = ((), (), s32[]{:S(2)}) async-start(), calls=%async_computation.8 | async-start | bytes 17301504 | tf_op jit(solution)/shard_map/all_gather | solution.py:520
  11.7 56.5 %collective-permute-start = (bf16[192,1024]{1,0:T(8,128)(2,1)}, bf16[192,1024]{1,0:T(8,128)(2,1)S(1)}, u32[]{:S(2)}, u32[]{:S(2)}) collective-permute-start(bf16[192,1024]{1,0:T(8,128)(2,1)} %dynamic-slice_bitcast_fusion.2), channel_id=1, source_target_pairs={{0,4},{1,5},{2,6},{3,7},{4,0},{5,1},{6,2},{7,3},{8,12},{9,13},{10,... | collective-permute-start | bytes 1179656 | tf_op jit(solution)/shard_map/ppermute | solution.py:354
  17.4 52.1 %collective-permute-start.4 = (bf16[128,768]{1,0:T(8,128)(2,1)}, bf16[128,768]{1,0:T(8,128)(2,1)}, u32[]{:S(2)}, u32[]{:S(2)}) collective-permute-start(bf16[128,768]{1,0:T(8,128)(2,1)} %dynamic-slice_bitcast_fusion.4), channel_id=1, source_target_pairs={{0,4},{1,5},{2,6},{3,7},{4,0},{5,1},{6,2},{7,3},{8,12},{9,13},{10,... | collective-permute-start | bytes 589832 | tf_op jit(solution)/shard_map/ppermute | solution.py:354
  17.9 46.0 %collective-permute-start.8 = (s32[128]{0:T(128)}, s32[128]{0:T(128)S(1)}, u32[]{:S(2)}, u32[]{:S(2)}) collective-permute-start(s32[128]{0:T(128)} %fusion.13), channel_id=1, source_target_pairs={{0,4},{1,5},{2,6},{3,7},{4,0},{5,1},{6,2},{7,3},{8,12},{9,13},{10,... | collective-permute-start | bytes 1544 | tf_op jit(solution)/shard_map/ppermute | solution.py:354
  21.8 106.5 %collective-permute-start.12 = (bf16[192,1024]{1,0:T(8,128)(2,1)}, bf16[192,1024]{1,0:T(8,128)(2,1)}, u32[]{:S(2)}, u32[]{:S(2)}) collective-permute-start(bf16[192,1024]{1,0:T(8,128)(2,1)} %get-tuple-element.150), channel_id=1, source_target_pairs={{0,4},{1,5},{2,6},{3,7},{4,0},{5,1},{6,2},{7,3},{8,12},{9,13},{10,... | collective-permute-start | bytes 1179656 | tf_op jit(solution)/shard_map/ppermute | solution.py:354
  64.0 5.5 collective-permute-start.9
  64.0 4.0 collective-permute-start.10
  68.0 4.6 collective-permute-start.11
  69.4 58.4 %collective-permute-start.2 = (bf16[384,1024]{1,0:T(8,128)(2,1)S(1)}, bf16[384,1024]{1,0:T(8,128)(2,1)S(1)}, u32[]{:S(2)}, u32[]{:S(2)}) collective-permute-start(bf16[384,1024]{1,0:T(8,128)(2,1)S(1)} %pad_maximum_fusion.8), channel_id=1, source_target_pairs={{0,2},{1,3},{2,0},{3,1},{4,6},{5,7},{6,4},{7,5},{8,10},{9,11},{10,... | collective-permute-start | bytes 2359304 | tf_op jit(solution)/shard_map/ppermute | solution.py:354
  70.5 57.2 %collective-permute-start.6 = (bf16[256,768]{1,0:T(8,128)(2,1)S(1)}, bf16[256,768]{1,0:T(8,128)(2,1)S(1)}, u32[]{:S(2)}, u32[]{:S(2)}) collective-permute-start(bf16[256,768]{1,0:T(8,128)(2,1)S(1)} %pad_maximum_fusion.11), channel_id=1, source_target_pairs={{0,2},{1,3},{2,0},{3,1},{4,6},{5,7},{6,4},{7,5},{8,10},{9,11},{10,... | collective-permute-start | bytes 1179656 | tf_op jit(solution)/shard_map/ppermute | solution.py:354
  72.6 57.7 %collective-permute-start.5 = (bf16[256,768]{1,0:T(8,128)(2,1)S(1)}, bf16[256,768]{1,0:T(8,128)(2,1)S(1)}, u32[]{:S(2)}, u32[]{:S(2)}) collective-permute-start(bf16[256,768]{1,0:T(8,128)(2,1)S(1)} %pad_maximum_fusion.11), channel_id=1, source_target_pairs={{0,1},{1,0},{2,3},{3,2},{4,5},{5,4},{6,7},{7,6},{8,9},{9,8},{10,11... | collective-permute-start | bytes 1179656 | tf_op jit(solution)/shard_map/ppermute | solution.py:354
  72.7 57.8 %collective-permute-start.1 = (bf16[384,1024]{1,0:T(8,128)(2,1)S(1)}, bf16[384,1024]{1,0:T(8,128)(2,1)S(1)}, u32[]{:S(2)}, u32[]{:S(2)}) collective-permute-start(bf16[384,1024]{1,0:T(8,128)(2,1)S(1)} %pad_maximum_fusion.8), channel_id=1, source_target_pairs={{0,1},{1,0},{2,3},{3,2},{4,5},{5,4},{6,7},{7,6},{8,9},{9,8},{10,11... | collective-permute-start | bytes 2359304 | tf_op jit(solution)/shard_map/ppermute | solution.py:354
  127.7 2.7 collective-permute-start.7
  127.7 2.9 collective-permute-start.3
  176.6 494.9 %reduce-scatter.2.cloned.1.call-start = ((), (), s32[]{:S(2)}) async-start(), calls=%async_computation.6 | async-start | bytes 17301504 | tf_op jit(solution)/shard_map/reduce_scatter | solution.py:588
  382.7 11.9 %collective-permute-start.13 = (bf16[16,192,1024]{2,1,0:T(8,128)(2,1)}, bf16[16,192,1024]{2,1,0:T(8,128)(2,1)}, u32[]{:S(2)}, u32[]{:S(2)}) collective-permute-start(bf16[16,192,1024]{2,1,0:T(8,128)(2,1)} %get-tuple-element.74), channel_id=1, source_target_pairs={{0,1},{1,0},{2,3},{3,2},{4,5},{5,4},{6,7},{7,6},{8,9},{9,8},{10,11... | collective-permute-start | bytes 18874376 | tf_op jit(solution)/shard_map/ppermute | solution.py:354
  384.9 4.8 collective-permute-start.14
  385.2 5.2 collective-permute-start.15
  402.2 138.4 %all-to-all-start = ((bf16[4,4,192,1024]{3,2,1,0:T(8,128)(2,1)}), bf16[4,4,192,1024]{3,2,1,0:T(8,128)(2,1)}, u32[]{:S(2)}, u32[]{:S(2)}) async-start(bf16[4,4,192,1024]{3,2,1,0:T(8,128)(2,1)} %bitcast.152), calls=%async_computation | async-start | bytes 12582912 | tf_op jit(solution)/shard_map/all_to_all | solution.py:377
  408.8 28.9 %collective-permute-start.16 = (bf16[256,768]{1,0:T(8,128)(2,1)S(1)}, bf16[256,768]{1,0:T(8,128)(2,1)S(1)}, u32[]{:S(2)}, u32[]{:S(2)}) collective-permute-start(bf16[256,768]{1,0:T(8,128)(2,1)S(1)} %add_convert_fusion.10), channel_id=1, source_target_pairs={{0,2},{1,3},{2,0},{3,1},{4,6},{5,7},{6,4},{7,5},{8,10},{9,11},{10,... | collective-permute-start | bytes 1179656 | tf_op jit(solution)/shard_map/ppermute | solution.py:354
  453.2 43.5 %collective-permute-start.17 = (bf16[16,96,1024]{2,1,0:T(8,128)(2,1)}, bf16[16,96,1024]{2,1,0:T(8,128)(2,1)}, u32[]{:S(2)}, u32[]{:S(2)}) collective-permute-start(bf16[16,96,1024]{2,1,0:T(8,128)(2,1)} %get-tuple-element.85), channel_id=1, source_target_pairs={{0,1},{1,0},{2,3},{3,2},{4,5},{5,4},{6,7},{7,6},{8,9},{9,8},{10,11... | collective-permute-start | bytes 9437192 | tf_op jit(solution)/shard_map/ppermute | solution.py:354
  454.0 38.8 %collective-permute-start.21 = (bf16[192,1024]{1,0:T(8,128)(2,1)}, bf16[192,1024]{1,0:T(8,128)(2,1)}, u32[]{:S(2)}, u32[]{:S(2)}) collective-permute-start(bf16[192,1024]{1,0:T(8,128)(2,1)} %get-tuple-element.148), channel_id=1, source_target_pairs={{0,4},{1,5},{2,6},{3,7},{4,0},{5,1},{6,2},{7,3},{8,12},{9,13},{10,... | collective-permute-start | bytes 1179656 | tf_op jit(solution)/shard_map/ppermute | solution.py:354
  465.9 30.8 %collective-permute-start.18 = (bf16[384,1024]{1,0:T(8,128)(2,1)}, bf16[384,1024]{1,0:T(8,128)(2,1)}, u32[]{:S(2)}, u32[]{:S(2)}) collective-permute-start(bf16[384,1024]{1,0:T(8,128)(2,1)} %get-tuple-element.139), channel_id=1, source_target_pairs={{0,1},{1,0},{2,3},{3,2},{4,5},{5,4},{6,7},{7,6},{8,9},{9,8},{10,11... | collective-permute-start | bytes 2359304 | tf_op jit(solution)/shard_map/ppermute | solution.py:354
  466.0 30.6 %collective-permute-start.19 = (bf16[384,1024]{1,0:T(8,128)(2,1)}, bf16[384,1024]{1,0:T(8,128)(2,1)}, u32[]{:S(2)}, u32[]{:S(2)}) collective-permute-start(bf16[384,1024]{1,0:T(8,128)(2,1)} %get-tuple-element.138), channel_id=1, source_target_pairs={{0,1},{1,0},{2,3},{3,2},{4,5},{5,4},{6,7},{7,6},{8,9},{9,8},{10,11... | collective-permute-start | bytes 2359304 | tf_op jit(solution)/shard_map/ppermute | solution.py:354
  496.6 16.5 %collective-permute-start.22 = (bf16[128,768]{1,0:T(8,128)(2,1)S(1)}, bf16[128,768]{1,0:T(8,128)(2,1)S(1)}, u32[]{:S(2)}, u32[]{:S(2)}) collective-permute-start(bf16[128,768]{1,0:T(8,128)(2,1)S(1)} %get-tuple-element.152), channel_id=1, source_target_pairs={{0,4},{1,5},{2,6},{3,7},{4,0},{5,1},{6,2},{7,3},{8,12},{9,13},{10,... | collective-permute-start | bytes 589832 | tf_op jit(solution)/shard_map/ppermute | solution.py:354
  498.1 42.4 %collective-permute-start.20 = (bf16[384,1024]{1,0:T(8,128)(2,1)S(1)}, bf16[384,1024]{1,0:T(8,128)(2,1)}, u32[]{:S(2)}, u32[]{:S(2)}) collective-permute-start(bf16[384,1024]{1,0:T(8,128)(2,1)S(1)} %add_convert_fusion.6), channel_id=1, source_target_pairs={{0,2},{1,3},{2,0},{3,1},{4,6},{5,7},{6,4},{7,5},{8,10},{9,11},{10,... | collective-permute-start | bytes 2359304 | tf_op jit(solution)/shard_map/ppermute | solution.py:354
  540.6 42.5 %all-to-all-start.1 = ((bf16[4,4,96,1024]{3,2,1,0:T(8,128)(2,1)}), bf16[4,4,96,1024]{3,2,1,0:T(8,128)(2,1)S(1)}, u32[]{:S(2)}, u32[]{:S(2)}) async-start(bf16[4,4,96,1024]{3,2,1,0:T(8,128)(2,1)} %bitcast.156), calls=%async_computation.1 | async-start | bytes 6291456 | tf_op jit(solution)/shard_map/all_to_all | solution.py:377
  583.1 41.2 %all-to-all-start.4 = ((bf16[4,192,1024]{2,1,0:T(8,128)(2,1)}), bf16[4,192,1024]{2,1,0:T(8,128)(2,1)}, u32[]{:S(2)}, u32[]{:S(2)}) async-start(bf16[4,192,1024]{2,1,0:T(8,128)(2,1)} %reduce_sum.224), calls=%async_computation.4 | async-start | bytes 3145728 | tf_op jit(solution)/shard_map/all_to_all | solution.py:379
  624.3 11.5 %all-to-all-start.2 = ((bf16[32,2,1024]{2,1,0:T(2,128)(2,1)}), bf16[32,2,1024]{2,1,0:T(2,128)(2,1)}, u32[]{:S(2)}, u32[]{:S(2)}) async-start(bf16[32,2,1024]{2,1,0:T(2,128)(2,1)} %reshape.430), calls=%async_computation.2 | async-start | bytes 262144 | tf_op jit(solution)/shard_map/all_to_all | solution.py:683
  629.5 30.2 %collective-permute-start.23 = (bf16[192,1024]{1,0:T(8,128)(2,1)}, bf16[192,1024]{1,0:T(8,128)(2,1)}, u32[]{:S(2)}, u32[]{:S(2)}) collective-permute-start(bf16[192,1024]{1,0:T(8,128)(2,1)} %get-tuple-element.146), channel_id=1, source_target_pairs={{0,4},{1,5},{2,6},{3,7},{4,0},{5,1},{6,2},{7,3},{8,12},{9,13},{10,... | collective-permute-start | bytes 1179656 | tf_op jit(solution)/shard_map/ppermute | solution.py:354
  635.8 34.2 %all-to-all-start.3 = ((bf16[4,96,1024]{2,1,0:T(8,128)(2,1)}), bf16[4,96,1024]{2,1,0:T(8,128)(2,1)S(1)}, u32[]{:S(2)}, u32[]{:S(2)}) async-start(bf16[4,96,1024]{2,1,0:T(8,128)(2,1)} %reduce_sum.222), calls=%async_computation.3 | async-start | bytes 1572864 | tf_op jit(solution)/shard_map/all_to_all | solution.py:379
  (72 other events, 973.3 us)
Sparse Core Ops, SparseCore 0:
  11.6 164.9 all-gather.4
  180.2 115.0 all-gather.6
  325.6 226.5 reduce-scatter.1

commit v3 on v2

--- a/solution.py
+++ b/solution.py
@@ -84,11 +84,7 @@
         ],
         compiler_params=params(),
         name="attend",
-        cost_estimate=pl.CostEstimate(
-            flops=16 * rows * total * width,
-            bytes_accessed=4 * width * (rows + total),
-            transcendentals=2 * pairs * rows * total,
-        ),
+        cost_estimate=pl.CostEstimate(flops=1, bytes_accessed=1, transcendentals=0),
     )(query, *kvs, *([bias] if masked else []))
 
 
@@ -145,40 +141,40 @@
         + [jax.ShapeDtypeStruct((slots, 2 * width), bf16)] * count,
         compiler_params=params(),
         name="attend_back",
-        cost_estimate=pl.CostEstimate(
-            flops=40 * rows * total * width,
-            bytes_accessed=8 * width * (rows + total),
-            transcendentals=2 * pairs * rows * total,
-        ),
+        cost_estimate=pl.CostEstimate(flops=1, bytes_accessed=1, transcendentals=0),
     )(query, *kvs, out, grad, lse, *([bias] if masked else []))
     return result[0], result[1:]
 
 
-def block_kernel(third_ref, cot_ref, gain_ref, shift_ref, dbias_ref, ubias_ref, up_ref, down_ref,
-                 result_ref, tgrad_ref, grads_ref, vec_ref, ubgrad_ref,
+def block_kernel(core_ref, third_ref, cot_ref, gain_ref, shift_ref, dbias_ref, ubias_ref, up_ref, down_ref,
+                 result_ref, tgrad_ref, keep_ref, send_ref, vec_ref, ubgrad_ref,
                  unit_s, final_s, final_t, out_s, fgrad_s, scale_s, wide_s, tall_s, sems):
     step = pl.program_id(0)
     last = pl.num_programs(0) - 1
     slot = lax.rem(step, 2)
-    _, parts, shard, tile = wide_s.shape
-    _, spread, tall, width = tall_s.shape
+    core = core_ref[0]
+    _, _, half, shard, tile = wide_s.shape
+    _, _, few, tall, width = tall_s.shape
     per = width // tile
 
     def copies(at, place):
         row = pl.multiple_of((at // per) * shard, shard)
         lane = pl.multiple_of(lax.rem(at, per) * tile, tile)
-        return (
-            pltpu.make_async_copy(
-                wide_s.at[place],
-                grads_ref.at[:, pl.ds(row, shard), pl.ds(lane, tile)],
-                sems.at[0, place],
-            ),
-            pltpu.make_async_copy(
-                tall_s.at[place],
-                grads_ref.at[pl.ds(at * spread, spread), pl.ds(tall, tall), :],
-                sems.at[1, place],
-            ),
-        )
+        found = []
+        for which, ref in enumerate((keep_ref, send_ref)):
+            found += [
+                pltpu.make_async_copy(
+                    wide_s.at[place, which],
+                    ref.at[:, pl.ds(row, shard), pl.ds(lane, tile)],
+                    sems.at[which, place],
+                ),
+                pltpu.make_async_copy(
+                    tall_s.at[place, which],
+                    ref.at[pl.ds(at * few, few), pl.ds(tall, tall), :],
+                    sems.at[2 + which, place],
+                ),
+            ]
+        return found
 
     @pl.when(step == 0)
     def _():
@@ -207,8 +203,12 @@
     out_s[...] += dot(active, down)
     fgrad_s[...] += dot(ugrad, up, NT)
     ubgrad_ref[...] = jnp.sum(ugrad.astype(f32), 0, keepdims=True)
-    wide_s[slot] = dot(final_t[...], ugrad).astype(bf16).reshape(wide_s.shape[1:])
-    tall_s[slot] = dot(jnp.transpose(active), cot).astype(bf16).reshape(tall_s.shape[1:])
+    wide = dot(final_t[...], ugrad).astype(bf16).reshape(half, 2, shard, tile)
+    wide_s[slot, core] = wide[:, 0]
+    wide_s[slot, 1 - core] = wide[:, 1]
+    slim = dot(jnp.transpose(active), cot).astype(bf16).reshape(few, 2, tall, width)
+    tall_s[slot, core] = slim[:, 0]
+    tall_s[slot, 1 - core] = slim[:, 1]
     for copy in copies(step, slot):
         copy.start()
 
@@ -225,7 +225,7 @@
             copy.wait()
 
 
-def feed_forward(third, cot, gain, shift, down_bias, up_bias, packed, shard):
+def feed_forward(core, third, cot, gain, shift, down_bias, up_bias, packed, shard):
     rows, width = third.shape
     parts = packed.shape[0]
     hidden = up_bias.shape[1]
@@ -234,53 +234,54 @@
     tall = hidden // parts
     spread = tile // tall
     steps = hidden // tile
-    whole = lambda shape: pl.BlockSpec(shape, lambda j: (0,) * len(shape))
+    whole = lambda shape: pl.BlockSpec(shape, lambda j, c: (0,) * len(shape))
     return pl.pallas_call(
         block_kernel,
-        grid=(steps,),
-        in_specs=[
-            whole((rows, width)),
-            whole((rows, width)),
-            whole((1, width)),
-            whole((1, width)),
-            whole((1, width)),
-            pl.BlockSpec((1, tile), lambda j: (0, j)),
-            pl.BlockSpec((parts, shard, tile), lambda j: (0, j // per, j % per)),
-            pl.BlockSpec((spread, tall, width), lambda j: (j, 1, 0)),
-        ],
-        out_specs=[
-            whole((rows, width)),
-            whole((rows, width)),
-            pl.BlockSpec(memory_space=pl.ANY),
-            whole((8, width)),
-            pl.BlockSpec((1, tile), lambda j: (0, j)),
-        ],
-        scratch_shapes=[
-            pltpu.VMEM((rows, width), f32),
-            pltpu.VMEM((rows, width), bf16),
-            pltpu.VMEM((width, rows), bf16),
-            pltpu.VMEM((rows, width), f32),
-            pltpu.VMEM((rows, width), f32),
-            pltpu.VMEM((rows, 1), f32),
-            pltpu.VMEM((2, parts, shard, tile), bf16),
-            pltpu.VMEM((2, spread, tall, width), bf16),
-            pltpu.SemaphoreType.DMA((2, 2)),
-        ],
+        grid_spec=pltpu.PrefetchScalarGridSpec(
+            num_scalar_prefetch=1,
+            grid=(steps,),
+            in_specs=[
+                whole((rows, width)),
+                whole((rows, width)),
+                whole((1, width)),
+                whole((1, width)),
+                whole((1, width)),
+                pl.BlockSpec((1, tile), lambda j, c: (0, j)),
+                pl.BlockSpec((parts, shard, tile), lambda j, c: (0, j // per, j % per)),
+                pl.BlockSpec((spread, tall, width), lambda j, c: (j, 1, 0)),
+            ],
+            out_specs=[
+                whole((rows, width)),
+                whole((rows, width)),
+                pl.BlockSpec(memory_space=pl.ANY),
+                pl.BlockSpec(memory_space=pl.ANY),
+                whole((8, width)),
+                pl.BlockSpec((1, tile), lambda j, c: (0, j)),
+            ],
+            scratch_shapes=[
+                pltpu.VMEM((rows, width), f32),
+                pltpu.VMEM((rows, width), bf16),
+                pltpu.VMEM((width, rows), bf16),
+                pltpu.VMEM((rows, width), f32),
+                pltpu.VMEM((rows, width), f32),
+                pltpu.VMEM((rows, 1), f32),
+                pltpu.VMEM((2, 2, parts // 2, shard, tile), bf16),
+                pltpu.VMEM((2, 2, spread // 2, tall, width), bf16),
+                pltpu.SemaphoreType.DMA((4, 2)),
+            ],
+        ),
         out_shape=[
             jax.ShapeDtypeStruct((rows, width), bf16),
             jax.ShapeDtypeStruct((rows, width), f32),
-            jax.ShapeDtypeStruct((parts, 2 * tall, width), bf16),
+            jax.ShapeDtypeStruct((parts // 2, 2 * tall, width), bf16),
+            jax.ShapeDtypeStruct((parts // 2, 2 * tall, width), bf16),
             jax.ShapeDtypeStruct((8, width), f32),
             jax.ShapeDtypeStruct((1, hidden), f32),
         ],
         compiler_params=params(),
         name="feed_forward",
-        cost_estimate=pl.CostEstimate(
-            flops=12 * rows * width * hidden,
-            bytes_accessed=8 * width * hidden + 12 * rows * width,
-            transcendentals=2 * rows * hidden,
-        ),
-    )(third, cot, gain, shift, down_bias, up_bias, packed, packed)
+        cost_estimate=pl.CostEstimate(flops=1, bytes_accessed=1, transcendentals=0),
+    )(core, third, cot, gain, shift, down_bias, up_bias, packed, packed)
 
 
 def grads_kernel(jobs, core_ref, *refs):
@@ -333,11 +334,7 @@
         out_shape=[jax.ShapeDtypeStruct((parts // 2, count * shard, width), bf16)] * 2,
         compiler_params=params(),
         name="weight_grads",
-        cost_estimate=pl.CostEstimate(
-            flops=flops,
-            bytes_accessed=2 * parts * count * shard * width + sum(2 * a.size for a in arrays),
-            transcendentals=0,
-        ),
+        cost_estimate=pl.CostEstimate(flops=1, bytes_accessed=1, transcendentals=0),
     )(core, *arrays)
 
 
@@ -374,10 +371,16 @@
         moved = yield self.swap(send, 1)
         total = add([keep, moved]).reshape(self.obj, self.seq // 2, *keep.shape[1:])
         total = yield total
-        moved = yield lax.all_to_all(total, "obj", 0, 0, tiled=True)
-        total = jnp.sum(moved.astype(f32), 0).astype(bf16)
-        moved = yield lax.all_to_all(total, "ring", 0, 0, tiled=True)
-        yield jnp.sum(moved.astype(f32), 0)
+        total = yield lax.psum_scatter(total, "obj", scatter_dimension=0, tiled=False)
+        terms = [total]
+        for mask in self.group[1:] + [self.far]:
+            terms = [t.reshape(t.shape[0] // 2, 2, *t.shape[1:]) for t in terms]
+            pick = lambda t, which: lax.dynamic_index_in_dim(t, which, 1, keepdims=False)
+            moved = self.swap(add([pick(t, 1 - self.bit(mask)) for t in terms]), mask)
+            if 4 * mask >= self.seq:
+                moved = yield moved
+            terms = [pick(t, self.bit(mask)) for t in terms] + [moved]
+        yield sum(t[0].astype(f32) for t in terms)
 
     def exchange_core(self, terms):
         return [self.swap(t, 1) for t in terms[1::2]]
@@ -462,9 +465,8 @@
         other = lax.dynamic_index_in_dim(value, 1 - half, 0, keepdims=False)
         return jnp.concatenate([mine, grid.swap(other, grid.far)], 0)
 
-    def spread(value):
-        rows = value.shape[0] // 2
-        mine, other = value[:rows], grid.swap(value[rows:], grid.far)
+    def spread(mine, other):
+        mine = mine[: other.shape[0]]
         return jnp.where(half == 0, jnp.stack([mine, other]), jnp.stack([other, mine]))
 
     shard = self_output.shape[0]
@@ -511,11 +513,10 @@
     tokens_all = jnp.concatenate(grid.gather_group(compact(tokens)), 0)
     feats_all = jnp.concatenate(grid.gather_group(compact(patches)), 0)
     views_all = jnp.concatenate(grid.gather_group(compact(patch_index)), 0) // VIEW_PATCHES
-    cot = compact(cotangent)
     first = lax.all_gather(first, BOTH, axis=0, tiled=False)
     ffn_mine = jnp.concatenate([stack_columns(low(up_weight), width), low(down_weight)], 0)
-    first, ffn_mine, tokens_all, feats_all, views_all, cot = together(
-        (first, ffn_mine, tokens_all, feats_all, views_all, cot)
+    first, ffn_mine, tokens_all, feats_all, views_all = together(
+        (first, ffn_mine, tokens_all, feats_all, views_all)
     )
     packed = lax.all_gather(ffn_mine, BOTH, axis=0, tiled=False)
 
@@ -574,6 +575,8 @@
     )
     bias = jnp.where(slots < live, 0.0, -1e30).astype(f32).reshape(1, -1)
 
+    query, kvs, mems, cotangent = together((query, kvs, mems, cotangent))
+    cot = compact(cotangent)
     attended, lse1 = attend(query, kvs, None)
     second = x + dot(attended, full_out)
     unit2, rstd2 = norm_parts(second)
@@ -581,18 +584,27 @@
     asked = low(low(dot(normed, full_cq)).astype(f32) * factor)
     crossed, lse2 = attend(asked, mems, bias)
     third = second + dot(crossed, full_co)
+    third, cot = together((third, cot))
     core_now = core.reshape(1).astype(jnp.int32)
-    result, third_grad, ffn_grads, last_vectors, up_bias_grad = feed_forward(
-        third, cot, g_last, b_last, b_down, b_up, packed, shard
-    )
-    ffn_grad = lax.psum_scatter(ffn_grads, BOTH, scatter_dimension=0, tiled=True)[0].astype(f32)
+    result, third_grad, ffn_keep, ffn_send, last_vectors, up_bias_grad = feed_forward(
+        core_now, third, cot, g_last, b_last, b_down, b_up, packed, shard
+    )
     tall = down_weight.shape[0]
 
     def chunks(terms):
         return jnp.split(terms, grid.seq // 2, 0)
 
+    ffn = grid.scatter(ffn_keep, ffn_send)
+    ffn_moved = next(ffn)
+    half_rows = result.shape[0] // 2
     third_low = low(third_grad)
     crossed_grad = low(dot(third_low, full_co, NT))
+    ffn_moved, crossed_grad = together((ffn_moved, crossed_grad))
+    ffn_moved = ffn.send(ffn_moved)
+    ffn_moved, crossed_grad = together((ffn_moved, crossed_grad))
+
+    ffn_moved = ffn.send(ffn_moved)
+    result_moved = grid.swap(result[half_rows:], grid.far)
     asked_grad, mem_terms = attend_back(asked, mems, crossed, crossed_grad, lse2, bias)
     mem_terms = mem_terms[0]
     normed_grad = dot(asked_grad, full_cq, NT)
@@ -617,17 +629,23 @@
     rest = grid.scatter(keep, send)
     moved = next(rest)
     patch_terms = chunks(low(dot(embedded_grad, full_patch, NT)))
+    attended_grad, patch_terms, moved = together((attended_grad, patch_terms, moved))
+    moved = rest.send(moved)
     patch_moved = grid.exchange_core(patch_terms)
-    moved, patch_moved = together((moved, patch_moved))
-    moved = rest.send(moved)
-    moved, attended_grad = together((moved, attended_grad))
+    attended_grad, patch_moved, moved = together((attended_grad, patch_moved, moved))
 
     moved = rest.send(moved)
     patch_mine, patch_moved = grid.exchange_line(patch_terms, patch_moved)
     query_grad, pair_terms = attend_back(query, kvs, attended, attended_grad, lse1, None)
     pair_terms = pair_terms[0]
-    patch_moved, query_grad, pair_terms = together((patch_moved, query_grad, pair_terms))
-
+    ffn_moved, result_moved, patch_moved, query_grad, pair_terms = together(
+        (ffn_moved, result_moved, patch_moved, query_grad, pair_terms)
+    )
+
+    ffn_moved = ffn.send(ffn_moved)
+    hidden_terms = chunks(low(dot(pair_terms, full_kv, NT)))
+    hidden_terms, pair_terms, query_grad = together((hidden_terms, pair_terms, query_grad))
+    hidden_moved = grid.exchange_core(hidden_terms)
     keep, send = weight_grads(
         core_now,
         [hidden, query_grad, hidden_all, pair_terms],
@@ -636,26 +654,29 @@
         shard,
         width,
     )
+    keep, send, hidden_moved, ffn_moved = together((keep, send, hidden_moved, ffn_moved))
+
     own_scatter = grid.scatter(keep, send)
     own_moved = next(own_scatter)
-    hidden_terms = chunks(low(dot(pair_terms, full_kv, NT)))
-    hidden_moved = grid.exchange_core(hidden_terms)
-    own_moved, hidden_moved = together((own_moved, hidden_moved))
-    own_moved = own_scatter.send(own_moved)
     hidden_mine, hidden_moved = grid.exchange_line(hidden_terms, hidden_moved)
-    hidden_query = dot(query_grad, full_q, NT)
-    patch_grad = spread(low(patch_mine.astype(f32) + patch_moved.astype(f32)))
-    result = spread(result)
-    moved, own_moved, hidden_query, hidden_moved, result, patch_grad = together(
-        (moved, own_moved, hidden_query, hidden_moved, result, patch_grad)
-    )
-    own_moved = own_scatter.send(own_moved)
+    patch_low = low(patch_mine.astype(f32) + patch_moved.astype(f32))
+    patch_half = patch_low.shape[0] // 2
     view_grad = jnp.stack(
         [jnp.sum(hot_all[:, v : v + 1] * embedded_grad.astype(f32), 0) for v in range(VIEWS)]
     )
+    own_moved, patch_low, view_grad = together((own_moved, patch_low, view_grad))
+    own_moved = own_scatter.send(own_moved)
+    own_moved, hidden_moved, moved = together((own_moved, hidden_moved, moved))
+
+    own_moved = own_scatter.send(own_moved)
+    ffn_moved = ffn.send(ffn_moved)
+    moved = rest.send(moved)
+    hidden_query = dot(query_grad, full_q, NT)
     hidden_grad = hidden_query + hidden_mine.astype(f32) + hidden_moved.astype(f32)
     token_grad = low(second_grad + norm_back(unit1, rstd1, hidden_grad * scale1))
-    token_grad = spread(token_grad)
+    token_grad, hidden_grad = together((token_grad, hidden_grad))
+    token_moved = grid.swap(token_grad[half_rows:], grid.far)
+    result = spread(result, result_moved)
     modulation_grad = jnp.concatenate(
         [jnp.sum(hidden_grad * unit1, 0), jnp.sum(hidden_grad, 0)]
     )
@@ -678,10 +699,21 @@
         1,
     )
     small_grad = jnp.pad(small_grad, ((0, 0), (0, small_count * width - small_grad.shape[1])))
-    own_moved, small_grad = together((own_moved, small_grad))
+    moved, small_grad, token_moved, ffn_moved, result = together(
+        (moved, small_grad, token_moved, ffn_moved, result)
+    )
     moved = rest.send(moved)
     small_grad = lax.all_to_all(small_grad.reshape(parts, small_count, width), BOTH, 0, 0, tiled=True)
+    patch_moved = grid.swap(patch_low[patch_half:], grid.far)
     tiny = jnp.sum(small_grad.astype(f32), 0).reshape(-1)
+    token_grad = spread(token_grad, token_moved)
+    ffn_grad = ffn.send(ffn_moved)
+    ffn_up, ffn_down = unstack_columns(ffn_grad[:tall], shard), ffn_grad[tall:]
+    own_moved, moved, token_grad, patch_moved, tiny, ffn_up, ffn_down = together(
+        (own_moved, moved, token_grad, patch_moved, tiny, ffn_up, ffn_down)
+    )
+    own_moved = own_scatter.send(own_moved)
+    patch_grad = spread(patch_low, patch_moved)
     own_moved = own_scatter.send(own_moved)
     rest_sum = rest.send(moved)
     self_sum = own_scatter.send(own_moved)
@@ -707,9 +739,9 @@
         rest_sum[:shard],
         pieces[4],
         pieces[5],
-        unstack_columns(ffn_grad[:tall], shard),
+        ffn_up,
         pieces[7],
-        ffn_grad[tall:],
+        ffn_down,
         pieces[6],
     )
 

time: 688 us -> 632 us (0.919)
  waiting for transfers between devices: 297 us -> 246 us
  starting transfers between devices: 40.4 us -> 33 us
    all_to_all x4 -> x0, waiting for transfers between devices: 52.4 us -> none  [the longest x2 30.9 us: scatter(): moved = (yield lax.all_to_all(total, 'obj', 0, 0, tiled=True))]
    ppermute x24 -> x31, waiting for transfers between devices: 178 us -> 155 us  [swap(): return lax.ppermute(value, BOTH, [(i, i ^ mask) for i in range(self.all)])]
    all_to_all x4 -> x0, starting transfers between devices: 18.2 us -> none  [the longest x2 10.1 us: scatter(): moved = (yield lax.all_to_all(total, 'obj', 0, 0, tiled=True))]
    all_gather x1, waiting for transfers between devices: 45 us -> 61.5 us  [on_device(): first = lax.all_gather(first, BOTH, axis=0, tiled=False)]
    convert_element_type x4 -> x8, other arithmetic: 14.7 us -> 25.2 us  [add(): return sum((t.astype(f32) for t in terms)).astype(bf16)]
    ppermute x24 -> x31, starting transfers between devices: 18.8 us -> 28.8 us  [swap(): return lax.ppermute(value, BOTH, [(i, i ^ mask) for i in range(self.all)])]
    reduce_sum x4 -> x1, other arithmetic: 9.77 us -> 2.39 us  [norm_back(): jnp.mean(grad, -1, keepdims=True)]
    unnamed x169 -> x187, local copies, waits for them, and re-layouts: 16.5 us -> 13.7 us
  transfers between devices with their start and end apart: 32 -> 37, of which waited for: 13 -> 15; matrix products, arithmetic and copies ran while one was open for 24% -> 25% of each run, Pallas kernels for 17% -> 19%
where the time goes in v3:
time: 632 us; the launch traced here: 627 us
  waiting for transfers between devices  246 us (39%)
  Pallas kernels  151 us (24%)
  other arithmetic  65.3 us (10%)
  matrix products  59.8 us (9%)
  local copies, waits for them, and re-layouts  56.6 us (9%)
  starting transfers between devices  33 us (5%)
  between operations  15.7 us (2%)
    ppermute x31, waiting for transfers between devices, swap(): return lax.ppermute(value, BOTH, [(i, i ^ mask) for i in range(self.all)])  155 us
    all_gather x1, waiting for transfers between devices, on_device(): first = lax.all_gather(first, BOTH, axis=0, tiled=False)  61.5 us
    dot_general x14, matrix products, dot(): return lax.dot_general(left, right, dims, preferred_element_type=f32)  59.8 us
    pallas_call x2, Pallas kernels, attend_back(): pl.pallas_call(partial(attend_back_kernel, count, masked), grid=(pairs,),...  49.1 us
    pallas_call x2, Pallas kernels, attend(): pl.pallas_call(partial(attend_kernel, count, masked), grid=(pairs,), in_s...  36 us
    pallas_call x2, Pallas kernels, weight_grads(): pl.pallas_call(partial(grads_kernel, jobs), grid_spec=pltpu.PrefetchScala...  34.7 us
    pallas_call x1, Pallas kernels, feed_forward(): pl.pallas_call(block_kernel, grid_spec=pltpu.PrefetchScalarGridSpec(num_s...  30.9 us
    ppermute x31, starting transfers between devices, swap(): return lax.ppermute(value, BOTH, [(i, i ^ mask) for i in range(self.all)])  28.8 us
  transfers between devices with their start and end apart: 37, of which 15 were waited for; matrix products, arithmetic and copies ran while one was open for 25% of the time, Pallas kernels for 19%

profile of v3, /device:TPU:0, one launch (start us, length us, event | category | flops | bytes accessed | tf_op | source)
XLA Modules:
  0.0 626.7 jit_solution(2925604781681211319)
XLA Ops:
  11.5 4.0 collective-permute-start.8
  24.6 32.7 %collective-permute-done = bf16[192,1024]{1,0:T(8,128)(2,1)S(1)} collective-permute-done((bf16[192,1024]{1,0:T(8,128)(2,1)}, bf16[192,1024]{1,0:T(8,128)(2,1)S(1)}, u32[]{:S(2)}, u32[]{:S(2)}) %collective-permute-start) | collective-permute-done | bytes 393248 | tf_op jit(solution)/shard_map/ppermute | solution.py:351
  61.3 47.7 %collective-permute-done.6 = bf16[256,768]{1,0:T(8,128)(2,1)S(1)} collective-permute-done((bf16[256,768]{1,0:T(8,128)(2,1)S(1)}, bf16[256,768]{1,0:T(8,128)(2,1)S(1)}, u32[]{:S(2)}, u32[]{:S(2)}) %collective-permute-start.6) | collective-permute-done | bytes 393248 | tf_op jit(solution)/shard_map/ppermute | solution.py:351
  112.0 61.5 %all-gather.5.cloned.1.call-done = bf16[9216,1024]{1,0:T(8,128)(2,1)} async-done(((bf16[288,1024]{1,0:T(8,128)(2,1)}), bf16[9216,1024]{1,0:T(8,128)(2,1)}) %all-gather.5.cloned.1.call-update) | async-done | bytes 18874384 | tf_op jit(solution)/shard_map/all_gather | solution.py:516
  185.0 9.6 %fusion.26 = (bf16[32,32,1024]{2,1,0:T(8,128)(2,1)}, bf16[32,32,1024]{2,1,0:T(8,128)(2,1)}, bf16[32,32,1024]{2,1,0:T(8,128)(2,1)}, bf16[32,32,1024]{2,1,0:T(8,12...) fusion(bf16[32,288,1024]{2,1,0:T(8,128)(2,1)} %bitcast.210), kind=kLoop, calls=%fused_computation.177 | loop fusion | bytes 33554432 | tf_op jit(solution)/shard_map/slice | solution.py:524
  194.7 3.8 subtract_multiply_fusion
  205.1 6.3 convolution_convert_fusion.2.refs_1_
  211.4 8.9 %convolution_convert_fusion.refs_1_ = bf16[1536,2048]{1,0:T(8,128)(2,1)} fusion(bf16[1536,1024]{1,0:T(8,128)(2,1)S(1)} %get-tuple-element.211.refs_2_, bf16[1024,1024]{1,0:T(8,128)(2,1)S(1)} %bitcast.216, bf16[1024,1024]{1,0:T(8,128)(2,1)S(1)} %bitcast.218), kind=kOutput, calls=%fused_computation.2 | convolution fusion | flops 6453985280 | bytes 13631488 | tf_op jit(solution)/shard_map/dot_general | solution.py:26
  222.7 21.1 %attend.2 = (bf16[384,1024]{1,0:T(8,128)(2,1)}, f32[8,384,128]{2,1,0:T(8,128)}) custom-call(bf16[384,1024]{1,0:T(8,128)(2,1)} %multiply_convert_fusion.1.refs_0_, bf16[1536,2048]{1,0:T(8,128)(2,1)} %convolution_convert_fusion.refs_1_), custom_call_target="tpu_custom_call" | custom-call | flops 1 | bytes 1 | tf_op jit(solution)/shard_map/attend/pallas_call | solution.py:76
  248.2 4.7 fusion.34
  256.4 15.0 %attend.3 = (bf16[384,1024]{1,0:T(8,128)(2,1)}, f32[8,384,128]{2,1,0:T(8,128)}) custom-call(bf16[384,1024]{1,0:T(8,128)(2,1)} %multiply_convert_fusion.refs_0_, bf16[1024,2048]{1,0:T(8,128)(2,1)} %convolution_convert_fusion.2.refs_1_, f32[1,1024]{1,0:T(1,128)} %compare_select_fusion.refs_2_.refs_5_), custom_call_target="tpu_custom_call" | custom-call | flops 1 | bytes 1 | tf_op jit(solution)/shard_map/attend/pallas_call | solution.py:76
  273.4 4.0 convolution_add_fusion.third_ref
  279.4 22.9 %all-gather.7.cloned.1.call-done = bf16[8192,1024]{1,0:T(8,128)(2,1)} async-done(((bf16[256,1024]{1,0:T(8,128)(2,1)}), bf16[8192,1024]{1,0:T(8,128)(2,1)}) %all-gather.7.cloned.1.call-update) | async-done | bytes 16777232 | tf_op jit(solution)/shard_map/all_gather | solution.py:521
  302.3 30.9 %feed_forward.1 = (bf16[384,1024]{1,0:T(8,128)(2,1)}, f32[384,1024]{1,0:T(8,128)}, bf16[16,256,1024]{2,1,0:T(8,128)(2,1)}, bf16[16,256,1024]{2,1,0:T(8,128)(2,1)}, f32[8,1024]{1,0:T(8,128)}, /*index=5*/f32[1,4096]{1,0:T(1,128)}) custom-call(s32[1]{0:T(128)} %bitcast.core_ref, f32[384,1024]{1,0:T(8,128)} %convolution_add_fusion.third_ref, ...), custom_call_target="tpu_custom_call" | custom-call | flops 1 | bytes 1 | tf_op jit(solution)/shard_map/feed_forward/pallas_call | solution.py:238
  337.1 9.4 %collective-permute-done.13 = bf16[16,256,1024]{2,1,0:T(8,128)(2,1)S(1)} collective-permute-done((bf16[16,256,1024]{2,1,0:T(8,128)(2,1)}, bf16[16,256,1024]{2,1,0:T(8,128)(2,1)S(1)}, u32[]{:S(2)}, u32[]{:S(2)}) %collective-permute-start.13) | collective-permute-done | bytes 8388640 | tf_op jit(solution)/shard_map/ppermute | solution.py:351
  346.6 9.1 %add_convert_fusion = bf16[16,256,1024]{2,1,0:T(8,128)(2,1)} fusion(bf16[16,256,1024]{2,1,0:T(8,128)(2,1)S(1)} %collective-permute-done.13, bf16[16,256,1024]{2,1,0:T(8,128)(2,1)} %get-tuple-element.111), kind=kLoop, calls=%fused_computation | loop fusion | flops 16777216 | bytes 25165824 | tf_op jit(solution)/shard_map/convert_element_type | solution.py:403
  355.8 21.0 %attend_back.2 = (bf16[384,1024]{1,0:T(8,128)(2,1)}, bf16[1024,2048]{1,0:T(8,128)(2,1)}) custom-call(bf16[384,1024]{1,0:T(8,128)(2,1)} %multiply_convert_fusion.refs_0_, bf16[1024,2048]{1,0:T(8,128)(2,1)} %convolution_convert_fusion.2.refs_1_, bf16[384,1024]{1,0:T(8,128)(2,1)} %get-tuple-element.106.refs_2_.refs_0_, ...), custom_call_target="tpu_custom_call" | custom-call | flops 1 | bytes 1 | tf_op jit(solution)/shard_map/attend_back/pallas_call | solution.py:132
  384.0 6.5 %fusion = (f32[1024]{0:T(1024)S(1)}, f32[1024]{0:T(1024)S(1)}, f32[1024]{0:T(1024)S(1)}, f32[1024]{0:T(1024)S(1)}, bf16[1024,1024]{1,0:T(8,128)(2,1)}) fusion(f32[1024]{0:T(1024)S(1)} %bitcast.280, f32[1024]{0:T(1024)S(1)} %bitcast.286, f32[1024]{0:T(1024)S(1)} %bitcast.284, f32[1024]{0:T(1024)S(1)} %bitcast.282, bf16[1024,2048]{1,0:T(8,128)(2,1)S(1)} %copy-done.5, ...), kind=kOutput, calls=%fused_computation.12 | convolution fusion | flops 4313837568 | bytes 10518528 | tf_op jit(solution)/shard_map/dot_general | solution.py:26
  390.5 19.6 %weight_grads.2 = (bf16[16,192,1024]{2,1,0:T(8,128)(2,1)}, bf16[16,192,1024]{2,1,0:T(8,128)(2,1)}) custom-call(s32[1]{0:T(128)} %bitcast.core_ref, bf16[384,1024]{1,0:T(8,128)(2,1)} %get-tuple-element.106.refs_2_.refs_0_, bf16[384,1024]{1,0:T(8,128)(2,1)} %copy-done.7, bf16[384,1024]{1,0:T(8,128)(2,1)} %copy-done.6, ...), custom_call_target="tpu_custom_call" | custom-call | flops 1 | bytes 1 | tf_op jit(solution)/shard_map/weight_grads/pallas_call | solution.py:326
  410.7 3.7 convolution_convert_fusion.3
  421.3 7.5 %add_convert_fusion.1 = bf16[16,192,1024]{2,1,0:T(8,128)(2,1)} fusion(bf16[16,192,1024]{2,1,0:T(8,128)(2,1)} %collective-permute-done.15, bf16[16,192,1024]{2,1,0:T(8,128)(2,1)S(1)} %bitcast.213), kind=kLoop, calls=%fused_computation.1 | loop fusion | flops 12582912 | bytes 18874368 | tf_op jit(solution)/shard_map/convert_element_type | solution.py:403
  434.9 28.1 %attend_back.3 = (bf16[384,1024]{1,0:T(8,128)(2,1)}, bf16[1536,2048]{1,0:T(8,128)(2,1)}) custom-call(bf16[384,1024]{1,0:T(8,128)(2,1)} %multiply_convert_fusion.1.refs_0_, bf16[1536,2048]{1,0:T(8,128)(2,1)} %convolution_convert_fusion.refs_1_, bf16[384,1024]{1,0:T(8,128)(2,1)} %get-tuple-element.104.refs_4_.refs_2_, ...), custom_call_target="tpu_custom_call" | custom-call | flops 1 | bytes 1 | tf_op jit(solution)/shard_map/attend_back/pallas_call | solution.py:132
  465.7 9.9 %convolution_convert_fusion.1 = bf16[1536,1024]{1,0:T(8,128)(2,1)S(1)} fusion(bf16[1536,2048]{1,0:T(8,128)(2,1)} %get-tuple-element.137.refs_3_, bf16[1024,1024]{1,0:T(8,128)(2,1)S(1)} %bitcast.217, bf16[1024,1024]{1,0:T(8,128)(2,1)} %bitcast.219), kind=kOutput, calls=%fused_computation.19 | convolution fusion | flops 6452412416 | bytes 13631488 | tf_op jit(solution)/shard_map/dot_general | solution.py:26
  478.6 15.1 %weight_grads.3 = (bf16[16,96,1024]{2,1,0:T(8,128)(2,1)}, bf16[16,96,1024]{2,1,0:T(8,128)(2,1)}) custom-call(s32[1]{0:T(128)} %bitcast.core_ref, bf16[384,1024]{1,0:T(8,128)(2,1)} %slice.267.refs_0_, bf16[384,1024]{1,0:T(8,128)(2,1)} %get-tuple-element.136.refs_1_, bf16[1536,1024]{1,0:T(8,128)(2,1)} %copy-done.2, bf16[1536,2048]{1,0:T(8,128)(2,1)} %get-tuple-element.137.refs_3_), custom_call_target="tpu_custom_call" | custom-call | flops 1 | bytes 1 | tf_op jit(solution)/shard_map/weight_grads/pallas_call | solution.py:326
  503.0 11.3 %collective-permute-done.23 = bf16[384,1024]{1,0:T(8,128)(2,1)} collective-permute-done((bf16[384,1024]{1,0:T(8,128)(2,1)S(1)}, bf16[384,1024]{1,0:T(8,128)(2,1)}, u32[]{:S(2)}, u32[]{:S(2)}) %collective-permute-start.23) | collective-permute-done | bytes 786464 | tf_op jit(solution)/shard_map/ppermute | solution.py:351
  541.0 17.3 %collective-permute-done.26 = bf16[1,256,1024]{2,1,0:T(8,128)(2,1)} collective-permute-done((bf16[1,256,1024]{2,1,0:T(8,128)(2,1)}, bf16[1,256,1024]{2,1,0:T(8,128)(2,1)}, u32[]{:S(2)}, u32[]{:S(2)}) %collective-permute-start.26) | collective-permute-done | bytes 524320 | tf_op jit(solution)/shard_map/ppermute | solution.py:351
  558.3 12.7 %collective-permute-done.25 = bf16[192,1024]{1,0:T(8,128)(2,1)} collective-permute-done((bf16[192,1024]{1,0:T(8,128)(2,1)}, bf16[192,1024]{1,0:T(8,128)(2,1)}, u32[]{:S(2)}, u32[]{:S(2)}) %collective-permute-start.25) | collective-permute-done | bytes 393248 | tf_op jit(solution)/shard_map/ppermute | solution.py:351
  571.0 5.7 collective-permute-done.24
  578.6 4.0 all-to-all-start
  588.0 6.3 %all-to-all-done = bf16[32,2,1024]{2,1,0:T(2,128)(2,1)S(1)} async-done(((bf16[32,2,1024]{2,1,0:T(2,128)(2,1)}), bf16[32,2,1024]{2,1,0:T(2,128)(2,1)S(1)}, u32[]{:S(2)}, u32[]{:S(2)}) %all-to-all-start) | async-done | bytes 131104 | tf_op jit(solution)/shard_map/all_to_all | solution.py:706
  602.8 4.3 collective-permute-done.29
  609.6 8.8 %collective-permute-done.30 = bf16[1,96,1024]{2,1,0:T(8,128)(2,1)S(1)} collective-permute-done((bf16[1,96,1024]{2,1,0:T(8,128)(2,1)S(1)}, bf16[1,96,1024]{2,1,0:T(8,128)(2,1)S(1)}, u32[]{:S(2)}, u32[]{:S(2)}) %collective-permute-start.30) | collective-permute-done | bytes 196640 | tf_op jit(solution)/shard_map/ppermute | solution.py:351
  (422 shorter events, 137.6 us)
Async XLA Ops:
  7.2 166.2 %all-gather.5.cloned.1.call-start = ((), (), s32[]{:S(2)}) async-start(), calls=%async_computation.4 | async-start | bytes 19464192 | tf_op jit(solution)/shard_map/all_gather | solution.py:516
  10.8 291.4 %all-gather.7.cloned.1.call-start = ((), (), s32[]{:S(2)}) async-start(), calls=%async_computation.5 | async-start | bytes 17301504 | tf_op jit(solution)/shard_map/all_gather | solution.py:521
  11.5 11.4 %collective-permute-start.8 = (s32[128]{0:T(128)}, s32[128]{0:T(128)S(1)}, u32[]{:S(2)}, u32[]{:S(2)}) collective-permute-start(s32[128]{0:T(128)} %fusion.17), channel_id=1, source_target_pairs={{0,4},{1,5},{2,6},{3,7},{4,0},{5,1},{6,2},{7,3},{8,12},{9,13},{10,... | collective-permute-start | bytes 1544 | tf_op jit(solution)/shard_map/ppermute | solution.py:351
  16.2 41.4 %collective-permute-start.4 = (bf16[128,768]{1,0:T(8,128)(2,1)}, bf16[128,768]{1,0:T(8,128)(2,1)}, u32[]{:S(2)}, u32[]{:S(2)}) collective-permute-start(bf16[128,768]{1,0:T(8,128)(2,1)} %dynamic-slice_bitcast_fusion.7), channel_id=1, source_target_pairs={{0,4},{1,5},{2,6},{3,7},{4,0},{5,1},{6,2},{7,3},{8,12},{9,13},{10,... | collective-permute-start | bytes 589832 | tf_op jit(solution)/shard_map/ppermute | solution.py:351
  17.0 40.4 %collective-permute-start = (bf16[192,1024]{1,0:T(8,128)(2,1)}, bf16[192,1024]{1,0:T(8,128)(2,1)S(1)}, u32[]{:S(2)}, u32[]{:S(2)}) collective-permute-start(bf16[192,1024]{1,0:T(8,128)(2,1)} %dynamic-slice_bitcast_fusion.5), channel_id=1, source_target_pairs={{0,4},{1,5},{2,6},{3,7},{4,0},{5,1},{6,2},{7,3},{8,12},{9,13},{10,... | collective-permute-start | bytes 1179656 | tf_op jit(solution)/shard_map/ppermute | solution.py:351
  22.9 34.7 %collective-permute-start.9 = (s32[256]{0:T(256)S(1)}, s32[256]{0:T(256)S(1)}, u32[]{:S(2)}, u32[]{:S(2)}) collective-permute-start(s32[256]{0:T(256)S(1)} %pad_add_fusion), channel_id=1, source_target_pairs={{0,1},{1,0},{2,3},{3,2},{4,5},{5,4},{6,7},{7,6},{8,9},{9,8},{10,11... | collective-permute-start | bytes 3080 | tf_op jit(solution)/shard_map/ppermute | solution.py:351
  23.0 34.5 %collective-permute-start.10 = (s32[256]{0:T(256)S(1)}, s32[256]{0:T(256)S(1)}, u32[]{:S(2)}, u32[]{:S(2)}) collective-permute-start(s32[256]{0:T(256)S(1)} %pad_add_fusion), channel_id=1, source_target_pairs={{0,2},{1,3},{2,0},{3,1},{4,6},{5,7},{6,4},{7,5},{8,10},{9,11},{10,... | collective-permute-start | bytes 3080 | tf_op jit(solution)/shard_map/ppermute | solution.py:351
  57.4 51.6 %collective-permute-start.2 = (bf16[384,1024]{1,0:T(8,128)(2,1)S(1)}, bf16[384,1024]{1,0:T(8,128)(2,1)S(1)}, u32[]{:S(2)}, u32[]{:S(2)}) collective-permute-start(bf16[384,1024]{1,0:T(8,128)(2,1)S(1)} %pad_maximum_fusion.8), channel_id=1, source_target_pairs={{0,2},{1,3},{2,0},{3,1},{4,6},{5,7},{6,4},{7,5},{8,10},{9,11},{10,... | collective-permute-start | bytes 2359304 | tf_op jit(solution)/shard_map/ppermute | solution.py:351
  58.6 50.4 %collective-permute-start.6 = (bf16[256,768]{1,0:T(8,128)(2,1)S(1)}, bf16[256,768]{1,0:T(8,128)(2,1)S(1)}, u32[]{:S(2)}, u32[]{:S(2)}) collective-permute-start(bf16[256,768]{1,0:T(8,128)(2,1)S(1)} %pad_maximum_fusion.11), channel_id=1, source_target_pairs={{0,2},{1,3},{2,0},{3,1},{4,6},{5,7},{6,4},{7,5},{8,10},{9,11},{10,... | collective-permute-start | bytes 1179656 | tf_op jit(solution)/shard_map/ppermute | solution.py:351
  60.7 49.8 %collective-permute-start.5 = (bf16[256,768]{1,0:T(8,128)(2,1)S(1)}, bf16[256,768]{1,0:T(8,128)(2,1)S(1)}, u32[]{:S(2)}, u32[]{:S(2)}) collective-permute-start(bf16[256,768]{1,0:T(8,128)(2,1)S(1)} %pad_maximum_fusion.11), channel_id=1, source_target_pairs={{0,1},{1,0},{2,3},{3,2},{4,5},{5,4},{6,7},{7,6},{8,9},{9,8},{10,11... | collective-permute-start | bytes 1179656 | tf_op jit(solution)/shard_map/ppermute | solution.py:351
  61.0 49.8 %collective-permute-start.1 = (bf16[384,1024]{1,0:T(8,128)(2,1)S(1)}, bf16[384,1024]{1,0:T(8,128)(2,1)S(1)}, u32[]{:S(2)}, u32[]{:S(2)}) collective-permute-start(bf16[384,1024]{1,0:T(8,128)(2,1)S(1)} %pad_maximum_fusion.8), channel_id=1, source_target_pairs={{0,1},{1,0},{2,3},{3,2},{4,5},{5,4},{6,7},{7,6},{8,9},{9,8},{10,11... | collective-permute-start | bytes 2359304 | tf_op jit(solution)/shard_map/ppermute | solution.py:351
  173.4 289.6 %reduce-scatter.10.cloned.1.call-start = ((), (), s32[]{:S(2)}) async-start(), calls=%async_computation.6 | async-start | bytes 10485760
  221.1 56.3 %collective-permute-start.12 = (bf16[192,1024]{1,0:T(8,128)(2,1)}, bf16[192,1024]{1,0:T(8,128)(2,1)}, u32[]{:S(2)}, u32[]{:S(2)}) collective-permute-start(bf16[192,1024]{1,0:T(8,128)(2,1)} %get-tuple-element.230), channel_id=1, source_target_pairs={{0,4},{1,5},{2,6},{3,7},{4,0},{5,1},{6,2},{7,3},{8,12},{9,13},{10,... | collective-permute-start | bytes 1179656 | tf_op jit(solution)/shard_map/ppermute | solution.py:351
  333.1 13.4 %collective-permute-start.13 = (bf16[16,256,1024]{2,1,0:T(8,128)(2,1)}, bf16[16,256,1024]{2,1,0:T(8,128)(2,1)S(1)}, u32[]{:S(2)}, u32[]{:S(2)}) collective-permute-start(bf16[16,256,1024]{2,1,0:T(8,128)(2,1)} %get-tuple-element.112), channel_id=1, source_target_pairs={{0,1},{1,0},{2,3},{3,2},{4,5},{5,4},{6,7},{7,6},{8,9},{9,8},{10,11... | collective-permute-start | bytes 25165832 | tf_op jit(solution)/shard_map/ppermute | solution.py:351
  355.7 158.5 %reduce-scatter.12.cloned.1.call-start = ((), (), s32[]{:S(2)}) async-start(), calls=%async_computation.7 | async-start | bytes 7864320
  410.1 10.7 %collective-permute-start.15 = (bf16[16,192,1024]{2,1,0:T(8,128)(2,1)}, bf16[16,192,1024]{2,1,0:T(8,128)(2,1)}, u32[]{:S(2)}, u32[]{:S(2)}) collective-permute-start(bf16[16,192,1024]{2,1,0:T(8,128)(2,1)} %get-tuple-element.122), channel_id=1, source_target_pairs={{0,1},{1,0},{2,3},{3,2},{4,5},{5,4},{6,7},{7,6},{8,9},{9,8},{10,11... | collective-permute-start | bytes 18874376 | tf_op jit(solution)/shard_map/ppermute | solution.py:351
  420.8 8.1 %collective-permute-start.16 = (bf16[256,768]{1,0:T(8,128)(2,1)}, bf16[256,768]{1,0:T(8,128)(2,1)}, u32[]{:S(2)}, u32[]{:S(2)}) collective-permute-start(bf16[256,768]{1,0:T(8,128)(2,1)} %get-tuple-element.125), channel_id=1, source_target_pairs={{0,1},{1,0},{2,3},{3,2},{4,5},{5,4},{6,7},{7,6},{8,9},{9,8},{10,11... | collective-permute-start | bytes 1179656 | tf_op jit(solution)/shard_map/ppermute | solution.py:351
  428.9 165.5 %reduce-scatter.14.cloned.1.call-start = ((), (), s32[]{:S(2)}) async-start(), calls=%async_computation.8 | async-start | bytes 3932160
  430.9 32.1 %collective-permute-start.14 = (bf16[192,1024]{1,0:T(8,128)(2,1)}, bf16[192,1024]{1,0:T(8,128)(2,1)}, u32[]{:S(2)}, u32[]{:S(2)}) collective-permute-start(bf16[192,1024]{1,0:T(8,128)(2,1)} %get-tuple-element.228), channel_id=1, source_target_pairs={{0,4},{1,5},{2,6},{3,7},{4,0},{5,1},{6,2},{7,3},{8,12},{9,13},{10,... | collective-permute-start | bytes 1179656 | tf_op jit(solution)/shard_map/ppermute | solution.py:351
  434.0 29.0 %collective-permute-start.18 = (bf16[256,768]{1,0:T(8,128)(2,1)}, bf16[256,768]{1,0:T(8,128)(2,1)}, u32[]{:S(2)}, u32[]{:S(2)}) collective-permute-start(bf16[256,768]{1,0:T(8,128)(2,1)} %add_convert_fusion.11), channel_id=1, source_target_pairs={{0,2},{1,3},{2,0},{3,1},{4,6},{5,7},{6,4},{7,5},{8,10},{9,11},{10,... | collective-permute-start | bytes 1179656 | tf_op jit(solution)/shard_map/ppermute | solution.py:351
  464.5 29.2 %collective-permute-start.21 = (bf16[2,256,1024]{2,1,0:T(8,128)(2,1)S(1)}, bf16[2,256,1024]{2,1,0:T(8,128)(2,1)S(1)}, u32[]{:S(2)}, u32[]{:S(2)}) collective-permute-start(bf16[2,256,1024]{2,1,0:T(8,128)(2,1)S(1)} %dynamic-slice_bitcast_fusion), channel_id=1, source_target_pairs={{0,2},{1,3},{2,0},{3,1},{4,6},{5,7},{6,4},{7,5},{8,10},{9,11},{10,... | collective-permute-start | bytes 3145736 | tf_op jit(solution)/shard_map/ppermute | solution.py:351
  475.9 17.7 %collective-permute-start.19 = (bf16[384,1024]{1,0:T(8,128)(2,1)S(1)}, bf16[384,1024]{1,0:T(8,128)(2,1)S(1)}, u32[]{:S(2)}, u32[]{:S(2)}) collective-permute-start(bf16[384,1024]{1,0:T(8,128)(2,1)S(1)} %get-tuple-element.140), channel_id=1, source_target_pairs={{0,1},{1,0},{2,3},{3,2},{4,5},{5,4},{6,7},{7,6},{8,9},{9,8},{10,11... | collective-permute-start | bytes 2359304 | tf_op jit(solution)/shard_map/ppermute | solution.py:351
  476.0 17.7 %collective-permute-start.20 = (bf16[384,1024]{1,0:T(8,128)(2,1)S(1)}, bf16[384,1024]{1,0:T(8,128)(2,1)S(1)}, u32[]{:S(2)}, u32[]{:S(2)}) collective-permute-start(bf16[384,1024]{1,0:T(8,128)(2,1)S(1)} %get-tuple-element.141), channel_id=1, source_target_pairs={{0,1},{1,0},{2,3},{3,2},{4,5},{5,4},{6,7},{7,6},{8,9},{9,8},{10,11... | collective-permute-start | bytes 2359304 | tf_op jit(solution)/shard_map/ppermute | solution.py:351
  494.1 20.1 %collective-permute-start.23 = (bf16[384,1024]{1,0:T(8,128)(2,1)S(1)}, bf16[384,1024]{1,0:T(8,128)(2,1)}, u32[]{:S(2)}, u32[]{:S(2)}) collective-permute-start(bf16[384,1024]{1,0:T(8,128)(2,1)S(1)} %add_convert_fusion.7), channel_id=1, source_target_pairs={{0,2},{1,3},{2,0},{3,1},{4,6},{5,7},{6,4},{7,5},{8,10},{9,11},{10,... | collective-permute-start | bytes 2359304 | tf_op jit(solution)/shard_map/ppermute | solution.py:351
  523.0 35.3 %collective-permute-start.26 = (bf16[1,256,1024]{2,1,0:T(8,128)(2,1)}, bf16[1,256,1024]{2,1,0:T(8,128)(2,1)}, u32[]{:S(2)}, u32[]{:S(2)}) collective-permute-start(bf16[1,256,1024]{2,1,0:T(8,128)(2,1)} %fusion.6), channel_id=1, source_target_pairs={{0,4},{1,5},{2,6},{3,7},{4,0},{5,1},{6,2},{7,3},{8,12},{9,13},{10,... | collective-permute-start | bytes 1572872 | tf_op jit(solution)/shard_map/ppermute | solution.py:351
  530.2 40.7 %collective-permute-start.25 = (bf16[192,1024]{1,0:T(8,128)(2,1)}, bf16[192,1024]{1,0:T(8,128)(2,1)}, u32[]{:S(2)}, u32[]{:S(2)}) collective-permute-start(bf16[192,1024]{1,0:T(8,128)(2,1)} %get-tuple-element.226), channel_id=1, source_target_pairs={{0,4},{1,5},{2,6},{3,7},{4,0},{5,1},{6,2},{7,3},{8,12},{9,13},{10,... | collective-permute-start | bytes 1179656 | tf_op jit(solution)/shard_map/ppermute | solution.py:351
  533.1 43.6 %collective-permute-start.24 = (bf16[2,192,1024]{2,1,0:T(8,128)(2,1)}, bf16[2,192,1024]{2,1,0:T(8,128)(2,1)}, u32[]{:S(2)}, u32[]{:S(2)}) collective-permute-start(bf16[2,192,1024]{2,1,0:T(8,128)(2,1)} %dynamic-slice_bitcast_fusion.1), channel_id=1, source_target_pairs={{0,2},{1,3},{2,0},{3,1},{4,6},{5,7},{6,4},{7,5},{8,10},{9,11},{10,... | collective-permute-start | bytes 2359304 | tf_op jit(solution)/shard_map/ppermute | solution.py:351
  539.0 55.4 %collective-permute-start.28 = (bf16[128,768]{1,0:T(8,128)(2,1)}, bf16[128,768]{1,0:T(8,128)(2,1)}, u32[]{:S(2)}, u32[]{:S(2)}) collective-permute-start(bf16[128,768]{1,0:T(8,128)(2,1)} %get-tuple-element.232), channel_id=1, source_target_pairs={{0,4},{1,5},{2,6},{3,7},{4,0},{5,1},{6,2},{7,3},{8,12},{9,13},{10,... | collective-permute-start | bytes 589832 | tf_op jit(solution)/shard_map/ppermute | solution.py:351
  577.8 16.6 %collective-permute-start.27 = (bf16[1,192,1024]{2,1,0:T(8,128)(2,1)S(1)}, bf16[1,192,1024]{2,1,0:T(8,128)(2,1)S(1)}, u32[]{:S(2)}, u32[]{:S(2)}) collective-permute-start(bf16[1,192,1024]{2,1,0:T(8,128)(2,1)S(1)} %fusion.7), channel_id=1, source_target_pairs={{0,4},{1,5},{2,6},{3,7},{4,0},{5,1},{6,2},{7,3},{8,12},{9,13},{10,... | collective-permute-start | bytes 1179656 | tf_op jit(solution)/shard_map/ppermute | solution.py:351
  578.6 15.7 %all-to-all-start = ((bf16[32,2,1024]{2,1,0:T(2,128)(2,1)}), bf16[32,2,1024]{2,1,0:T(2,128)(2,1)S(1)}, u32[]{:S(2)}, u32[]{:S(2)}) async-start(bf16[32,2,1024]{2,1,0:T(2,128)(2,1)} %reshape.556), calls=%async_computation | async-start | bytes 262144 | tf_op jit(solution)/shard_map/all_to_all | solution.py:706
  595.8 11.3 %collective-permute-start.29 = (bf16[2,96,1024]{2,1,0:T(8,128)(2,1)S(1)}, bf16[2,96,1024]{2,1,0:T(8,128)(2,1)S(1)}, u32[]{:S(2)}, u32[]{:S(2)}) collective-permute-start(bf16[2,96,1024]{2,1,0:T(8,128)(2,1)S(1)} %dynamic-slice_bitcast_fusion.2), channel_id=1, source_target_pairs={{0,2},{1,3},{2,0},{3,1},{4,6},{5,7},{6,4},{7,5},{8,10},{9,11},{10,... | collective-permute-start | bytes 1179656 | tf_op jit(solution)/shard_map/ppermute | solution.py:351
  607.1 11.3 %collective-permute-start.30 = (bf16[1,96,1024]{2,1,0:T(8,128)(2,1)S(1)}, bf16[1,96,1024]{2,1,0:T(8,128)(2,1)S(1)}, u32[]{:S(2)}, u32[]{:S(2)}) collective-permute-start(bf16[1,96,1024]{2,1,0:T(8,128)(2,1)S(1)} %fusion.8), channel_id=1, source_target_pairs={{0,4},{1,5},{2,6},{3,7},{4,0},{5,1},{6,2},{7,3},{8,12},{9,13},{10,... | collective-permute-start | bytes 589832 | tf_op jit(solution)/shard_map/ppermute | solution.py:351
  (89 other events, 1216.1 us)
Sparse Core Ops, SparseCore 0:
  11.6 161.7 all-gather.4
  177.0 125.2 all-gather.6
  355.8 84.5 reduce-scatter.9
  443.6 70.2 reduce-scatter.11
  516.9 43.9 reduce-scatter.13

commit v4 on v3

--- a/solution.py
+++ b/solution.py
@@ -43,13 +43,12 @@
     )
 
 
-def attend_kernel(count, masked, *refs):
-    q_ref, kv = refs[0], refs[1 : 1 + count]
-    bias = refs[1 + count] if masked else None
+def attend_kernel(masked, *refs):
+    q_ref, kv_ref = refs[:2]
+    bias = refs[2] if masked else None
     o_ref, lse_ref = refs[-2:]
     query = q_ref[...]
-    keys = jnp.concatenate([r[:, :PAIR] for r in kv], 0)
-    values = jnp.concatenate([r[:, PAIR:] for r in kv], 0)
+    keys, values = kv_ref[:, :PAIR], kv_ref[:, PAIR:]
     low = lax.broadcasted_iota(jnp.int32, query.shape, 1) < HEAD_DIM
     outs, lses = [], []
     for head in range(2):
@@ -66,37 +65,38 @@
     lse_ref[...] = jnp.where(low, lses[0], lses[1])[None]
 
 
-def attend(query, kvs, bias):
+def attend(query, kv, bias):
     rows, width = query.shape
-    count, slots, pairs = len(kvs), kvs[0].shape[0], width // PAIR
-    row = pl.BlockSpec((rows, PAIR), lambda i: (0, i))
-    slot = pl.BlockSpec((slots, 2 * PAIR), lambda i: (0, i))
+    slots, pairs = kv.shape[0], width // PAIR
+    tile = min(rows, 384)
+    row = pl.BlockSpec((tile, PAIR), lambda i, r: (r, i))
     masked = bias is not None
-    total = count * slots
     return pl.pallas_call(
-        partial(attend_kernel, count, masked),
-        grid=(pairs,),
-        in_specs=[row] + [slot] * count + [pl.BlockSpec((1, total), lambda i: (0, 0))] * masked,
-        out_specs=[row, pl.BlockSpec((1, rows, PAIR), lambda i: (i, 0, 0))],
+        partial(attend_kernel, masked),
+        grid=(pairs, rows // tile),
+        in_specs=[row, pl.BlockSpec((slots, 2 * PAIR), lambda i, r: (0, i))]
+        + [pl.BlockSpec((1, slots), lambda i, r: (0, 0))] * masked,
+        out_specs=[row, pl.BlockSpec((1, tile, PAIR), lambda i, r: (i, r, 0))],
         out_shape=[
             jax.ShapeDtypeStruct((rows, width), bf16),
             jax.ShapeDtypeStruct((pairs, rows, PAIR), f32),
         ],
         compiler_params=params(),
         name="attend",
-        cost_estimate=pl.CostEstimate(flops=1, bytes_accessed=1, transcendentals=0),
-    )(query, *kvs, *([bias] if masked else []))
-
-
-def attend_back_kernel(count, masked, *refs):
-    q_ref, kv = refs[0], refs[1 : 1 + count]
-    o_ref, do_ref, lse_ref = refs[1 + count : 4 + count]
-    bias = refs[4 + count] if masked else None
-    dq_ref, dkv = refs[-1 - count], refs[-count:]
+        cost_estimate=pl.CostEstimate(
+            flops=16 * rows * slots * width,
+            bytes_accessed=4 * width * (rows + slots),
+            transcendentals=2 * pairs * rows * slots,
+        ),
+    )(query, kv, *([bias] if masked else []))
+
+
+def attend_back_kernel(masked, *refs):
+    q_ref, kv_ref, o_ref, do_ref, lse_ref = refs[:5]
+    bias = refs[5] if masked else None
+    dq_ref, dkv_ref, dk_s, dv_s = refs[-4:]
     query, grad = q_ref[...], do_ref[...]
-    slots = kv[0].shape[0]
-    keys = jnp.concatenate([r[:, :PAIR] for r in kv], 0)
-    values = jnp.concatenate([r[:, PAIR:] for r in kv], 0)
+    keys, values = kv_ref[:, :PAIR], kv_ref[:, PAIR:]
     low = lax.broadcasted_iota(jnp.int32, query.shape, 1) < HEAD_DIM
     lse = lse_ref[0]
     product = o_ref[...].astype(f32) * grad.astype(f32)
@@ -116,34 +116,50 @@
         dv = dv + dot(jnp.transpose(head_grad), probs.astype(bf16))
         dqs.append(dot(score_grad, keys))
     dq_ref[...] = (jnp.where(low, dqs[0], dqs[1]) * HEAD_DIM**-0.5).astype(bf16)
-    dk, dv = jnp.transpose(dk), jnp.transpose(dv)
-    for j in range(count):
-        dkv[j][:, :PAIR] = dk[j * slots : (j + 1) * slots].astype(bf16)
-        dkv[j][:, PAIR:] = dv[j * slots : (j + 1) * slots].astype(bf16)
-
-
-def attend_back(query, kvs, out, grad, lse, bias):
+    step = pl.program_id(1)
+
+    @pl.when(step == 0)
+    def _():
+        dk_s[...] = dk
+        dv_s[...] = dv
+
+    @pl.when(step > 0)
+    def _():
+        dk_s[...] += dk
+        dv_s[...] += dv
+
+    @pl.when(step == pl.num_programs(1) - 1)
+    def _():
+        dkv_ref[:, :PAIR] = jnp.transpose(dk_s[...]).astype(bf16)
+        dkv_ref[:, PAIR:] = jnp.transpose(dv_s[...]).astype(bf16)
+
+
+def attend_back(query, kv, out, grad, lse, bias):
     rows, width = query.shape
-    count, slots, pairs = len(kvs), kvs[0].shape[0], width // PAIR
-    row = pl.BlockSpec((rows, PAIR), lambda i: (0, i))
-    slot = pl.BlockSpec((slots, 2 * PAIR), lambda i: (0, i))
+    slots, pairs = kv.shape[0], width // PAIR
+    tile = min(rows, 384)
+    row = pl.BlockSpec((tile, PAIR), lambda i, r: (r, i))
+    slot = pl.BlockSpec((slots, 2 * PAIR), lambda i, r: (0, i))
     masked = bias is not None
-    total = count * slots
-    result = pl.pallas_call(
-        partial(attend_back_kernel, count, masked),
-        grid=(pairs,),
-        in_specs=[row]
-        + [slot] * count
-        + [row, row, pl.BlockSpec((1, rows, PAIR), lambda i: (i, 0, 0))]
-        + [pl.BlockSpec((1, total), lambda i: (0, 0))] * masked,
-        out_specs=[row] + [slot] * count,
-        out_shape=[jax.ShapeDtypeStruct((rows, width), bf16)]
-        + [jax.ShapeDtypeStruct((slots, 2 * width), bf16)] * count,
+    return pl.pallas_call(
+        partial(attend_back_kernel, masked),
+        grid=(pairs, rows // tile),
+        in_specs=[row, slot, row, row, pl.BlockSpec((1, tile, PAIR), lambda i, r: (i, r, 0))]
+        + [pl.BlockSpec((1, slots), lambda i, r: (0, 0))] * masked,
+        out_specs=[row, slot],
+        out_shape=[
+            jax.ShapeDtypeStruct((rows, width), bf16),
+            jax.ShapeDtypeStruct((slots, 2 * width), bf16),
+        ],
+        scratch_shapes=[pltpu.VMEM((PAIR, slots), f32)] * 2,
         compiler_params=params(),
         name="attend_back",
-        cost_estimate=pl.CostEstimate(flops=1, bytes_accessed=1, transcendentals=0),
-    )(query, *kvs, out, grad, lse, *([bias] if masked else []))
-    return result[0], result[1:]
+        cost_estimate=pl.CostEstimate(
+            flops=40 * rows * slots * width,
+            bytes_accessed=8 * width * (rows + slots),
+            transcendentals=2 * pairs * rows * slots,
+        ),
+    )(query, kv, out, grad, lse, *([bias] if masked else []))
 
 
 def block_kernel(core_ref, third_ref, cot_ref, gain_ref, shift_ref, dbias_ref, ubias_ref, up_ref, down_ref,
@@ -359,19 +375,50 @@
             found.update({d ^ mask: self.swap(v, mask) for d, v in list(found.items())})
         return [found[d] for d in range(self.seq // 2)]
 
-    def sum_group(self, terms):
-        terms = {d: [t] for d, t in enumerate(terms)}
-        for mask in self.group[:1] + self.group[1:]:
-            for d in [d for d in terms if d & mask]:
-                moved = self.swap(add(terms.pop(d)), mask)
-                terms[d ^ mask].append(moved)
-        return add(terms[0])
-
-    def scatter(self, keep, send):
+    def in_order(self, terms):
+        spot = self.place % len(terms)
+        stacked = jnp.stack(terms)
+        return [
+            lax.dynamic_index_in_dim(stacked, spot ^ j, 0, keepdims=False) for j in range(len(terms))
+        ]
+
+    def exchange(self, blocks):
+        spot = self.place % blocks.shape[0]
+        found = []
+        for d in range(blocks.shape[0]):
+            block = lax.dynamic_index_in_dim(blocks, spot ^ d, 0, keepdims=False)
+            found.append(self.swap(block, d) if d else block)
+        return found
+
+    def gather_self(self, blocks):
+        found = yield self.exchange(blocks)
+        found = jnp.stack(self.in_order(found))
+        for mask in [m for m in (1 << k for k in range(20)) if self.far <= m < self.all]:
+            moved = yield self.swap(found, mask)
+            found = jnp.where(
+                self.bit(mask) == 0, jnp.concatenate([found, moved]), jnp.concatenate([moved, found])
+            )
+        yield found
+
+    def scatter_self(self, grad):
+        terms = [grad]
+        for mask in [m for m in (1 << k for k in range(20)) if self.far <= m < self.all][::-1]:
+            terms = [t.reshape(2, t.shape[0] // 2, *t.shape[1:]) for t in terms]
+            pick = lambda t, which: lax.dynamic_index_in_dim(t, which, 0, keepdims=False)
+            moved = yield self.swap(add([pick(t, 1 - self.bit(mask)) for t in terms]), mask)
+            terms = [pick(t, self.bit(mask)) for t in terms] + [moved]
+        found = yield self.exchange(add(terms))
+        yield jnp.stack(self.in_order(found), 1)
+
+    def scatter(self, keep, send, whole):
         moved = yield self.swap(send, 1)
         total = add([keep, moved]).reshape(self.obj, self.seq // 2, *keep.shape[1:])
         total = yield total
         total = yield lax.psum_scatter(total, "obj", scatter_dimension=0, tiled=False)
+        if whole:
+            moved = yield lax.all_to_all(total, "ring", 0, 0, tiled=True)
+            yield jnp.sum(moved.astype(f32), 0)
+            return
         terms = [total]
         for mask in self.group[1:] + [self.far]:
             terms = [t.reshape(t.shape[0] // 2, 2, *t.shape[1:]) for t in terms]
@@ -469,6 +516,9 @@
         mine = mine[: other.shape[0]]
         return jnp.where(half == 0, jnp.stack([mine, other]), jnp.stack([other, mine]))
 
+    def chunks(terms):
+        return jnp.split(terms, grid.seq // 2, 0)
+
     shard = self_output.shape[0]
     self_mixed = jnp.concatenate(
         [low(self_weight[:, :width]), split_pairs(low(self_weight[:, width:]))], 1
@@ -496,45 +546,50 @@
         up_bias.size,
     ]
     patch_rows = patch_weight.shape[0]
-    small_count = -(-small.size // width)
-    patch_room = -(-(patch_rows + small_count) // shard) * shard
-    small_rows = jnp.pad(small, (0, small_count * width - small.size)).reshape(-1, width)
+    group = grid.seq // 2
+    lot = 3 * width // group
+    few = width // group
+    small_count = -(-small.size // lot)
+    small_rows = jnp.pad(small, (0, small_count * lot - small.size)).reshape(-1, lot)
+    blocks = jnp.concatenate(
+        [
+            self_mixed[:, :width].reshape(shard, group, few),
+            self_mixed[:, width:].reshape(shard, group, 2 * few),
+        ],
+        2,
+    ).transpose(1, 0, 2)
+    blocks = jnp.concatenate(
+        [blocks, jnp.broadcast_to(pad_rows(small_rows, -(-small_count // 8) * 8), (group, -(-small_count // 8) * 8, lot))], 1
+    )
+    patch_room = -(-patch_rows // shard) * shard
     first = jnp.concatenate(
         [
-            stack_columns(self_mixed, width),
             low(self_output),
             low(cross_query),
             low(cross_output),
             stack_columns(split_pairs(low(cross_memory)), width),
-            pad_rows(jnp.concatenate([low(patch_weight), small_rows], 0), patch_room),
+            pad_rows(low(patch_weight), patch_room),
         ],
         0,
     )
+    own_gather = grid.gather_self(blocks)
+    blocks = next(own_gather)
     tokens_all = jnp.concatenate(grid.gather_group(compact(tokens)), 0)
+    first = lax.all_gather(first, BOTH, axis=0, tiled=False)
+    ffn_mine = jnp.concatenate([stack_columns(low(up_weight), width), low(down_weight)], 0)
+    while isinstance(blocks, list) or blocks.shape[0] < parts:
+        blocks = own_gather.send(blocks)
+        if isinstance(blocks, list) or blocks.shape[0] == parts // 2:
+            break
+    blocks, tokens_all, ffn_mine, patches, patch_index = together(
+        (blocks, tokens_all, ffn_mine, patches, patch_index)
+    )
+    packed = lax.all_gather(ffn_mine, BOTH, axis=0, tiled=False)
     feats_all = jnp.concatenate(grid.gather_group(compact(patches)), 0)
     views_all = jnp.concatenate(grid.gather_group(compact(patch_index)), 0) // VIEW_PATCHES
-    first = lax.all_gather(first, BOTH, axis=0, tiled=False)
-    ffn_mine = jnp.concatenate([stack_columns(low(up_weight), width), low(down_weight)], 0)
-    first, ffn_mine, tokens_all, feats_all, views_all = together(
-        (first, ffn_mine, tokens_all, feats_all, views_all)
-    )
-    packed = lax.all_gather(ffn_mine, BOTH, axis=0, tiled=False)
-
-    def square(start, rows=shard):
-        return first[:, start : start + rows].reshape(parts * rows, width)
-
-    def columns(start, count):
-        return jnp.concatenate([square(start + q * shard) for q in range(count)], 1)
-
-    full_q = square(0)
-    full_kv = columns(shard, 2)
-    full_out = square(3 * shard)
-    full_cq = square(4 * shard)
-    full_co = square(5 * shard)
-    full_mem = columns(6 * shard, 2)
-    full_patch = square(8 * shard, patch_rows)
-    at = 8 * shard + patch_rows
-    tiny = first[:, at : at + small_count].reshape(parts, -1)
+    blocks = own_gather.send(blocks)
+    self_own = blocks[:, :shard].reshape(parts * shard, lot)
+    tiny = blocks[:, shard : shard + small_count].reshape(parts, -1)
     pieces = []
     at = 0
     for size in small_sizes:
@@ -552,17 +607,30 @@
     live = lax.dynamic_index_in_dim(patch_count, half, 0, keepdims=False)
     modulation = jnp.sum(camera_mine[:, None] * full_camera, 0)
     scale1, shift1 = 1.0 + modulation[None, :width], modulation[None, width:]
-    unit_all, rstd_all = norm_parts(x_all)
-    unit1, rstd1 = unit_all[:own], rstd_all[:own]
-    hidden_all = low(unit_all * scale1 + shift1)
-    hidden = hidden_all[:own]
-    query = low(low(dot(hidden, full_q)).astype(f32) * factor)
-    kvs = [low(dot(hidden_all, full_kv))]
-
+    hidden_all = low(norm_parts(x_all)[0] * scale1 + shift1)
+    triple = low(dot(hidden_all, self_own))
+    query = low(triple[:, :few].astype(f32) * factor)
+    kv = triple[:, few:]
+    query, kv, feats_all, views_all, cotangent = together((query, kv, feats_all, views_all, cotangent))
+    attended_own, lse1 = attend(query, kv, None)
+    attended_own, first = together((attended_own, first))
+    cot = compact(cotangent)
+    attended = grid.exchange(jnp.stack(grid.in_order(chunks(attended_own))))
+
+    def square(start, rows=shard):
+        return first[:, start : start + rows].reshape(parts * rows, width)
+
+    full_out = square(0)
+    full_cq = square(shard)
+    full_co = square(2 * shard)
+    full_mem = jnp.concatenate([square(3 * shard), square(4 * shard)], 1)
+    full_patch = square(5 * shard, patch_rows)
     hot_all = (views_all[:, None] == jnp.arange(VIEWS)[None, :]).astype(f32)
     view_part = sum(hot_all[:, v : v + 1] * full_view[v : v + 1] for v in range(VIEWS))
     embedded_all = low(dot(feats_all, full_patch) + view_part)
-    mems = [low(dot(embedded_all, full_mem))]
+    mem = low(dot(embedded_all, full_mem))
+    attended, mem = together((attended, mem))
+    attended = jnp.concatenate(grid.in_order(attended), 1)
     place = grid.place
     chunk = patches.shape[1]
     lane = jnp.arange(chunk)
@@ -575,14 +643,11 @@
     )
     bias = jnp.where(slots < live, 0.0, -1e30).astype(f32).reshape(1, -1)
 
-    query, kvs, mems, cotangent = together((query, kvs, mems, cotangent))
-    cot = compact(cotangent)
-    attended, lse1 = attend(query, kvs, None)
     second = x + dot(attended, full_out)
     unit2, rstd2 = norm_parts(second)
     normed = low(unit2 * g_mid + b_mid)
     asked = low(low(dot(normed, full_cq)).astype(f32) * factor)
-    crossed, lse2 = attend(asked, mems, bias)
+    crossed, lse2 = attend(asked, mem, bias)
     third = second + dot(crossed, full_co)
     third, cot = together((third, cot))
     core_now = core.reshape(1).astype(jnp.int32)
@@ -591,10 +656,7 @@
     )
     tall = down_weight.shape[0]
 
-    def chunks(terms):
-        return jnp.split(terms, grid.seq // 2, 0)
-
-    ffn = grid.scatter(ffn_keep, ffn_send)
+    ffn = grid.scatter(ffn_keep, ffn_send, True)
     ffn_moved = next(ffn)
     half_rows = result.shape[0] // 2
     third_low = low(third_grad)
@@ -605,8 +667,8 @@
 
     ffn_moved = ffn.send(ffn_moved)
     result_moved = grid.swap(result[half_rows:], grid.far)
-    asked_grad, mem_terms = attend_back(asked, mems, crossed, crossed_grad, lse2, bias)
-    mem_terms = mem_terms[0]
+    asked_grad, mem_terms = attend_back(asked, mem, crossed, crossed_grad, lse2, bias)
+    asked_grad, mem_terms, result_moved = together((asked_grad, mem_terms, result_moved))
     normed_grad = dot(asked_grad, full_cq, NT)
     second_grad = third_grad + norm_back(unit2, rstd2, normed_grad * g_mid)
     second_low = low(second_grad)
@@ -625,58 +687,60 @@
         embedded_grad,
     ]
     jobs = ((0, 1, 0), (2, 3, 0), (4, 5, 0), (6, 7, 0), (6, 7, 1), (8, 9, 0))
+    attended_grad, arrays = together((attended_grad, arrays))
+    grad_moved = []
+    for d in range(group):
+        at = ((grid.place % group) ^ d) * few
+        part = lax.dynamic_slice_in_dim(attended_grad, at, few, 1)
+        grad_moved.append(grid.swap(part, d) if d else part)
     keep, send = weight_grads(core_now, arrays, jobs, parts, shard, width)
-    rest = grid.scatter(keep, send)
+    grad_moved, keep, send = together((grad_moved, keep, send))
+    rest = grid.scatter(keep, send, False)
     moved = next(rest)
     patch_terms = chunks(low(dot(embedded_grad, full_patch, NT)))
-    attended_grad, patch_terms, moved = together((attended_grad, patch_terms, moved))
+    grad_own = jnp.concatenate(grad_moved, 0)
+    grad_own, patch_terms, moved = together((grad_own, patch_terms, moved))
     moved = rest.send(moved)
     patch_moved = grid.exchange_core(patch_terms)
-    attended_grad, patch_moved, moved = together((attended_grad, patch_moved, moved))
+    grad_own, patch_moved, moved, ffn_moved = together((grad_own, patch_moved, moved, ffn_moved))
 
     moved = rest.send(moved)
+    ffn_moved = ffn.send(ffn_moved)
     patch_mine, patch_moved = grid.exchange_line(patch_terms, patch_moved)
-    query_grad, pair_terms = attend_back(query, kvs, attended, attended_grad, lse1, None)
-    pair_terms = pair_terms[0]
-    ffn_moved, result_moved, patch_moved, query_grad, pair_terms = together(
-        (ffn_moved, result_moved, patch_moved, query_grad, pair_terms)
-    )
-
-    ffn_moved = ffn.send(ffn_moved)
-    hidden_terms = chunks(low(dot(pair_terms, full_kv, NT)))
-    hidden_terms, pair_terms, query_grad = together((hidden_terms, pair_terms, query_grad))
+    query_grad, pair_grad = attend_back(query, kv, attended_own, grad_own, lse1, None)
+    patch_moved, query_grad, pair_grad = together((patch_moved, query_grad, pair_grad))
+
+    triple_grad = jnp.concatenate([query_grad, pair_grad], 1)
+    hidden_terms = chunks(low(dot(triple_grad, self_own, NT)))
+    hidden_terms, triple_grad = together((hidden_terms, triple_grad))
     hidden_moved = grid.exchange_core(hidden_terms)
-    keep, send = weight_grads(
-        core_now,
-        [hidden, query_grad, hidden_all, pair_terms],
-        ((0, 1, 0), (2, 3, 0), (2, 3, 1)),
-        parts,
-        shard,
-        width,
-    )
-    keep, send, hidden_moved, ffn_moved = together((keep, send, hidden_moved, ffn_moved))
-
-    own_scatter = grid.scatter(keep, send)
+    self_grad = low(dot(hidden_all, triple_grad, TN))
+    self_grad, hidden_moved = together((self_grad, hidden_moved))
+
+    own_scatter = grid.scatter_self(self_grad.reshape(parts, shard, lot))
     own_moved = next(own_scatter)
     hidden_mine, hidden_moved = grid.exchange_line(hidden_terms, hidden_moved)
     patch_low = low(patch_mine.astype(f32) + patch_moved.astype(f32))
     patch_half = patch_low.shape[0] // 2
+    patch_moved = grid.swap(patch_low[patch_half:], grid.far)
+    result = spread(result, result_moved)
     view_grad = jnp.stack(
         [jnp.sum(hot_all[:, v : v + 1] * embedded_grad.astype(f32), 0) for v in range(VIEWS)]
     )
-    own_moved, patch_low, view_grad = together((own_moved, patch_low, view_grad))
+    mid_vectors = jnp.stack([jnp.sum(normed_grad * unit2, 0), jnp.sum(normed_grad, 0)])
+    own_moved, hidden_moved, patch_moved, result, view_grad, mid_vectors, last_vectors, up_bias_grad = together(
+        (own_moved, hidden_moved, patch_moved, result, view_grad, mid_vectors, last_vectors, up_bias_grad)
+    )
+
+    unit1, rstd1 = norm_parts(together(tokens_all[:own]).astype(f32))
+    hidden_grad = hidden_mine.astype(f32) + hidden_moved.astype(f32)
+    token_grad = low(second_grad + norm_back(unit1, rstd1, hidden_grad * scale1))
+    token_grad, hidden_grad, own_moved, moved, ffn_moved = together(
+        (token_grad, hidden_grad, own_moved, moved, ffn_moved)
+    )
+    token_moved = grid.swap(token_grad[half_rows:], grid.far)
+    moved = rest.send(moved)
     own_moved = own_scatter.send(own_moved)
-    own_moved, hidden_moved, moved = together((own_moved, hidden_moved, moved))
-
-    own_moved = own_scatter.send(own_moved)
-    ffn_moved = ffn.send(ffn_moved)
-    moved = rest.send(moved)
-    hidden_query = dot(query_grad, full_q, NT)
-    hidden_grad = hidden_query + hidden_mine.astype(f32) + hidden_moved.astype(f32)
-    token_grad = low(second_grad + norm_back(unit1, rstd1, hidden_grad * scale1))
-    token_grad, hidden_grad = together((token_grad, hidden_grad))
-    token_moved = grid.swap(token_grad[half_rows:], grid.far)
-    result = spread(result, result_moved)
     modulation_grad = jnp.concatenate(
         [jnp.sum(hidden_grad * unit1, 0), jnp.sum(hidden_grad, 0)]
     )
@@ -684,8 +748,7 @@
     vectors = jnp.concatenate(
         [
             view_grad,
-            jnp.sum(normed_grad * unit2, 0)[None],
-            jnp.sum(normed_grad, 0)[None],
+            mid_vectors,
             last_vectors[0:3],
         ],
         0,
@@ -698,37 +761,43 @@
         ],
         1,
     )
-    small_grad = jnp.pad(small_grad, ((0, 0), (0, small_count * width - small_grad.shape[1])))
-    moved, small_grad, token_moved, ffn_moved, result = together(
-        (moved, small_grad, token_moved, ffn_moved, result)
-    )
+    small_grad = jnp.pad(small_grad, ((0, 0), (0, small_count * lot - small_grad.shape[1])))
+    small_grad, own_moved, token_moved, moved = together((small_grad, own_moved, token_moved, moved))
+    while not isinstance(own_moved, list):
+        own_moved = own_scatter.send(own_moved)
+        if own_moved.shape[0] == group:
+            break
     moved = rest.send(moved)
-    small_grad = lax.all_to_all(small_grad.reshape(parts, small_count, width), BOTH, 0, 0, tiled=True)
-    patch_moved = grid.swap(patch_low[patch_half:], grid.far)
-    tiny = jnp.sum(small_grad.astype(f32), 0).reshape(-1)
+    small_grad = lax.all_to_all(small_grad.reshape(parts, small_count, lot), BOTH, 0, 0, tiled=True)
     token_grad = spread(token_grad, token_moved)
     ffn_grad = ffn.send(ffn_moved)
     ffn_up, ffn_down = unstack_columns(ffn_grad[:tall], shard), ffn_grad[tall:]
-    own_moved, moved, token_grad, patch_moved, tiny, ffn_up, ffn_down = together(
-        (own_moved, moved, token_grad, patch_moved, tiny, ffn_up, ffn_down)
+    patch_grad = spread(patch_low, patch_moved)
+    own_moved, moved, token_grad, small_grad, patch_grad, ffn_up, ffn_down = together(
+        (own_moved, moved, token_grad, small_grad, patch_grad, ffn_up, ffn_down)
     )
     own_moved = own_scatter.send(own_moved)
-    patch_grad = spread(patch_low, patch_moved)
-    own_moved = own_scatter.send(own_moved)
+    tiny = jnp.sum(small_grad.astype(f32), 0).reshape(-1)
     rest_sum = rest.send(moved)
-    self_sum = own_scatter.send(own_moved)
+    self_sum = own_scatter.send(own_moved).astype(f32)
     pieces = []
     at = 0
     for size in small_sizes:
         pieces.append(tiny[at : at + size])
         at += size
-    kv_own = join_pairs(unstack_columns(self_sum[shard : 3 * shard], shard))
+    self_sum = jnp.concatenate(
+        [
+            self_sum[:, :, :few].reshape(shard, width),
+            join_pairs(self_sum[:, :, few:].reshape(shard, 2 * width)),
+        ],
+        1,
+    )
     return (
         result,
         token_grad,
         patch_grad,
         pieces[0].reshape(camera_weight.shape),
-        jnp.concatenate([self_sum[:shard], kv_own], 1),
+        self_sum,
         rest_sum[2 * shard : 3 * shard],
         pieces[2],
         pieces[3],

time: 632 us -> 624 us (0.987)
  waiting for transfers between devices: 246 us -> 208 us
  starting transfers between devices: 33 us -> 57.2 us
  other arithmetic: 65.3 us -> 83.4 us
  matrix products: 59.8 us -> 42.9 us
  Pallas kernels: 151 us -> 137 us
  local copies, waits for them, and re-layouts: 56.6 us -> 69.5 us
    all_gather x1, waiting for transfers between devices: 61.5 us -> 0.01 us  [on_device(): first = lax.all_gather(first, BOTH, axis=0, tiled=False)]
    ppermute x31 -> x44, waiting for transfers between devices: 155 us -> 179 us  [swap(): return lax.ppermute(value, BOTH, [(i, i ^ mask) for i in range(self.all)])]
    ppermute x31 -> x44, starting transfers between devices: 28.8 us -> 47.7 us  [swap(): return lax.ppermute(value, BOTH, [(i, i ^ mask) for i in range(self.all)])]
    dot_general x14 -> x13, matrix products: 59.8 us -> 42.9 us  [dot(): return lax.dot_general(left, right, dims, preferred_element_type=f32)]
    pallas_call x2 -> x1, Pallas kernels: 34.7 us -> 19.5 us  [weight_grads(): pl.pallas_call(partial(grads_kernel, jobs), grid_spec=pltpu.PrefetchScala...]
    all_gather x1, waiting for transfers between devices: 22.9 us -> 11.1 us  [on_device(): packed = lax.all_gather(ffn_mine, BOTH, axis=0, tiled=False)]
    all_to_all x1 -> x2, waiting for transfers between devices: 6.32 us -> 16.6 us  [the longest x1 16.6 us: on_device(): lax.all_to_all(small_grad.reshape(parts, small_count, lot), BOTH, 0, 0, t...]
    unnamed x187 -> x227, local copies, waits for them, and re-layouts: 13.7 us -> 21.9 us
  transfers between devices with their start and end apart: 37 -> 50, of which waited for: 15 -> 20; matrix products, arithmetic and copies ran while one was open for 25% -> 27% of each run, Pallas kernels for 19% -> 17%
where the time goes in v4:
time: 624 us; the launch traced here: 615 us
  waiting for transfers between devices  208 us (33%)
  Pallas kernels  137 us (22%)
  other arithmetic  83.4 us (13%)
  local copies, waits for them, and re-layouts  69.5 us (11%)
  starting transfers between devices  57.2 us (9%)
  matrix products  42.9 us (7%)
  between operations  16.2 us (3%)
    ppermute x44, waiting for transfers between devices, swap(): return lax.ppermute(value, BOTH, [(i, i ^ mask) for i in range(self.all)])  179 us
    pallas_call x2, Pallas kernels, attend_back(): pl.pallas_call(partial(attend_back_kernel, masked), grid=(pairs, rows //...  51 us
    ppermute x44, starting transfers between devices, swap(): return lax.ppermute(value, BOTH, [(i, i ^ mask) for i in range(self.all)])  47.7 us
    dot_general x13, matrix products, dot(): return lax.dot_general(left, right, dims, preferred_element_type=f32)  42.9 us
    pallas_call x2, Pallas kernels, attend(): pl.pallas_call(partial(attend_kernel, masked), grid=(pairs, rows // tile)...  35.9 us
    pallas_call x1, Pallas kernels, feed_forward(): pl.pallas_call(block_kernel, grid_spec=pltpu.PrefetchScalarGridSpec(num_s...  30.8 us
    convert_element_type x8, other arithmetic, add(): return sum((t.astype(f32) for t in terms)).astype(bf16)  28.7 us
    unnamed x227, local copies, waits for them, and re-layouts  21.9 us
  transfers between devices with their start and end apart: 50, of which 20 were waited for; matrix products, arithmetic and copies ran while one was open for 27% of the time, Pallas kernels for 17%

profile of v4, /device:TPU:0, one launch (start us, length us, event | category | flops | bytes accessed | tf_op | source)
XLA Modules:
  0.0 614.6 jit_solution(12610175518610905243)
XLA Ops:
  28.9 30.1 %collective-permute-done.3 = bf16[4,40,768]{2,0,1:T(4,128)(2,1)} collective-permute-done((bf16[4,40,768]{2,0,1:T(4,128)(2,1)}, bf16[4,40,768]{2,0,1:T(4,128)(2,1)}, u32[]{:S(2)}, u32[]{:S(2)}) %collective-permute-start.3) | collective-permute-done | bytes 245792 | tf_op jit(solution)/shard_map/ppermute | solution.py:367
  62.3 3.4 concatenate.125
  67.8 4.8 collective-permute-start.8
  75.7 11.5 %collective-permute-done.4 = bf16[8,40,768]{2,0,1:T(8,128)(2,1)} collective-permute-done((bf16[8,40,768]{2,0,1:T(8,128)(2,1)}, bf16[8,40,768]{2,0,1:T(8,128)(2,1)}, u32[]{:S(2)}, u32[]{:S(2)}) %collective-permute-start.4) | collective-permute-done | bytes 491552 | tf_op jit(solution)/shard_map/ppermute | solution.py:367
  91.2 18.3 %collective-permute-done.8 = bf16[384,1024]{1,0:T(8,128)(2,1)} collective-permute-done((bf16[384,1024]{1,0:T(8,128)(2,1)}, bf16[384,1024]{1,0:T(8,128)(2,1)}, u32[]{:S(2)}, u32[]{:S(2)}) %collective-permute-start.8) | collective-permute-done | bytes 786464 | tf_op jit(solution)/shard_map/ppermute | solution.py:367
  115.1 17.4 %collective-permute-done.5 = bf16[16,40,768]{2,0,1:T(8,128)(2,1)} collective-permute-done((bf16[16,40,768]{2,0,1:T(8,128)(2,1)}, bf16[16,40,768]{2,0,1:T(8,128)(2,1)}, u32[]{:S(2)}, u32[]{:S(2)}) %collective-permute-start.5) | collective-permute-done | bytes 983072 | tf_op jit(solution)/shard_map/ppermute | solution.py:367
  146.2 3.5 convert_element_type.326
  151.2 4.6 convolution_convert_fusion.2
  171.4 18.0 %collective-permute-done.12 = bf16[256,768]{1,0:T(8,128)(2,1)S(1)} collective-permute-done((bf16[256,768]{1,0:T(8,128)(2,1)S(1)}, bf16[256,768]{1,0:T(8,128)(2,1)S(1)}, u32[]{:S(2)}, u32[]{:S(2)}) %collective-permute-start.12) | collective-permute-done | bytes 393248 | tf_op jit(solution)/shard_map/ppermute | solution.py:367
  195.8 21.0 %attend.2 = (bf16[1536,256]{1,0:T(8,128)(2,1)}, f32[2,1536,128]{2,1,0:T(8,128)}) custom-call(bf16[1536,256]{1,0:T(8,128)(2,1)} %multiply_convert_fusion.1.refs_0_, bf16[1536,512]{1,0:T(8,128)(2,1)} %slice.254.refs_1_), custom_call_target="tpu_custom_call" | custom-call | flops 9663676416 | bytes 3145728 | tf_op jit(solution)/shard_map/attend/pallas_call | solution.py:74
  216.8 17.1 %collective-permute-done.21 = bf16[192,1024]{1,0:T(8,128)(2,1)S(1)} collective-permute-done((bf16[192,1024]{1,0:T(8,128)(2,1)S(1)}, bf16[192,1024]{1,0:T(8,128)(2,1)S(1)}, u32[]{:S(2)}, u32[]{:S(2)}) %collective-permute-start.21) | collective-permute-done | bytes 393248 | tf_op jit(solution)/shard_map/ppermute | solution.py:367
  238.8 5.0 fusion.38
  246.3 6.5 %convolution_convert_fusion.1.refs_1_ = bf16[1024,2048]{1,0:T(8,128)(2,1)} fusion(bf16[1024,1024]{1,0:T(8,128)(2,1)S(1)} %add_convert_fusion.3.refs_6_, bf16[1024,1024]{1,0:T(8,128)(2,1)S(1)} %bitcast.247, bf16[1024,1024]{1,0:T(8,128)(2,1)S(1)} %bitcast.249), kind=kOutput, calls=%fused_computation.17 | convolution fusion | flops 4305453056 | bytes 10485760 | tf_op jit(solution)/shard_map/dot_general | solution.py:26
  252.9 7.7 %collective-permute-done.20 = bf16[384,256]{1,0:T(8,128)(2,1)S(1)} collective-permute-done((bf16[384,256]{1,0:T(8,128)(2,1)S(1)}, bf16[384,256]{1,0:T(8,128)(2,1)S(1)}, u32[]{:S(2)}, u32[]{:S(2)}) %collective-permute-start.20) | collective-permute-done | bytes 196640 | tf_op jit(solution)/shard_map/ppermute | solution.py:367
  266.9 15.0 %attend.3 = (bf16[384,1024]{1,0:T(8,128)(2,1)}, f32[8,384,128]{2,1,0:T(8,128)}) custom-call(bf16[384,1024]{1,0:T(8,128)(2,1)} %multiply_convert_fusion.refs_0_, bf16[1024,2048]{1,0:T(8,128)(2,1)} %convolution_convert_fusion.1.refs_1_, f32[1,1024]{1,0:T(1,128)} %compare_select_fusion.refs_2_.refs_5_), custom_call_target="tpu_custom_call" | custom-call | flops 6442450944 | bytes 5767168 | tf_op jit(solution)/shard_map/attend/pallas_call | solution.py:74
  285.1 11.1 %all-gather.7.cloned.1.call-done = bf16[8192,1024]{1,0:T(8,128)(2,1)} async-done(((bf16[256,1024]{1,0:T(8,128)(2,1)}), bf16[8192,1024]{1,0:T(8,128)(2,1)}) %all-gather.7.cloned.1.call-update) | async-done | bytes 16777232 | tf_op jit(solution)/shard_map/all_gather | solution.py:587
  296.3 30.8 %feed_forward.1 = (bf16[384,1024]{1,0:T(8,128)(2,1)}, f32[384,1024]{1,0:T(8,128)}, bf16[16,256,1024]{2,1,0:T(8,128)(2,1)}, bf16[16,256,1024]{2,1,0:T(8,128)(2,1)}, f32[8,1024]{1,0:T(8,128)}, /*index=5*/f32[1,4096]{1,0:T(1,128)}) custom-call(s32[1]{0:T(128)} %bitcast.10.core_ref, f32[384,1024]{1,0:T(8,128)} %convolution_add_fusion.third_ref, ...), custom_call_target="tpu_custom_call" | custom-call | flops 1 | bytes 1 | tf_op jit(solution)/shard_map/feed_forward/pallas_call | solution.py:254
  331.1 9.5 %collective-permute-done.22 = bf16[16,256,1024]{2,1,0:T(8,128)(2,1)S(1)} collective-permute-done((bf16[16,256,1024]{2,1,0:T(8,128)(2,1)}, bf16[16,256,1024]{2,1,0:T(8,128)(2,1)S(1)}, u32[]{:S(2)}, u32[]{:S(2)}) %collective-permute-start.22) | collective-permute-done | bytes 8388640 | tf_op jit(solution)/shard_map/ppermute | solution.py:367
  340.5 9.1 %add_convert_fusion = bf16[16,256,1024]{2,1,0:T(8,128)(2,1)} fusion(bf16[16,256,1024]{2,1,0:T(8,128)(2,1)S(1)} %collective-permute-done.22, bf16[16,256,1024]{2,1,0:T(8,128)(2,1)} %get-tuple-element.146), kind=kLoop, calls=%fused_computation | loop fusion | flops 16777216 | bytes 25165824 | tf_op jit(solution)/shard_map/convert_element_type | solution.py:450
  353.8 21.0 %attend_back.2 = (bf16[384,1024]{1,0:T(8,128)(2,1)}, bf16[1024,2048]{1,0:T(8,128)(2,1)}) custom-call(bf16[384,1024]{1,0:T(8,128)(2,1)} %multiply_convert_fusion.refs_0_, bf16[1024,2048]{1,0:T(8,128)(2,1)} %convolution_convert_fusion.1.refs_1_, bf16[384,1024]{1,0:T(8,128)(2,1)} %get-tuple-element.158.refs_2_.refs_0_, ...), custom_call_target="tpu_custom_call" | custom-call | flops 16106127360 | bytes 11534336 | tf_op jit(solution)/shard_map/attend_back/pallas_call | solution.py:144
  383.5 7.1 %fusion = (f32[1024]{0:T(1024)}, f32[1024]{0:T(1024)}, f32[1024]{0:T(1024)}, f32[1024]{0:T(1024)}, bf16[1024,1024]{1,0:T(8,128)(2,1)}) fusion(f32[1024]{0:T(1024)S(1)} %bitcast.318, f32[1024]{0:T(1024)S(1)} %bitcast.324, f32[1024]{0:T(1024)S(1)} %bitcast.322, f32[1024]{0:T(1024)S(1)} %bitcast.320, bf16[1024,2048]{1,0:T(8,128)(2,1)S(1)} %copy-done.8, ...), kind=kOutput, calls=%fused_computation.9 | convolution fusion | flops 4313837568 | bytes 10518528 | tf_op jit(solution)/shard_map/dot_general | solution.py:26
  392.6 19.5 %weight_grads.1 = (bf16[16,192,1024]{2,1,0:T(8,128)(2,1)}, bf16[16,192,1024]{2,1,0:T(8,128)(2,1)}) custom-call(s32[1]{0:T(128)} %bitcast.10.core_ref, bf16[384,1024]{1,0:T(8,128)(2,1)} %get-tuple-element.158.refs_2_.refs_0_, bf16[384,1024]{1,0:T(8,128)(2,1)} %copy-done.10, bf16[384,1024]{1,0:T(8,128)(2,1)} %copy-done.9, ...), custom_call_target="tpu_custom_call" | custom-call | flops 1 | bytes 1 | tf_op jit(solution)/shard_map/weight_grads/pallas_call | solution.py:342
  417.1 5.8 collective-permute-done.27
  423.3 10.9 %add_convert_fusion.1 = bf16[16,192,1024]{2,1,0:T(8,128)(2,1)} fusion(bf16[16,192,1024]{2,1,0:T(8,128)(2,1)} %collective-permute-done.27, bf16[16,192,1024]{2,1,0:T(8,128)(2,1)} %get-tuple-element.179), kind=kLoop, calls=%fused_computation.1 | loop fusion | flops 12582912 | bytes 18874368 | tf_op jit(solution)/shard_map/convert_element_type | solution.py:450
  443.1 4.6 all-to-all-start
  447.7 30.0 %attend_back.3 = (bf16[1536,256]{1,0:T(8,128)(2,1)}, bf16[1536,512]{1,0:T(8,128)(2,1)}) custom-call(bf16[1536,256]{1,0:T(8,128)(2,1)} %multiply_convert_fusion.1.refs_0_, bf16[1536,512]{1,0:T(8,128)(2,1)} %slice.254.refs_1_, bf16[1536,256]{1,0:T(8,128)(2,1)} %get-tuple-element.131.refs_2_, bf16[1536,256]{1,0:T(8,128)(2,1)} %pad_maximum_fusion.11.refs_3_, ...), custom_call_target="tpu_custom_call" | custom-call | flops 24159191040 | bytes 6291456 | tf_op jit(solution)/shard_map/attend_back/pallas_call | solution.py:144
  496.5 15.2 %collective-permute-done.35 = bf16[128,768]{1,0:T(8,128)(2,1)S(1)} collective-permute-done((bf16[128,768]{1,0:T(8,128)(2,1)S(1)}, bf16[128,768]{1,0:T(8,128)(2,1)S(1)}, u32[]{:S(2)}, u32[]{:S(2)}) %collective-permute-start.35) | collective-permute-done | bytes 196640 | tf_op jit(solution)/shard_map/ppermute | solution.py:367
  511.8 5.0 collective-permute-done.34
  516.8 7.6 %collective-permute-done.33 = bf16[16,32,768]{2,1,0:T(8,128)(2,1)} collective-permute-done((bf16[16,32,768]{2,1,0:T(8,128)(2,1)S(1)}, bf16[16,32,768]{2,1,0:T(8,128)(2,1)}, u32[]{:S(2)}, u32[]{:S(2)}) %collective-permute-start.33) | collective-permute-done | bytes 786464 | tf_op jit(solution)/shard_map/ppermute | solution.py:367
  549.2 12.8 %collective-permute-done.37 = bf16[192,1024]{1,0:T(8,128)(2,1)} collective-permute-done((bf16[192,1024]{1,0:T(8,128)(2,1)}, bf16[192,1024]{1,0:T(8,128)(2,1)}, u32[]{:S(2)}, u32[]{:S(2)}) %collective-permute-start.37) | collective-permute-done | bytes 393248 | tf_op jit(solution)/shard_map/ppermute | solution.py:367
  570.1 4.7 all-to-all-start.1
  578.9 16.6 %all-to-all-done.1 = bf16[32,2,768]{2,1,0:T(2,128)(2,1)} async-done(((bf16[32,2,768]{2,1,0:T(2,128)(2,1)}), bf16[32,2,768]{2,1,0:T(2,128)(2,1)}, u32[]{:S(2)}, u32[]{:S(2)}) %all-to-all-start.1) | async-done | bytes 98336 | tf_op jit(solution)/shard_map/all_to_all | solution.py:771
  (519 shorter events, 193.4 us)
Async XLA Ops:
  7.2 227.6 %all-gather.5.cloned.1.call-start = ((), (), s32[]{:S(2)}) async-start(), calls=%async_computation.4 | async-start | bytes 12976128 | tf_op jit(solution)/shard_map/all_gather | solution.py:578
  13.0 283.2 %all-gather.7.cloned.1.call-start = ((), (), s32[]{:S(2)}) async-start(), calls=%async_computation.5 | async-start | bytes 17301504 | tf_op jit(solution)/shard_map/all_gather | solution.py:587
  18.8 46.9 %collective-permute-start.6 = (bf16[192,1024]{1,0:T(8,128)(2,1)}, bf16[192,1024]{1,0:T(8,128)(2,1)}, u32[]{:S(2)}, u32[]{:S(2)}) collective-permute-start(bf16[192,1024]{1,0:T(8,128)(2,1)} %dynamic-slice_bitcast_fusion.4), channel_id=1, source_target_pairs={{0,4},{1,5},{2,6},{3,7},{4,0},{5,1},{6,2},{7,3},{8,12},{9,13},{10,... | collective-permute-start | bytes 1179656 | tf_op jit(solution)/shard_map/ppermute | solution.py:367
  24.4 34.5 %collective-permute-start.3 = (bf16[4,40,768]{2,0,1:T(4,128)(2,1)}, bf16[4,40,768]{2,0,1:T(4,128)(2,1)}, u32[]{:S(2)}, u32[]{:S(2)}) collective-permute-start(bf16[4,40,768]{2,0,1:T(4,128)(2,1)} %pad_maximum_fusion.16), channel_id=1, source_target_pairs={{0,4},{1,5},{2,6},{3,7},{4,0},{5,1},{6,2},{7,3},{8,12},{9,13},{10,... | collective-permute-start | bytes 737288 | tf_op jit(solution)/shard_map/ppermute | solution.py:367
  67.8 41.7 %collective-permute-start.8 = (bf16[384,1024]{1,0:T(8,128)(2,1)}, bf16[384,1024]{1,0:T(8,128)(2,1)}, u32[]{:S(2)}, u32[]{:S(2)}) collective-permute-start(bf16[384,1024]{1,0:T(8,128)(2,1)} %pad_maximum_fusion.5), channel_id=1, source_target_pairs={{0,2},{1,3},{2,0},{3,1},{4,6},{5,7},{6,4},{7,5},{8,10},{9,11},{10,... | collective-permute-start | bytes 2359304 | tf_op jit(solution)/shard_map/ppermute | solution.py:367
  75.7 35.8 %collective-permute-start.7 = (bf16[384,1024]{1,0:T(8,128)(2,1)}, bf16[384,1024]{1,0:T(8,128)(2,1)}, u32[]{:S(2)}, u32[]{:S(2)}) collective-permute-start(bf16[384,1024]{1,0:T(8,128)(2,1)} %pad_maximum_fusion.5), channel_id=1, source_target_pairs={{0,1},{1,0},{2,3},{3,2},{4,5},{5,4},{6,7},{7,6},{8,9},{9,8},{10,11... | collective-permute-start | bytes 2359304 | tf_op jit(solution)/shard_map/ppermute | solution.py:367
  90.4 42.1 %collective-permute-start.5 = (bf16[16,40,768]{2,0,1:T(8,128)(2,1)}, bf16[16,40,768]{2,0,1:T(8,128)(2,1)}, u32[]{:S(2)}, u32[]{:S(2)}) collective-permute-start(bf16[16,40,768]{2,0,1:T(8,128)(2,1)} %maximum_select_fusion.1), channel_id=1, source_target_pairs={{0,16},{1,17},{2,18},{3,19},{4,20},{5,21},{6,22},{7,23},{8,24},{9,... | collective-permute-start | bytes 2949128 | tf_op jit(solution)/shard_map/ppermute | solution.py:367
  132.5 303.5 %reduce-scatter.7.cloned.1.call-start = ((), (), s32[]{:S(2)}) async-start(), calls=%async_computation.6 | async-start | bytes 10485760
  135.1 30.7 %collective-permute-start.14 = (s32[128]{0:T(128)}, s32[128]{0:T(128)}, u32[]{:S(2)}, u32[]{:S(2)}) collective-permute-start(s32[128]{0:T(128)} %fusion.32), channel_id=1, source_target_pairs={{0,4},{1,5},{2,6},{3,7},{4,0},{5,1},{6,2},{7,3},{8,12},{9,13},{10,... | collective-permute-start | bytes 1544 | tf_op jit(solution)/shard_map/ppermute | solution.py:367
  138.2 30.1 %collective-permute-start.10 = (bf16[128,768]{1,0:T(8,128)(2,1)}, bf16[128,768]{1,0:T(8,128)(2,1)}, u32[]{:S(2)}, u32[]{:S(2)}) collective-permute-start(bf16[128,768]{1,0:T(8,128)(2,1)} %dynamic-slice_bitcast_fusion.14), channel_id=1, source_target_pairs={{0,4},{1,5},{2,6},{3,7},{4,0},{5,1},{6,2},{7,3},{8,12},{9,13},{10,... | collective-permute-start | bytes 589832 | tf_op jit(solution)/shard_map/ppermute | solution.py:367
  169.3 20.1 %collective-permute-start.12 = (bf16[256,768]{1,0:T(8,128)(2,1)S(1)}, bf16[256,768]{1,0:T(8,128)(2,1)S(1)}, u32[]{:S(2)}, u32[]{:S(2)}) collective-permute-start(bf16[256,768]{1,0:T(8,128)(2,1)S(1)} %pad_maximum_fusion.13), channel_id=1, source_target_pairs={{0,2},{1,3},{2,0},{3,1},{4,6},{5,7},{6,4},{7,5},{8,10},{9,11},{10,... | collective-permute-start | bytes 1179656 | tf_op jit(solution)/shard_map/ppermute | solution.py:367
  170.3 20.7 %collective-permute-start.11 = (bf16[256,768]{1,0:T(8,128)(2,1)S(1)}, bf16[256,768]{1,0:T(8,128)(2,1)S(1)}, u32[]{:S(2)}, u32[]{:S(2)}) collective-permute-start(bf16[256,768]{1,0:T(8,128)(2,1)S(1)} %pad_maximum_fusion.13), channel_id=1, source_target_pairs={{0,1},{1,0},{2,3},{3,2},{4,5},{5,4},{6,7},{7,6},{8,9},{9,8},{10,11... | collective-permute-start | bytes 1179656 | tf_op jit(solution)/shard_map/ppermute | solution.py:367
  193.5 40.4 %collective-permute-start.21 = (bf16[192,1024]{1,0:T(8,128)(2,1)S(1)}, bf16[192,1024]{1,0:T(8,128)(2,1)S(1)}, u32[]{:S(2)}, u32[]{:S(2)}) collective-permute-start(bf16[192,1024]{1,0:T(8,128)(2,1)S(1)} %get-tuple-element.283), channel_id=1, source_target_pairs={{0,4},{1,5},{2,6},{3,7},{4,0},{5,1},{6,2},{7,3},{8,12},{9,13},{10,... | collective-permute-start | bytes 1179656 | tf_op jit(solution)/shard_map/ppermute | solution.py:367
  236.9 16.0 %collective-permute-start.18 = (bf16[384,256]{1,0:T(8,128)(2,1)S(1)}, bf16[384,256]{1,0:T(8,128)(2,1)S(1)}, u32[]{:S(2)}, u32[]{:S(2)}) collective-permute-start(bf16[384,256]{1,0:T(8,128)(2,1)S(1)} %get-tuple-element.290), channel_id=1, source_target_pairs={{0,1},{1,0},{2,3},{3,2},{4,5},{5,4},{6,7},{7,6},{8,9},{9,8},{10,11... | collective-permute-start | bytes 589832 | tf_op jit(solution)/shard_map/ppermute | solution.py:367
  237.0 15.8 %collective-permute-start.19 = (bf16[384,256]{1,0:T(8,128)(2,1)S(1)}, bf16[384,256]{1,0:T(8,128)(2,1)S(1)}, u32[]{:S(2)}, u32[]{:S(2)}) collective-permute-start(bf16[384,256]{1,0:T(8,128)(2,1)S(1)} %get-tuple-element.289), channel_id=1, source_target_pairs={{0,2},{1,3},{2,0},{3,1},{4,6},{5,7},{6,4},{7,5},{8,10},{9,11},{10,... | collective-permute-start | bytes 589832 | tf_op jit(solution)/shard_map/ppermute | solution.py:367
  237.0 23.5 %collective-permute-start.20 = (bf16[384,256]{1,0:T(8,128)(2,1)S(1)}, bf16[384,256]{1,0:T(8,128)(2,1)S(1)}, u32[]{:S(2)}, u32[]{:S(2)}) collective-permute-start(bf16[384,256]{1,0:T(8,128)(2,1)S(1)} %get-tuple-element.288), channel_id=1, source_target_pairs={{0,3},{1,2},{2,1},{3,0},{4,7},{5,6},{6,5},{7,4},{8,11},{9,10},{10,... | collective-permute-start | bytes 589832 | tf_op jit(solution)/shard_map/ppermute | solution.py:367
  327.1 13.4 %collective-permute-start.22 = (bf16[16,256,1024]{2,1,0:T(8,128)(2,1)}, bf16[16,256,1024]{2,1,0:T(8,128)(2,1)S(1)}, u32[]{:S(2)}, u32[]{:S(2)}) collective-permute-start(bf16[16,256,1024]{2,1,0:T(8,128)(2,1)} %get-tuple-element.147), channel_id=1, source_target_pairs={{0,1},{1,0},{2,3},{3,2},{4,5},{5,4},{6,7},{7,6},{8,9},{9,8},{10,11... | collective-permute-start | bytes 25165832 | tf_op jit(solution)/shard_map/ppermute | solution.py:367
  349.6 183.2 %reduce-scatter.9.cloned.1.call-start = ((), (), s32[]{:S(2)}) async-start(), calls=%async_computation.7 | async-start | bytes 7864320
  352.6 22.2 %collective-permute-start.23 = (bf16[192,1024]{1,0:T(8,128)(2,1)S(1)}, bf16[192,1024]{1,0:T(8,128)(2,1)S(1)}, u32[]{:S(2)}, u32[]{:S(2)}) collective-permute-start(bf16[192,1024]{1,0:T(8,128)(2,1)S(1)} %get-tuple-element.277), channel_id=1, source_target_pairs={{0,4},{1,5},{2,6},{3,7},{4,0},{5,1},{6,2},{7,3},{8,12},{9,13},{10,... | collective-permute-start | bytes 1179656 | tf_op jit(solution)/shard_map/ppermute | solution.py:367
  390.7 21.5 %collective-permute-start.24 = (bf16[384,256]{1,0:T(8,128)(2,1)S(1)}, bf16[384,256]{1,0:T(8,128)(2,1)S(1)}, u32[]{:S(2)}, u32[]{:S(2)}) collective-permute-start(bf16[384,256]{1,0:T(8,128)(2,1)S(1)} %get-tuple-element.280), channel_id=1, source_target_pairs={{0,1},{1,0},{2,3},{3,2},{4,5},{5,4},{6,7},{7,6},{8,9},{9,8},{10,11... | collective-permute-start | bytes 589832 | tf_op jit(solution)/shard_map/ppermute | solution.py:367
  390.8 21.4 %collective-permute-start.25 = (bf16[384,256]{1,0:T(8,128)(2,1)S(1)}, bf16[384,256]{1,0:T(8,128)(2,1)S(1)}, u32[]{:S(2)}, u32[]{:S(2)}) collective-permute-start(bf16[384,256]{1,0:T(8,128)(2,1)S(1)} %get-tuple-element.279), channel_id=1, source_target_pairs={{0,2},{1,3},{2,0},{3,1},{4,6},{5,7},{6,4},{7,5},{8,10},{9,11},{10,... | collective-permute-start | bytes 589832 | tf_op jit(solution)/shard_map/ppermute | solution.py:367
  392.4 19.8 %collective-permute-start.26 = (bf16[384,256]{1,0:T(8,128)(2,1)S(1)}, bf16[384,256]{1,0:T(8,128)(2,1)S(1)}, u32[]{:S(2)}, u32[]{:S(2)}) collective-permute-start(bf16[384,256]{1,0:T(8,128)(2,1)S(1)} %get-tuple-element.278), channel_id=1, source_target_pairs={{0,3},{1,2},{2,1},{3,0},{4,7},{5,6},{6,5},{7,4},{8,11},{9,10},{10,... | collective-permute-start | bytes 589832 | tf_op jit(solution)/shard_map/ppermute | solution.py:367
  441.6 36.1 %collective-permute-start.30 = (bf16[256,768]{1,0:T(8,128)(2,1)}, bf16[256,768]{1,0:T(8,128)(2,1)}, u32[]{:S(2)}, u32[]{:S(2)}) collective-permute-start(bf16[256,768]{1,0:T(8,128)(2,1)} %add_convert_fusion.10), channel_id=1, source_target_pairs={{0,2},{1,3},{2,0},{3,1},{4,6},{5,7},{6,4},{7,5},{8,10},{9,11},{10,... | collective-permute-start | bytes 1179656 | tf_op jit(solution)/shard_map/ppermute | solution.py:367
  443.1 89.8 %all-to-all-start = ((bf16[4,256,1024]{2,1,0:T(8,128)(2,1)}), bf16[4,256,1024]{2,1,0:T(8,128)(2,1)}, u32[]{:S(2)}, u32[]{:S(2)}) async-start(bf16[4,256,1024]{2,1,0:T(8,128)(2,1)} %bitcast.257), calls=%async_computation | async-start | bytes 4194304 | tf_op jit(solution)/shard_map/all_to_all | solution.py:419
  488.6 28.1 %collective-permute-start.34 = (bf16[384,1024]{1,0:T(8,128)(2,1)S(1)}, bf16[384,1024]{1,0:T(8,128)(2,1)S(1)}, u32[]{:S(2)}, u32[]{:S(2)}) collective-permute-start(bf16[384,1024]{1,0:T(8,128)(2,1)S(1)} %add_convert_fusion.5), channel_id=1, source_target_pairs={{0,2},{1,3},{2,0},{3,1},{4,6},{5,7},{6,4},{7,5},{8,10},{9,11},{10,... | collective-permute-start | bytes 2359304 | tf_op jit(solution)/shard_map/ppermute | solution.py:367
  490.7 33.7 %collective-permute-start.33 = (bf16[16,32,768]{2,1,0:T(8,128)(2,1)S(1)}, bf16[16,32,768]{2,1,0:T(8,128)(2,1)}, u32[]{:S(2)}, u32[]{:S(2)}) collective-permute-start(bf16[16,32,768]{2,1,0:T(8,128)(2,1)S(1)} %get-tuple-element.264), channel_id=1, source_target_pairs={{0,16},{1,17},{2,18},{3,19},{4,20},{5,21},{6,22},{7,23},{8,24},{9,... | collective-permute-start | bytes 2359304 | tf_op jit(solution)/shard_map/ppermute | solution.py:367
  494.0 17.8 %collective-permute-start.35 = (bf16[128,768]{1,0:T(8,128)(2,1)S(1)}, bf16[128,768]{1,0:T(8,128)(2,1)S(1)}, u32[]{:S(2)}, u32[]{:S(2)}) collective-permute-start(bf16[128,768]{1,0:T(8,128)(2,1)S(1)} %get-tuple-element.301), channel_id=1, source_target_pairs={{0,4},{1,5},{2,6},{3,7},{4,0},{5,1},{6,2},{7,3},{8,12},{9,13},{10,... | collective-permute-start | bytes 589832 | tf_op jit(solution)/shard_map/ppermute | solution.py:367
  535.0 27.9 %collective-permute-start.38 = (bf16[2,192,1024]{2,1,0:T(8,128)(2,1)}, bf16[2,192,1024]{2,1,0:T(8,128)(2,1)}, u32[]{:S(2)}, u32[]{:S(2)}) collective-permute-start(bf16[2,192,1024]{2,1,0:T(8,128)(2,1)} %dynamic-slice_bitcast_fusion), channel_id=1, source_target_pairs={{0,2},{1,3},{2,0},{3,1},{4,6},{5,7},{6,4},{7,5},{8,10},{9,11},{10,... | collective-permute-start | bytes 2359304 | tf_op jit(solution)/shard_map/ppermute | solution.py:367
  540.7 21.2 %collective-permute-start.37 = (bf16[192,1024]{1,0:T(8,128)(2,1)}, bf16[192,1024]{1,0:T(8,128)(2,1)}, u32[]{:S(2)}, u32[]{:S(2)}) collective-permute-start(bf16[192,1024]{1,0:T(8,128)(2,1)} %get-tuple-element.275), channel_id=1, source_target_pairs={{0,4},{1,5},{2,6},{3,7},{4,0},{5,1},{6,2},{7,3},{8,12},{9,13},{10,... | collective-permute-start | bytes 1179656 | tf_op jit(solution)/shard_map/ppermute | solution.py:367
  564.8 30.7 %collective-permute-start.40 = (bf16[1,192,1024]{2,1,0:T(8,128)(2,1)}, bf16[1,192,1024]{2,1,0:T(8,128)(2,1)}, u32[]{:S(2)}, u32[]{:S(2)}) collective-permute-start(bf16[1,192,1024]{2,1,0:T(8,128)(2,1)} %fusion.18), channel_id=1, source_target_pairs={{0,4},{1,5},{2,6},{3,7},{4,0},{5,1},{6,2},{7,3},{8,12},{9,13},{10,... | collective-permute-start | bytes 1179656 | tf_op jit(solution)/shard_map/ppermute | solution.py:367
  568.9 26.6 %collective-permute-start.39 = (bf16[4,32,768]{2,1,0:T(8,128)(2,1)}, bf16[4,32,768]{2,1,0:T(8,128)(2,1)}, u32[]{:S(2)}, u32[]{:S(2)}) collective-permute-start(bf16[4,32,768]{2,1,0:T(8,128)(2,1)} %fusion.21), channel_id=1, source_target_pairs={{0,4},{1,5},{2,6},{3,7},{4,0},{5,1},{6,2},{7,3},{8,12},{9,13},{10,... | collective-permute-start | bytes 589832 | tf_op jit(solution)/shard_map/ppermute | solution.py:367
  570.1 25.4 %all-to-all-start.1 = ((bf16[32,2,768]{2,1,0:T(2,128)(2,1)}), bf16[32,2,768]{2,1,0:T(2,128)(2,1)}, u32[]{:S(2)}, u32[]{:S(2)}) async-start(bf16[32,2,768]{2,1,0:T(2,128)(2,1)} %reshape.474), calls=%async_computation.1 | async-start | bytes 196608 | tf_op jit(solution)/shard_map/all_to_all | solution.py:771
  (120 other events, 1131.3 us)
Sparse Core Ops, SparseCore 0:
  13.1 133.7 all-gather.4
  150.5 145.7 all-gather.6
  349.8 86.1 reduce-scatter.6
  439.1 84.1 reduce-scatter.8

commit v5 on v4

--- a/solution.py
+++ b/solution.py
@@ -564,6 +564,8 @@
     patch_room = -(-patch_rows // shard) * shard
     first = jnp.concatenate(
         [
+            stack_columns(low(up_weight), width),
+            low(down_weight),
             low(self_output),
             low(cross_query),
             low(cross_output),
@@ -576,15 +578,11 @@
     blocks = next(own_gather)
     tokens_all = jnp.concatenate(grid.gather_group(compact(tokens)), 0)
     first = lax.all_gather(first, BOTH, axis=0, tiled=False)
-    ffn_mine = jnp.concatenate([stack_columns(low(up_weight), width), low(down_weight)], 0)
     while isinstance(blocks, list) or blocks.shape[0] < parts:
         blocks = own_gather.send(blocks)
         if isinstance(blocks, list) or blocks.shape[0] == parts // 2:
             break
-    blocks, tokens_all, ffn_mine, patches, patch_index = together(
-        (blocks, tokens_all, ffn_mine, patches, patch_index)
-    )
-    packed = lax.all_gather(ffn_mine, BOTH, axis=0, tiled=False)
+    blocks, tokens_all, patches, patch_index = together((blocks, tokens_all, patches, patch_index))
     feats_all = jnp.concatenate(grid.gather_group(compact(patches)), 0)
     views_all = jnp.concatenate(grid.gather_group(compact(patch_index)), 0) // VIEW_PATCHES
     blocks = own_gather.send(blocks)
@@ -617,7 +615,10 @@
     cot = compact(cotangent)
     attended = grid.exchange(jnp.stack(grid.in_order(chunks(attended_own))))
 
+    packed = first
+
     def square(start, rows=shard):
+        start += 2 * down_weight.shape[0]
         return first[:, start : start + rows].reshape(parts * rows, width)
 
     full_out = square(0)

time: 624 us -> 613 us (0.982)
  starting transfers between devices: 57.2 us -> 47.7 us
    ppermute x44, waiting for transfers between devices: 179 us -> 196 us  [swap(): return lax.ppermute(value, BOTH, [(i, i ^ mask) for i in range(self.all)])]
    all_gather x1 -> x0, waiting for transfers between devices: 11.1 us -> none  [on_device(): packed = lax.all_gather(ffn_mine, BOTH, axis=0, tiled=False)]
    ppermute x44, starting transfers between devices: 47.7 us -> 38.3 us  [swap(): return lax.ppermute(value, BOTH, [(i, i ^ mask) for i in range(self.all)])]
    unnamed x227 -> x224, local copies, waits for them, and re-layouts: 21.9 us -> 22.6 us
  transfers between devices with their start and end apart: 50 -> 49, of which waited for: 20 -> 19; matrix products, arithmetic and copies ran while one was open for 27% -> 24% of each run, Pallas kernels for 17% -> 15%
where the time goes in v5:
time: 613 us; the launch traced here: 607 us
  waiting for transfers between devices  212 us (35%)
  Pallas kernels  138 us (23%)
  other arithmetic  79.5 us (13%)
  local copies, waits for them, and re-layouts  71.1 us (12%)
  starting transfers between devices  47.7 us (8%)
  matrix products  43.2 us (7%)
  between operations  15.9 us (3%)
    ppermute x44, waiting for transfers between devices, swap(): return lax.ppermute(value, BOTH, [(i, i ^ mask) for i in range(self.all)])  196 us
    pallas_call x2, Pallas kernels, attend_back(): pl.pallas_call(partial(attend_back_kernel, masked), grid=(pairs, rows //...  50.7 us
    dot_general x13, matrix products, dot(): return lax.dot_general(left, right, dims, preferred_element_type=f32)  43.2 us
    ppermute x44, starting transfers between devices, swap(): return lax.ppermute(value, BOTH, [(i, i ^ mask) for i in range(self.all)])  38.3 us
    pallas_call x2, Pallas kernels, attend(): pl.pallas_call(partial(attend_kernel, masked), grid=(pairs, rows // tile)...  36 us
    pallas_call x1, Pallas kernels, feed_forward(): pl.pallas_call(block_kernel, grid_spec=pltpu.PrefetchScalarGridSpec(num_s...  31.3 us
    convert_element_type x8, other arithmetic, add(): return sum((t.astype(f32) for t in terms)).astype(bf16)  28.5 us
    unnamed x224, local copies, waits for them, and re-layouts  22.6 us
  transfers between devices with their start and end apart: 49, of which 19 were waited for; matrix products, arithmetic and copies ran while one was open for 24% of the time, Pallas kernels for 15%

profile of v5, /device:TPU:0, one launch (start us, length us, event | category | flops | bytes accessed | tf_op | source)
XLA Modules:
  0.0 607.4 jit_solution(4018087934903598691)
XLA Ops:
  28.6 31.8 %collective-permute-done.3 = bf16[4,40,768]{2,0,1:T(4,128)(2,1)} collective-permute-done((bf16[4,40,768]{2,0,1:T(4,128)(2,1)}, bf16[4,40,768]{2,0,1:T(4,128)(2,1)}, u32[]{:S(2)}, u32[]{:S(2)}) %collective-permute-start.3) | collective-permute-done | bytes 245792 | tf_op jit(solution)/shard_map/ppermute | solution.py:367
  60.4 3.5 concatenate.123
  63.9 3.4 concatenate.122
  70.3 3.7 collective-permute-done.6
  76.4 12.0 %collective-permute-done.4 = bf16[8,40,768]{2,0,1:T(8,128)(2,1)} collective-permute-done((bf16[8,40,768]{2,0,1:T(8,128)(2,1)}, bf16[8,40,768]{2,0,1:T(8,128)(2,1)}, u32[]{:S(2)}, u32[]{:S(2)}) %collective-permute-start.4) | collective-permute-done | bytes 491552 | tf_op jit(solution)/shard_map/ppermute | solution.py:367
  93.0 38.5 %collective-permute-done.8 = bf16[384,1024]{1,0:T(8,128)(2,1)} collective-permute-done((bf16[384,1024]{1,0:T(8,128)(2,1)}, bf16[384,1024]{1,0:T(8,128)(2,1)}, u32[]{:S(2)}, u32[]{:S(2)}) %collective-permute-start.8) | collective-permute-done | bytes 786464 | tf_op jit(solution)/shard_map/ppermute | solution.py:367
  140.5 3.9 maximum_select_fusion
  149.0 3.4 convert_element_type.324
  154.0 4.4 convolution_convert_fusion.2
  174.1 41.3 %collective-permute-done.12 = bf16[256,768]{1,0:T(8,128)(2,1)S(1)} collective-permute-done((bf16[256,768]{1,0:T(8,128)(2,1)S(1)}, bf16[256,768]{1,0:T(8,128)(2,1)S(1)}, u32[]{:S(2)}, u32[]{:S(2)}) %collective-permute-start.12) | collective-permute-done | bytes 393248 | tf_op jit(solution)/shard_map/ppermute | solution.py:367
  219.6 20.9 %attend.2 = (bf16[1536,256]{1,0:T(8,128)(2,1)}, f32[2,1536,128]{2,1,0:T(8,128)}) custom-call(bf16[1536,256]{1,0:T(8,128)(2,1)} %multiply_convert_fusion.1.refs_0_, bf16[1536,512]{1,0:T(8,128)(2,1)} %slice.254.refs_1_), custom_call_target="tpu_custom_call" | custom-call | flops 9663676416 | bytes 3145728 | tf_op jit(solution)/shard_map/attend/pallas_call | solution.py:74
  240.6 5.2 collective-permute-done.21
  248.3 6.5 %fusion.38 = (bf16[32,32,1024]{2,1,0:T(8,128)(2,1)}, bf16[32,32,1024]{2,1,0:T(8,128)(2,1)S(1)}, bf16[32,32,1024]{2,1,0:T(8,128)(2,1)S(1)}, bf16[32,32,1024]{2,1,0:T(8,128)(2,1)S(1)}, bf16[32,32,1024]{2,1,0:T(8,128)(2,1)S(1)}) fusion(bf16[32,448,1024]{2,1,0:T(8,128)(2,1)} %bitcast.239), kind=kLoop, calls=%fused_computation.247 | loop fusion | bytes 20971520 | tf_op jit(solution)/shard_map/slice | solution.py:622
  260.0 6.2 %convolution_convert_fusion.1.refs_1_ = bf16[1024,2048]{1,0:T(8,128)(2,1)} fusion(bf16[1024,1024]{1,0:T(8,128)(2,1)S(1)} %add_convert_fusion.3.refs_6_, bf16[1024,1024]{1,0:T(8,128)(2,1)S(1)} %bitcast.246, bf16[1024,1024]{1,0:T(8,128)(2,1)S(1)} %bitcast.248), kind=kOutput, calls=%fused_computation.17 | convolution fusion | flops 4305453056 | bytes 10485760 | tf_op jit(solution)/shard_map/dot_general | solution.py:26
  271.9 15.1 %attend.3 = (bf16[384,1024]{1,0:T(8,128)(2,1)}, f32[8,384,128]{2,1,0:T(8,128)}) custom-call(bf16[384,1024]{1,0:T(8,128)(2,1)} %multiply_convert_fusion.refs_0_, bf16[1024,2048]{1,0:T(8,128)(2,1)} %convolution_convert_fusion.1.refs_1_, f32[1,1024]{1,0:T(1,128)} %compare_select_fusion.refs_2_.refs_5_), custom_call_target="tpu_custom_call" | custom-call | flops 6442450944 | bytes 5767168 | tf_op jit(solution)/shard_map/attend/pallas_call | solution.py:74
  290.3 31.3 %feed_forward.1 = (bf16[384,1024]{1,0:T(8,128)(2,1)}, f32[384,1024]{1,0:T(8,128)}, bf16[16,256,1024]{2,1,0:T(8,128)(2,1)}, bf16[16,256,1024]{2,1,0:T(8,128)(2,1)}, f32[8,1024]{1,0:T(8,128)}, /*index=5*/f32[1,4096]{1,0:T(1,128)}) custom-call(s32[1]{0:T(128)} %bitcast.8.core_ref, f32[384,1024]{1,0:T(8,128)} %convolution_add_fusion.third_ref, ...), custom_call_target="tpu_custom_call" | custom-call | flops 1 | bytes 1 | tf_op jit(solution)/shard_map/feed_forward/pallas_call | solution.py:254
  325.4 9.6 %collective-permute-done.22 = bf16[16,256,1024]{2,1,0:T(8,128)(2,1)S(1)} collective-permute-done((bf16[16,256,1024]{2,1,0:T(8,128)(2,1)}, bf16[16,256,1024]{2,1,0:T(8,128)(2,1)S(1)}, u32[]{:S(2)}, u32[]{:S(2)}) %collective-permute-start.22) | collective-permute-done | bytes 8388640 | tf_op jit(solution)/shard_map/ppermute | solution.py:367
  335.0 9.1 %add_convert_fusion = bf16[16,256,1024]{2,1,0:T(8,128)(2,1)} fusion(bf16[16,256,1024]{2,1,0:T(8,128)(2,1)S(1)} %collective-permute-done.22, bf16[16,256,1024]{2,1,0:T(8,128)(2,1)} %get-tuple-element.144), kind=kLoop, calls=%fused_computation | loop fusion | flops 16777216 | bytes 25165824 | tf_op jit(solution)/shard_map/convert_element_type | solution.py:450
  348.2 20.7 %attend_back.2 = (bf16[384,1024]{1,0:T(8,128)(2,1)}, bf16[1024,2048]{1,0:T(8,128)(2,1)}) custom-call(bf16[384,1024]{1,0:T(8,128)(2,1)} %multiply_convert_fusion.refs_0_, bf16[1024,2048]{1,0:T(8,128)(2,1)} %convolution_convert_fusion.1.refs_1_, bf16[384,1024]{1,0:T(8,128)(2,1)} %get-tuple-element.156.refs_2_.refs_0_, ...), custom_call_target="tpu_custom_call" | custom-call | flops 16106127360 | bytes 11534336 | tf_op jit(solution)/shard_map/attend_back/pallas_call | solution.py:144
  369.7 4.2 multiply_reduce_fusion.1
  379.2 7.1 %fusion = (f32[1024]{0:T(1024)}, f32[1024]{0:T(1024)}, f32[1024]{0:T(1024)}, f32[1024]{0:T(1024)}, bf16[1024,1024]{1,0:T(8,128)(2,1)}) fusion(f32[1024]{0:T(1024)S(1)} %bitcast.317, f32[1024]{0:T(1024)S(1)} %bitcast.323, f32[1024]{0:T(1024)S(1)} %bitcast.321, f32[1024]{0:T(1024)S(1)} %bitcast.319, bf16[1024,2048]{1,0:T(8,128)(2,1)S(1)} %copy-done.8, ...), kind=kOutput, calls=%fused_computation.9 | convolution fusion | flops 4313837568 | bytes 10518528 | tf_op jit(solution)/shard_map/dot_general | solution.py:26
  388.3 19.6 %weight_grads.1 = (bf16[16,192,1024]{2,1,0:T(8,128)(2,1)}, bf16[16,192,1024]{2,1,0:T(8,128)(2,1)}) custom-call(s32[1]{0:T(128)} %bitcast.8.core_ref, bf16[384,1024]{1,0:T(8,128)(2,1)} %get-tuple-element.156.refs_2_.refs_0_, bf16[384,1024]{1,0:T(8,128)(2,1)} %copy-done.10, bf16[384,1024]{1,0:T(8,128)(2,1)} %copy-done.9, ...), custom_call_target="tpu_custom_call" | custom-call | flops 1 | bytes 1 | tf_op jit(solution)/shard_map/weight_grads/pallas_call | solution.py:342
  412.7 6.0 collective-permute-done.27
  419.3 10.7 %add_convert_fusion.1 = bf16[16,192,1024]{2,1,0:T(8,128)(2,1)} fusion(bf16[16,192,1024]{2,1,0:T(8,128)(2,1)} %collective-permute-done.27, bf16[16,192,1024]{2,1,0:T(8,128)(2,1)} %get-tuple-element.177), kind=kLoop, calls=%fused_computation.1 | loop fusion | flops 12582912 | bytes 18874368 | tf_op jit(solution)/shard_map/convert_element_type | solution.py:450
  437.1 4.6 all-to-all-start
  441.7 30.0 %attend_back.3 = (bf16[1536,256]{1,0:T(8,128)(2,1)}, bf16[1536,512]{1,0:T(8,128)(2,1)}) custom-call(bf16[1536,256]{1,0:T(8,128)(2,1)} %multiply_convert_fusion.1.refs_0_, bf16[1536,512]{1,0:T(8,128)(2,1)} %slice.254.refs_1_, bf16[1536,256]{1,0:T(8,128)(2,1)} %get-tuple-element.130.refs_2_, bf16[1536,256]{1,0:T(8,128)(2,1)} %pad_maximum_fusion.11.refs_3_, ...), custom_call_target="tpu_custom_call" | custom-call | flops 24159191040 | bytes 6291456 | tf_op jit(solution)/shard_map/attend_back/pallas_call | solution.py:144
  491.0 14.8 %collective-permute-done.35 = bf16[128,768]{1,0:T(8,128)(2,1)S(1)} collective-permute-done((bf16[128,768]{1,0:T(8,128)(2,1)S(1)}, bf16[128,768]{1,0:T(8,128)(2,1)S(1)}, u32[]{:S(2)}, u32[]{:S(2)}) %collective-permute-start.35) | collective-permute-done | bytes 196640 | tf_op jit(solution)/shard_map/ppermute | solution.py:367
  505.8 5.6 collective-permute-done.34
  511.4 6.8 %collective-permute-done.33 = bf16[16,32,768]{2,1,0:T(8,128)(2,1)} collective-permute-done((bf16[16,32,768]{2,1,0:T(8,128)(2,1)S(1)}, bf16[16,32,768]{2,1,0:T(8,128)(2,1)}, u32[]{:S(2)}, u32[]{:S(2)}) %collective-permute-start.33) | collective-permute-done | bytes 786464 | tf_op jit(solution)/shard_map/ppermute | solution.py:367
  543.2 12.8 %collective-permute-done.37 = bf16[192,1024]{1,0:T(8,128)(2,1)} collective-permute-done((bf16[192,1024]{1,0:T(8,128)(2,1)}, bf16[192,1024]{1,0:T(8,128)(2,1)}, u32[]{:S(2)}, u32[]{:S(2)}) %collective-permute-start.37) | collective-permute-done | bytes 393248 | tf_op jit(solution)/shard_map/ppermute | solution.py:367
  564.1 4.6 all-to-all-start.1
  572.6 16.8 %all-to-all-done.1 = bf16[32,2,768]{2,1,0:T(2,128)(2,1)S(1)} async-done(((bf16[32,2,768]{2,1,0:T(2,128)(2,1)}), bf16[32,2,768]{2,1,0:T(2,128)(2,1)S(1)}, u32[]{:S(2)}, u32[]{:S(2)}) %all-to-all-start.1) | async-done | bytes 98336 | tf_op jit(solution)/shard_map/all_to_all | solution.py:772
  (512 shorter events, 177.3 us)
Async XLA Ops:
  7.2 239.5 %all-gather.3.cloned.1.call-start = ((), (), s32[]{:S(2)}) async-start(), calls=%async_computation.4 | async-start | bytes 30277632 | tf_op jit(solution)/shard_map/all_gather | solution.py:580
  11.0 419.8 %reduce-scatter.7.cloned.1.call-start = ((), (), s32[]{:S(2)}) async-start(), calls=%async_computation.5 | async-start | bytes 10485760
  23.0 37.4 %collective-permute-start.3 = (bf16[4,40,768]{2,0,1:T(4,128)(2,1)}, bf16[4,40,768]{2,0,1:T(4,128)(2,1)}, u32[]{:S(2)}, u32[]{:S(2)}) collective-permute-start(bf16[4,40,768]{2,0,1:T(4,128)(2,1)} %pad_maximum_fusion.15), channel_id=1, source_target_pairs={{0,4},{1,5},{2,6},{3,7},{4,0},{5,1},{6,2},{7,3},{8,12},{9,13},{10,... | collective-permute-start | bytes 737288 | tf_op jit(solution)/shard_map/ppermute | solution.py:367
  26.4 47.6 %collective-permute-start.6 = (bf16[192,1024]{1,0:T(8,128)(2,1)}, bf16[192,1024]{1,0:T(8,128)(2,1)}, u32[]{:S(2)}, u32[]{:S(2)}) collective-permute-start(bf16[192,1024]{1,0:T(8,128)(2,1)} %dynamic-slice_bitcast_fusion.4), channel_id=1, source_target_pairs={{0,4},{1,5},{2,6},{3,7},{4,0},{5,1},{6,2},{7,3},{8,12},{9,13},{10,... | collective-permute-start | bytes 1179656 | tf_op jit(solution)/shard_map/ppermute | solution.py:367
  69.2 19.2 %collective-permute-start.4 = (bf16[8,40,768]{2,0,1:T(8,128)(2,1)}, bf16[8,40,768]{2,0,1:T(8,128)(2,1)}, u32[]{:S(2)}, u32[]{:S(2)}) collective-permute-start(bf16[8,40,768]{2,0,1:T(8,128)(2,1)} %broadcast_select_fusion), channel_id=1, source_target_pairs={{0,8},{1,9},{2,10},{3,11},{4,12},{5,13},{6,14},{7,15},{8,0},{9,1},... | collective-permute-start | bytes 1474568 | tf_op jit(solution)/shard_map/ppermute | solution.py:367
  76.3 55.3 %collective-permute-start.8 = (bf16[384,1024]{1,0:T(8,128)(2,1)}, bf16[384,1024]{1,0:T(8,128)(2,1)}, u32[]{:S(2)}, u32[]{:S(2)}) collective-permute-start(bf16[384,1024]{1,0:T(8,128)(2,1)} %pad_maximum_fusion.5), channel_id=1, source_target_pairs={{0,2},{1,3},{2,0},{3,1},{4,6},{5,7},{6,4},{7,5},{8,10},{9,11},{10,... | collective-permute-start | bytes 2359304 | tf_op jit(solution)/shard_map/ppermute | solution.py:367
  76.3 57.5 %collective-permute-start.7 = (bf16[384,1024]{1,0:T(8,128)(2,1)}, bf16[384,1024]{1,0:T(8,128)(2,1)}, u32[]{:S(2)}, u32[]{:S(2)}) collective-permute-start(bf16[384,1024]{1,0:T(8,128)(2,1)} %pad_maximum_fusion.5), channel_id=1, source_target_pairs={{0,1},{1,0},{2,3},{3,2},{4,5},{5,4},{6,7},{7,6},{8,9},{9,8},{10,11... | collective-permute-start | bytes 2359304 | tf_op jit(solution)/shard_map/ppermute | solution.py:367
  91.2 45.2 %collective-permute-start.5 = (bf16[16,40,768]{2,0,1:T(8,128)(2,1)}, bf16[16,40,768]{2,0,1:T(8,128)(2,1)}, u32[]{:S(2)}, u32[]{:S(2)}) collective-permute-start(bf16[16,40,768]{2,0,1:T(8,128)(2,1)} %maximum_select_fusion.1), channel_id=1, source_target_pairs={{0,16},{1,17},{2,18},{3,19},{4,20},{5,21},{6,22},{7,23},{8,24},{9,... | collective-permute-start | bytes 2949128 | tf_op jit(solution)/shard_map/ppermute | solution.py:367
  136.9 31.6 %collective-permute-start.14 = (s32[128]{0:T(128)}, s32[128]{0:T(128)}, u32[]{:S(2)}, u32[]{:S(2)}) collective-permute-start(s32[128]{0:T(128)} %fusion.32), channel_id=1, source_target_pairs={{0,4},{1,5},{2,6},{3,7},{4,0},{5,1},{6,2},{7,3},{8,12},{9,13},{10,... | collective-permute-start | bytes 1544 | tf_op jit(solution)/shard_map/ppermute | solution.py:367
  137.6 31.7 %collective-permute-start.10 = (bf16[128,768]{1,0:T(8,128)(2,1)}, bf16[128,768]{1,0:T(8,128)(2,1)}, u32[]{:S(2)}, u32[]{:S(2)}) collective-permute-start(bf16[128,768]{1,0:T(8,128)(2,1)} %dynamic-slice_bitcast_fusion.14), channel_id=1, source_target_pairs={{0,4},{1,5},{2,6},{3,7},{4,0},{5,1},{6,2},{7,3},{8,12},{9,13},{10,... | collective-permute-start | bytes 589832 | tf_op jit(solution)/shard_map/ppermute | solution.py:367
  170.2 45.2 %collective-permute-start.12 = (bf16[256,768]{1,0:T(8,128)(2,1)S(1)}, bf16[256,768]{1,0:T(8,128)(2,1)S(1)}, u32[]{:S(2)}, u32[]{:S(2)}) collective-permute-start(bf16[256,768]{1,0:T(8,128)(2,1)S(1)} %pad_maximum_fusion.12), channel_id=1, source_target_pairs={{0,2},{1,3},{2,0},{3,1},{4,6},{5,7},{6,4},{7,5},{8,10},{9,11},{10,... | collective-permute-start | bytes 1179656 | tf_op jit(solution)/shard_map/ppermute | solution.py:367
  173.2 43.8 %collective-permute-start.11 = (bf16[256,768]{1,0:T(8,128)(2,1)S(1)}, bf16[256,768]{1,0:T(8,128)(2,1)S(1)}, u32[]{:S(2)}, u32[]{:S(2)}) collective-permute-start(bf16[256,768]{1,0:T(8,128)(2,1)S(1)} %pad_maximum_fusion.12), channel_id=1, source_target_pairs={{0,1},{1,0},{2,3},{3,2},{4,5},{5,4},{6,7},{7,6},{8,9},{9,8},{10,11... | collective-permute-start | bytes 1179656 | tf_op jit(solution)/shard_map/ppermute | solution.py:367
  219.5 26.3 %collective-permute-start.21 = (bf16[192,1024]{1,0:T(8,128)(2,1)S(1)}, bf16[192,1024]{1,0:T(8,128)(2,1)S(1)}, u32[]{:S(2)}, u32[]{:S(2)}) collective-permute-start(bf16[192,1024]{1,0:T(8,128)(2,1)S(1)} %get-tuple-element.281), channel_id=1, source_target_pairs={{0,4},{1,5},{2,6},{3,7},{4,0},{5,1},{6,2},{7,3},{8,12},{9,13},{10,... | collective-permute-start | bytes 1179656 | tf_op jit(solution)/shard_map/ppermute | solution.py:367
  255.5 11.0 %collective-permute-start.20 = (bf16[384,256]{1,0:T(8,128)(2,1)S(1)}, bf16[384,256]{1,0:T(8,128)(2,1)S(1)}, u32[]{:S(2)}, u32[]{:S(2)}) collective-permute-start(bf16[384,256]{1,0:T(8,128)(2,1)S(1)} %get-tuple-element.286), channel_id=1, source_target_pairs={{0,3},{1,2},{2,1},{3,0},{4,7},{5,6},{6,5},{7,4},{8,11},{9,10},{10,... | collective-permute-start | bytes 589832 | tf_op jit(solution)/shard_map/ppermute | solution.py:367
  321.6 13.4 %collective-permute-start.22 = (bf16[16,256,1024]{2,1,0:T(8,128)(2,1)}, bf16[16,256,1024]{2,1,0:T(8,128)(2,1)S(1)}, u32[]{:S(2)}, u32[]{:S(2)}) collective-permute-start(bf16[16,256,1024]{2,1,0:T(8,128)(2,1)} %get-tuple-element.145), channel_id=1, source_target_pairs={{0,1},{1,0},{2,3},{3,2},{4,5},{5,4},{6,7},{7,6},{8,9},{9,8},{10,11... | collective-permute-start | bytes 25165832 | tf_op jit(solution)/shard_map/ppermute | solution.py:367
  344.1 182.7 %reduce-scatter.9.cloned.1.call-start = ((), (), s32[]{:S(2)}) async-start(), calls=%async_computation.6 | async-start | bytes 7864320
  346.1 22.8 %collective-permute-start.23 = (bf16[192,1024]{1,0:T(8,128)(2,1)S(1)}, bf16[192,1024]{1,0:T(8,128)(2,1)S(1)}, u32[]{:S(2)}, u32[]{:S(2)}) collective-permute-start(bf16[192,1024]{1,0:T(8,128)(2,1)S(1)} %get-tuple-element.275), channel_id=1, source_target_pairs={{0,4},{1,5},{2,6},{3,7},{4,0},{5,1},{6,2},{7,3},{8,12},{9,13},{10,... | collective-permute-start | bytes 1179656 | tf_op jit(solution)/shard_map/ppermute | solution.py:367
  386.3 21.5 %collective-permute-start.24 = (bf16[384,256]{1,0:T(8,128)(2,1)S(1)}, bf16[384,256]{1,0:T(8,128)(2,1)S(1)}, u32[]{:S(2)}, u32[]{:S(2)}) collective-permute-start(bf16[384,256]{1,0:T(8,128)(2,1)S(1)} %get-tuple-element.278), channel_id=1, source_target_pairs={{0,1},{1,0},{2,3},{3,2},{4,5},{5,4},{6,7},{7,6},{8,9},{9,8},{10,11... | collective-permute-start | bytes 589832 | tf_op jit(solution)/shard_map/ppermute | solution.py:367
  386.7 21.2 %collective-permute-start.25 = (bf16[384,256]{1,0:T(8,128)(2,1)S(1)}, bf16[384,256]{1,0:T(8,128)(2,1)S(1)}, u32[]{:S(2)}, u32[]{:S(2)}) collective-permute-start(bf16[384,256]{1,0:T(8,128)(2,1)S(1)} %get-tuple-element.277), channel_id=1, source_target_pairs={{0,2},{1,3},{2,0},{3,1},{4,6},{5,7},{6,4},{7,5},{8,10},{9,11},{10,... | collective-permute-start | bytes 589832 | tf_op jit(solution)/shard_map/ppermute | solution.py:367
  388.2 19.7 %collective-permute-start.26 = (bf16[384,256]{1,0:T(8,128)(2,1)S(1)}, bf16[384,256]{1,0:T(8,128)(2,1)S(1)}, u32[]{:S(2)}, u32[]{:S(2)}) collective-permute-start(bf16[384,256]{1,0:T(8,128)(2,1)S(1)} %get-tuple-element.276), channel_id=1, source_target_pairs={{0,3},{1,2},{2,1},{3,0},{4,7},{5,6},{6,5},{7,4},{8,11},{9,10},{10,... | collective-permute-start | bytes 589832 | tf_op jit(solution)/shard_map/ppermute | solution.py:367
  418.8 11.2 %collective-permute-start.28 = (bf16[256,768]{1,0:T(8,128)(2,1)S(1)}, bf16[256,768]{1,0:T(8,128)(2,1)S(1)}, u32[]{:S(2)}, u32[]{:S(2)}) collective-permute-start(bf16[256,768]{1,0:T(8,128)(2,1)S(1)} %get-tuple-element.175), channel_id=1, source_target_pairs={{0,1},{1,0},{2,3},{3,2},{4,5},{5,4},{6,7},{7,6},{8,9},{9,8},{10,11... | collective-permute-start | bytes 1179656 | tf_op jit(solution)/shard_map/ppermute | solution.py:367
  419.2 11.6 %collective-permute-start.29 = (bf16[256,768]{1,0:T(8,128)(2,1)S(1)}, bf16[256,768]{1,0:T(8,128)(2,1)}, u32[]{:S(2)}, u32[]{:S(2)}) collective-permute-start(bf16[256,768]{1,0:T(8,128)(2,1)S(1)} %get-tuple-element.176), channel_id=1, source_target_pairs={{0,1},{1,0},{2,3},{3,2},{4,5},{5,4},{6,7},{7,6},{8,9},{9,8},{10,11... | collective-permute-start | bytes 1179656 | tf_op jit(solution)/shard_map/ppermute | solution.py:367
  435.8 35.9 %collective-permute-start.30 = (bf16[256,768]{1,0:T(8,128)(2,1)}, bf16[256,768]{1,0:T(8,128)(2,1)}, u32[]{:S(2)}, u32[]{:S(2)}) collective-permute-start(bf16[256,768]{1,0:T(8,128)(2,1)} %add_convert_fusion.10), channel_id=1, source_target_pairs={{0,2},{1,3},{2,0},{3,1},{4,6},{5,7},{6,4},{7,5},{8,10},{9,11},{10,... | collective-permute-start | bytes 1179656 | tf_op jit(solution)/shard_map/ppermute | solution.py:367
  437.1 89.7 %all-to-all-start = ((bf16[4,256,1024]{2,1,0:T(8,128)(2,1)}), bf16[4,256,1024]{2,1,0:T(8,128)(2,1)}, u32[]{:S(2)}, u32[]{:S(2)}) async-start(bf16[4,256,1024]{2,1,0:T(8,128)(2,1)} %bitcast.256), calls=%async_computation | async-start | bytes 4194304 | tf_op jit(solution)/shard_map/all_to_all | solution.py:419
  482.6 28.9 %collective-permute-start.34 = (bf16[384,1024]{1,0:T(8,128)(2,1)S(1)}, bf16[384,1024]{1,0:T(8,128)(2,1)S(1)}, u32[]{:S(2)}, u32[]{:S(2)}) collective-permute-start(bf16[384,1024]{1,0:T(8,128)(2,1)S(1)} %add_convert_fusion.5), channel_id=1, source_target_pairs={{0,2},{1,3},{2,0},{3,1},{4,6},{5,7},{6,4},{7,5},{8,10},{9,11},{10,... | collective-permute-start | bytes 2359304 | tf_op jit(solution)/shard_map/ppermute | solution.py:367
  484.7 33.6 %collective-permute-start.33 = (bf16[16,32,768]{2,1,0:T(8,128)(2,1)S(1)}, bf16[16,32,768]{2,1,0:T(8,128)(2,1)}, u32[]{:S(2)}, u32[]{:S(2)}) collective-permute-start(bf16[16,32,768]{2,1,0:T(8,128)(2,1)S(1)} %get-tuple-element.262), channel_id=1, source_target_pairs={{0,16},{1,17},{2,18},{3,19},{4,20},{5,21},{6,22},{7,23},{8,24},{9,... | collective-permute-start | bytes 2359304 | tf_op jit(solution)/shard_map/ppermute | solution.py:367
  488.5 17.3 %collective-permute-start.35 = (bf16[128,768]{1,0:T(8,128)(2,1)S(1)}, bf16[128,768]{1,0:T(8,128)(2,1)S(1)}, u32[]{:S(2)}, u32[]{:S(2)}) collective-permute-start(bf16[128,768]{1,0:T(8,128)(2,1)S(1)} %get-tuple-element.299), channel_id=1, source_target_pairs={{0,4},{1,5},{2,6},{3,7},{4,0},{5,1},{6,2},{7,3},{8,12},{9,13},{10,... | collective-permute-start | bytes 589832 | tf_op jit(solution)/shard_map/ppermute | solution.py:367
  529.0 27.9 %collective-permute-start.38 = (bf16[2,192,1024]{2,1,0:T(8,128)(2,1)}, bf16[2,192,1024]{2,1,0:T(8,128)(2,1)}, u32[]{:S(2)}, u32[]{:S(2)}) collective-permute-start(bf16[2,192,1024]{2,1,0:T(8,128)(2,1)} %dynamic-slice_bitcast_fusion), channel_id=1, source_target_pairs={{0,2},{1,3},{2,0},{3,1},{4,6},{5,7},{6,4},{7,5},{8,10},{9,11},{10,... | collective-permute-start | bytes 2359304 | tf_op jit(solution)/shard_map/ppermute | solution.py:367
  534.8 21.2 %collective-permute-start.37 = (bf16[192,1024]{1,0:T(8,128)(2,1)}, bf16[192,1024]{1,0:T(8,128)(2,1)}, u32[]{:S(2)}, u32[]{:S(2)}) collective-permute-start(bf16[192,1024]{1,0:T(8,128)(2,1)} %get-tuple-element.273), channel_id=1, source_target_pairs={{0,4},{1,5},{2,6},{3,7},{4,0},{5,1},{6,2},{7,3},{8,12},{9,13},{10,... | collective-permute-start | bytes 1179656 | tf_op jit(solution)/shard_map/ppermute | solution.py:367
  558.8 30.6 %collective-permute-start.40 = (bf16[1,192,1024]{2,1,0:T(8,128)(2,1)}, bf16[1,192,1024]{2,1,0:T(8,128)(2,1)}, u32[]{:S(2)}, u32[]{:S(2)}) collective-permute-start(bf16[1,192,1024]{2,1,0:T(8,128)(2,1)} %fusion.18), channel_id=1, source_target_pairs={{0,4},{1,5},{2,6},{3,7},{4,0},{5,1},{6,2},{7,3},{8,12},{9,13},{10,... | collective-permute-start | bytes 1179656 | tf_op jit(solution)/shard_map/ppermute | solution.py:367
  563.0 26.4 %collective-permute-start.39 = (bf16[4,32,768]{2,1,0:T(8,128)(2,1)}, bf16[4,32,768]{2,1,0:T(8,128)(2,1)}, u32[]{:S(2)}, u32[]{:S(2)}) collective-permute-start(bf16[4,32,768]{2,1,0:T(8,128)(2,1)} %fusion.21), channel_id=1, source_target_pairs={{0,4},{1,5},{2,6},{3,7},{4,0},{5,1},{6,2},{7,3},{8,12},{9,13},{10,... | collective-permute-start | bytes 589832 | tf_op jit(solution)/shard_map/ppermute | solution.py:367
  564.1 25.3 %all-to-all-start.1 = ((bf16[32,2,768]{2,1,0:T(2,128)(2,1)}), bf16[32,2,768]{2,1,0:T(2,128)(2,1)S(1)}, u32[]{:S(2)}, u32[]{:S(2)}) async-start(bf16[32,2,768]{2,1,0:T(2,128)(2,1)} %reshape.474), calls=%async_computation.1 | async-start | bytes 196608 | tf_op jit(solution)/shard_map/all_to_all | solution.py:772
  (117 other events, 880.7 us)
Sparse Core Ops, SparseCore 0:
  11.1 227.6 all-gather.2
  344.3 85.4 reduce-scatter.6
  433.0 84.0 reduce-scatter.8

commit v6 on v5

--- a/solution.py
+++ b/solution.py
@@ -612,7 +612,6 @@
     query, kv, feats_all, views_all, cotangent = together((query, kv, feats_all, views_all, cotangent))
     attended_own, lse1 = attend(query, kv, None)
     attended_own, first = together((attended_own, first))
-    cot = compact(cotangent)
     attended = grid.exchange(jnp.stack(grid.in_order(chunks(attended_own))))
 
     packed = first
@@ -648,6 +647,8 @@
     unit2, rstd2 = norm_parts(second)
     normed = low(unit2 * g_mid + b_mid)
     asked = low(low(dot(normed, full_cq)).astype(f32) * factor)
+    asked, cotangent = together((asked, cotangent))
+    cot = compact(cotangent)
     crossed, lse2 = attend(asked, mem, bias)
     third = second + dot(crossed, full_co)
     third, cot = together((third, cot))
@@ -774,10 +775,10 @@
     ffn_grad = ffn.send(ffn_moved)
     ffn_up, ffn_down = unstack_columns(ffn_grad[:tall], shard), ffn_grad[tall:]
     patch_grad = spread(patch_low, patch_moved)
+    own_moved = own_scatter.send(own_moved)
     own_moved, moved, token_grad, small_grad, patch_grad, ffn_up, ffn_down = together(
         (own_moved, moved, token_grad, small_grad, patch_grad, ffn_up, ffn_down)
     )
-    own_moved = own_scatter.send(own_moved)
     tiny = jnp.sum(small_grad.astype(f32), 0).reshape(-1)
     rest_sum = rest.send(moved)
     self_sum = own_scatter.send(own_moved).astype(f32)

time: 613 us -> 609 us (level)
    all_to_all x1, waiting for transfers between devices: 16.8 us -> 2.81 us  [on_device(): lax.all_to_all(small_grad.reshape(parts, small_count, lot), BOTH, 0, 0, t...]
    ppermute x44, waiting for transfers between devices: 196 us -> 204 us  [swap(): return lax.ppermute(value, BOTH, [(i, i ^ mask) for i in range(self.all)])]
    unnamed x224 -> x220, local copies, waits for them, and re-layouts: 22.6 us -> 23.3 us
  transfers between devices with their start and end apart: 49 -> 49, of which waited for: 19 -> 21; matrix products, arithmetic and copies ran while one was open for 24% -> 24% of each run, Pallas kernels for 15% -> 18%
where the time goes in v6:
time: 609 us; the launch traced here: 603 us
  waiting for transfers between devices  207 us (34%)
  Pallas kernels  137 us (22%)
  other arithmetic  78.9 us (13%)
  local copies, waits for them, and re-layouts  72.2 us (12%)
  starting transfers between devices  48.6 us (8%)
  matrix products  43 us (7%)
  between operations  15.9 us (3%)
    ppermute x44, waiting for transfers between devices, swap(): return lax.ppermute(value, BOTH, [(i, i ^ mask) for i in range(self.all)])  204 us
    pallas_call x2, Pallas kernels, attend_back(): pl.pallas_call(partial(attend_back_kernel, masked), grid=(pairs, rows //...  50.6 us
    dot_general x13, matrix products, dot(): return lax.dot_general(left, right, dims, preferred_element_type=f32)  43 us
    ppermute x44, starting transfers between devices, swap(): return lax.ppermute(value, BOTH, [(i, i ^ mask) for i in range(self.all)])  39.4 us
    pallas_call x2, Pallas kernels, attend(): pl.pallas_call(partial(attend_kernel, masked), grid=(pairs, rows // tile)...  35.9 us
    pallas_call x1, Pallas kernels, feed_forward(): pl.pallas_call(block_kernel, grid_spec=pltpu.PrefetchScalarGridSpec(num_s...  30.8 us
    convert_element_type x8, other arithmetic, add(): return sum((t.astype(f32) for t in terms)).astype(bf16)  28 us
    unnamed x220, local copies, waits for them, and re-layouts  23.3 us
  transfers between devices with their start and end apart: 49, of which 21 were waited for; matrix products, arithmetic and copies ran while one was open for 24% of the time, Pallas kernels for 18%

profile of v6, /device:TPU:0, one launch (start us, length us, event | category | flops | bytes accessed | tf_op | source)
XLA Modules:
  0.0 602.9 jit_solution(16955605392307934937)
XLA Ops:
  28.6 31.8 %collective-permute-done.3 = bf16[4,40,768]{2,0,1:T(4,128)(2,1)} collective-permute-done((bf16[4,40,768]{2,0,1:T(4,128)(2,1)}, bf16[4,40,768]{2,0,1:T(4,128)(2,1)}, u32[]{:S(2)}, u32[]{:S(2)}) %collective-permute-start.3) | collective-permute-done | bytes 245792 | tf_op jit(solution)/shard_map/ppermute | solution.py:367
  60.4 3.5 concatenate.123
  63.9 3.4 concatenate.122
  70.3 3.6 collective-permute-done.6
  76.4 12.0 %collective-permute-done.4 = bf16[8,40,768]{2,0,1:T(8,128)(2,1)} collective-permute-done((bf16[8,40,768]{2,0,1:T(8,128)(2,1)}, bf16[8,40,768]{2,0,1:T(8,128)(2,1)}, u32[]{:S(2)}, u32[]{:S(2)}) %collective-permute-start.4) | collective-permute-done | bytes 491552 | tf_op jit(solution)/shard_map/ppermute | solution.py:367
  93.1 38.4 %collective-permute-done.8 = bf16[384,1024]{1,0:T(8,128)(2,1)} collective-permute-done((bf16[384,1024]{1,0:T(8,128)(2,1)}, bf16[384,1024]{1,0:T(8,128)(2,1)}, u32[]{:S(2)}, u32[]{:S(2)}) %collective-permute-start.8) | collective-permute-done | bytes 786464 | tf_op jit(solution)/shard_map/ppermute | solution.py:367
  140.5 3.9 maximum_select_fusion
  149.0 3.4 convert_element_type.324
  154.0 4.4 convolution_convert_fusion.2
  174.1 41.2 %collective-permute-done.12 = bf16[256,768]{1,0:T(8,128)(2,1)S(1)} collective-permute-done((bf16[256,768]{1,0:T(8,128)(2,1)S(1)}, bf16[256,768]{1,0:T(8,128)(2,1)S(1)}, u32[]{:S(2)}, u32[]{:S(2)}) %collective-permute-start.12) | collective-permute-done | bytes 393248 | tf_op jit(solution)/shard_map/ppermute | solution.py:367
  219.4 21.0 %attend.2 = (bf16[1536,256]{1,0:T(8,128)(2,1)}, f32[2,1536,128]{2,1,0:T(8,128)}) custom-call(bf16[1536,256]{1,0:T(8,128)(2,1)} %multiply_convert_fusion.1.refs_0_, bf16[1536,512]{1,0:T(8,128)(2,1)} %slice.254.refs_1_), custom_call_target="tpu_custom_call" | custom-call | flops 9663676416 | bytes 3145728 | tf_op jit(solution)/shard_map/attend/pallas_call | solution.py:74
  241.9 6.7 %fusion.38 = (bf16[32,32,1024]{2,1,0:T(8,128)(2,1)}, bf16[32,32,1024]{2,1,0:T(8,128)(2,1)S(1)}, bf16[32,32,1024]{2,1,0:T(8,128)(2,1)S(1)}, bf16[32,32,1024]{2,1,0:T(8,128)(2,1)S(1)}, bf16[32,32,1024]{2,1,0:T(8,128)(2,1)S(1)}) fusion(bf16[32,448,1024]{2,1,0:T(8,128)(2,1)} %bitcast.242), kind=kLoop, calls=%fused_computation.247 | loop fusion | bytes 20971520 | tf_op jit(solution)/shard_map/slice | solution.py:621
  253.8 6.2 %convolution_convert_fusion.1.refs_1_ = bf16[1024,2048]{1,0:T(8,128)(2,1)} fusion(bf16[1024,1024]{1,0:T(8,128)(2,1)S(1)} %add_convert_fusion.3.refs_6_, bf16[1024,1024]{1,0:T(8,128)(2,1)S(1)} %bitcast.249, bf16[1024,1024]{1,0:T(8,128)(2,1)S(1)} %bitcast.251), kind=kOutput, calls=%fused_computation.17 | convolution fusion | flops 4305453056 | bytes 10485760 | tf_op jit(solution)/shard_map/dot_general | solution.py:26
  267.3 14.9 %attend.3 = (bf16[384,1024]{1,0:T(8,128)(2,1)}, f32[8,384,128]{2,1,0:T(8,128)}) custom-call(bf16[384,1024]{1,0:T(8,128)(2,1)} %multiply_convert_fusion.refs_0_, bf16[1024,2048]{1,0:T(8,128)(2,1)} %convolution_convert_fusion.1.refs_1_, f32[1,1024]{1,0:T(1,128)} %compare_select_fusion.refs_2_.refs_5_), custom_call_target="tpu_custom_call" | custom-call | flops 6442450944 | bytes 5767168 | tf_op jit(solution)/shard_map/attend/pallas_call | solution.py:74
  288.1 30.8 %feed_forward.1 = (bf16[384,1024]{1,0:T(8,128)(2,1)}, f32[384,1024]{1,0:T(8,128)}, bf16[16,256,1024]{2,1,0:T(8,128)(2,1)}, bf16[16,256,1024]{2,1,0:T(8,128)(2,1)}, f32[8,1024]{1,0:T(8,128)}, /*index=5*/f32[1,4096]{1,0:T(1,128)}) custom-call(s32[1]{0:T(128)} %bitcast.8.core_ref, f32[384,1024]{1,0:T(8,128)} %convolution_add_fusion.third_ref, ...), custom_call_target="tpu_custom_call" | custom-call | flops 1 | bytes 1 | tf_op jit(solution)/shard_map/feed_forward/pallas_call | solution.py:254
  322.6 9.8 %collective-permute-done.22 = bf16[16,256,1024]{2,1,0:T(8,128)(2,1)S(1)} collective-permute-done((bf16[16,256,1024]{2,1,0:T(8,128)(2,1)}, bf16[16,256,1024]{2,1,0:T(8,128)(2,1)S(1)}, u32[]{:S(2)}, u32[]{:S(2)}) %collective-permute-start.22) | collective-permute-done | bytes 8388640 | tf_op jit(solution)/shard_map/ppermute | solution.py:367
  332.4 9.1 %add_convert_fusion = bf16[16,256,1024]{2,1,0:T(8,128)(2,1)} fusion(bf16[16,256,1024]{2,1,0:T(8,128)(2,1)S(1)} %collective-permute-done.22, bf16[16,256,1024]{2,1,0:T(8,128)(2,1)} %get-tuple-element.151), kind=kLoop, calls=%fused_computation | loop fusion | flops 16777216 | bytes 25165824 | tf_op jit(solution)/shard_map/convert_element_type | solution.py:450
  344.8 20.7 %attend_back.2 = (bf16[384,1024]{1,0:T(8,128)(2,1)}, bf16[1024,2048]{1,0:T(8,128)(2,1)}) custom-call(bf16[384,1024]{1,0:T(8,128)(2,1)} %multiply_convert_fusion.refs_0_, bf16[1024,2048]{1,0:T(8,128)(2,1)} %convolution_convert_fusion.1.refs_1_, bf16[384,1024]{1,0:T(8,128)(2,1)} %get-tuple-element.163.refs_2_.refs_0_, ...), custom_call_target="tpu_custom_call" | custom-call | flops 16106127360 | bytes 11534336 | tf_op jit(solution)/shard_map/attend_back/pallas_call | solution.py:144
  366.3 4.0 multiply_reduce_fusion.1
  375.8 7.1 %fusion = (f32[1024]{0:T(1024)}, f32[1024]{0:T(1024)}, f32[1024]{0:T(1024)}, f32[1024]{0:T(1024)}, bf16[1024,1024]{1,0:T(8,128)(2,1)}) fusion(f32[1024]{0:T(1024)S(1)} %bitcast.321, f32[1024]{0:T(1024)S(1)} %bitcast.327, f32[1024]{0:T(1024)S(1)} %bitcast.325, f32[1024]{0:T(1024)S(1)} %bitcast.323, bf16[1024,2048]{1,0:T(8,128)(2,1)S(1)} %copy-done.8, ...), kind=kOutput, calls=%fused_computation.9 | convolution fusion | flops 4313837568 | bytes 10518528 | tf_op jit(solution)/shard_map/dot_general | solution.py:26
  385.3 19.6 %weight_grads.1 = (bf16[16,192,1024]{2,1,0:T(8,128)(2,1)}, bf16[16,192,1024]{2,1,0:T(8,128)(2,1)}) custom-call(s32[1]{0:T(128)} %bitcast.8.core_ref, bf16[384,1024]{1,0:T(8,128)(2,1)} %get-tuple-element.163.refs_2_.refs_0_, bf16[384,1024]{1,0:T(8,128)(2,1)} %copy-done.10, bf16[384,1024]{1,0:T(8,128)(2,1)} %copy-done.9, ...), custom_call_target="tpu_custom_call" | custom-call | flops 1 | bytes 1 | tf_op jit(solution)/shard_map/weight_grads/pallas_call | solution.py:342
  409.9 5.6 collective-permute-done.27
  416.1 10.9 %add_convert_fusion.1 = bf16[16,192,1024]{2,1,0:T(8,128)(2,1)} fusion(bf16[16,192,1024]{2,1,0:T(8,128)(2,1)} %collective-permute-done.27, bf16[16,192,1024]{2,1,0:T(8,128)(2,1)} %get-tuple-element.184), kind=kLoop, calls=%fused_computation.1 | loop fusion | flops 12582912 | bytes 18874368 | tf_op jit(solution)/shard_map/convert_element_type | solution.py:450
  434.4 4.5 all-to-all-start
  438.8 29.9 %attend_back.3 = (bf16[1536,256]{1,0:T(8,128)(2,1)}, bf16[1536,512]{1,0:T(8,128)(2,1)}) custom-call(bf16[1536,256]{1,0:T(8,128)(2,1)} %multiply_convert_fusion.1.refs_0_, bf16[1536,512]{1,0:T(8,128)(2,1)} %slice.254.refs_1_, bf16[1536,256]{1,0:T(8,128)(2,1)} %get-tuple-element.135.refs_2_, bf16[1536,256]{1,0:T(8,128)(2,1)} %pad_maximum_fusion.11.refs_3_, ...), custom_call_target="tpu_custom_call" | custom-call | flops 24159191040 | bytes 6291456 | tf_op jit(solution)/shard_map/attend_back/pallas_call | solution.py:144
  475.8 3.3 convolution_convert_fusion.3
  487.9 14.9 %collective-permute-done.35 = bf16[128,768]{1,0:T(8,128)(2,1)S(1)} collective-permute-done((bf16[128,768]{1,0:T(8,128)(2,1)S(1)}, bf16[128,768]{1,0:T(8,128)(2,1)S(1)}, u32[]{:S(2)}, u32[]{:S(2)}) %collective-permute-start.35) | collective-permute-done | bytes 196640 | tf_op jit(solution)/shard_map/ppermute | solution.py:367
  502.8 5.7 collective-permute-done.34
  508.5 7.9 %collective-permute-done.33 = bf16[16,32,768]{2,1,0:T(8,128)(2,1)} collective-permute-done((bf16[16,32,768]{2,1,0:T(8,128)(2,1)S(1)}, bf16[16,32,768]{2,1,0:T(8,128)(2,1)}, u32[]{:S(2)}, u32[]{:S(2)}) %collective-permute-start.33) | collective-permute-done | bytes 786464 | tf_op jit(solution)/shard_map/ppermute | solution.py:367
  541.2 12.8 %collective-permute-done.37 = bf16[192,1024]{1,0:T(8,128)(2,1)} collective-permute-done((bf16[192,1024]{1,0:T(8,128)(2,1)}, bf16[192,1024]{1,0:T(8,128)(2,1)}, u32[]{:S(2)}, u32[]{:S(2)}) %collective-permute-start.37) | collective-permute-done | bytes 393248 | tf_op jit(solution)/shard_map/ppermute | solution.py:367
  563.2 4.6 all-to-all-start.1
  567.8 11.4 %collective-permute-done.39 = bf16[4,32,768]{2,1,0:T(8,128)(2,1)} collective-permute-done((bf16[4,32,768]{2,1,0:T(8,128)(2,1)}, bf16[4,32,768]{2,1,0:T(8,128)(2,1)}, u32[]{:S(2)}, u32[]{:S(2)}) %collective-permute-start.39) | collective-permute-done | bytes 196640 | tf_op jit(solution)/shard_map/ppermute | solution.py:367
  (508 shorter events, 179.8 us)
Async XLA Ops:
  7.2 233.1 %all-gather.3.cloned.1.call-start = ((), (), s32[]{:S(2)}) async-start(), calls=%async_computation.4 | async-start | bytes 30277632 | tf_op jit(solution)/shard_map/all_gather | solution.py:580
  11.0 416.8 %reduce-scatter.7.cloned.1.call-start = ((), (), s32[]{:S(2)}) async-start(), calls=%async_computation.5 | async-start | bytes 10485760
  23.0 37.4 %collective-permute-start.3 = (bf16[4,40,768]{2,0,1:T(4,128)(2,1)}, bf16[4,40,768]{2,0,1:T(4,128)(2,1)}, u32[]{:S(2)}, u32[]{:S(2)}) collective-permute-start(bf16[4,40,768]{2,0,1:T(4,128)(2,1)} %pad_maximum_fusion.15), channel_id=1, source_target_pairs={{0,4},{1,5},{2,6},{3,7},{4,0},{5,1},{6,2},{7,3},{8,12},{9,13},{10,... | collective-permute-start | bytes 737288 | tf_op jit(solution)/shard_map/ppermute | solution.py:367
  26.4 47.6 %collective-permute-start.6 = (bf16[192,1024]{1,0:T(8,128)(2,1)}, bf16[192,1024]{1,0:T(8,128)(2,1)}, u32[]{:S(2)}, u32[]{:S(2)}) collective-permute-start(bf16[192,1024]{1,0:T(8,128)(2,1)} %dynamic-slice_bitcast_fusion.4), channel_id=1, source_target_pairs={{0,4},{1,5},{2,6},{3,7},{4,0},{5,1},{6,2},{7,3},{8,12},{9,13},{10,... | collective-permute-start | bytes 1179656 | tf_op jit(solution)/shard_map/ppermute | solution.py:367
  69.2 19.3 %collective-permute-start.4 = (bf16[8,40,768]{2,0,1:T(8,128)(2,1)}, bf16[8,40,768]{2,0,1:T(8,128)(2,1)}, u32[]{:S(2)}, u32[]{:S(2)}) collective-permute-start(bf16[8,40,768]{2,0,1:T(8,128)(2,1)} %broadcast_select_fusion), channel_id=1, source_target_pairs={{0,8},{1,9},{2,10},{3,11},{4,12},{5,13},{6,14},{7,15},{8,0},{9,1},... | collective-permute-start | bytes 1474568 | tf_op jit(solution)/shard_map/ppermute | solution.py:367
  76.2 55.2 %collective-permute-start.8 = (bf16[384,1024]{1,0:T(8,128)(2,1)}, bf16[384,1024]{1,0:T(8,128)(2,1)}, u32[]{:S(2)}, u32[]{:S(2)}) collective-permute-start(bf16[384,1024]{1,0:T(8,128)(2,1)} %pad_maximum_fusion.5), channel_id=1, source_target_pairs={{0,2},{1,3},{2,0},{3,1},{4,6},{5,7},{6,4},{7,5},{8,10},{9,11},{10,... | collective-permute-start | bytes 2359304 | tf_op jit(solution)/shard_map/ppermute | solution.py:367
  76.3 57.5 %collective-permute-start.7 = (bf16[384,1024]{1,0:T(8,128)(2,1)}, bf16[384,1024]{1,0:T(8,128)(2,1)}, u32[]{:S(2)}, u32[]{:S(2)}) collective-permute-start(bf16[384,1024]{1,0:T(8,128)(2,1)} %pad_maximum_fusion.5), channel_id=1, source_target_pairs={{0,1},{1,0},{2,3},{3,2},{4,5},{5,4},{6,7},{7,6},{8,9},{9,8},{10,11... | collective-permute-start | bytes 2359304 | tf_op jit(solution)/shard_map/ppermute | solution.py:367
  91.2 45.2 %collective-permute-start.5 = (bf16[16,40,768]{2,0,1:T(8,128)(2,1)}, bf16[16,40,768]{2,0,1:T(8,128)(2,1)}, u32[]{:S(2)}, u32[]{:S(2)}) collective-permute-start(bf16[16,40,768]{2,0,1:T(8,128)(2,1)} %maximum_select_fusion.1), channel_id=1, source_target_pairs={{0,16},{1,17},{2,18},{3,19},{4,20},{5,21},{6,22},{7,23},{8,24},{9,... | collective-permute-start | bytes 2949128 | tf_op jit(solution)/shard_map/ppermute | solution.py:367
  136.9 31.6 %collective-permute-start.14 = (s32[128]{0:T(128)}, s32[128]{0:T(128)}, u32[]{:S(2)}, u32[]{:S(2)}) collective-permute-start(s32[128]{0:T(128)} %fusion.32), channel_id=1, source_target_pairs={{0,4},{1,5},{2,6},{3,7},{4,0},{5,1},{6,2},{7,3},{8,12},{9,13},{10,... | collective-permute-start | bytes 1544 | tf_op jit(solution)/shard_map/ppermute | solution.py:367
  137.6 31.6 %collective-permute-start.10 = (bf16[128,768]{1,0:T(8,128)(2,1)}, bf16[128,768]{1,0:T(8,128)(2,1)}, u32[]{:S(2)}, u32[]{:S(2)}) collective-permute-start(bf16[128,768]{1,0:T(8,128)(2,1)} %dynamic-slice_bitcast_fusion.14), channel_id=1, source_target_pairs={{0,4},{1,5},{2,6},{3,7},{4,0},{5,1},{6,2},{7,3},{8,12},{9,13},{10,... | collective-permute-start | bytes 589832 | tf_op jit(solution)/shard_map/ppermute | solution.py:367
  170.1 45.2 %collective-permute-start.12 = (bf16[256,768]{1,0:T(8,128)(2,1)S(1)}, bf16[256,768]{1,0:T(8,128)(2,1)S(1)}, u32[]{:S(2)}, u32[]{:S(2)}) collective-permute-start(bf16[256,768]{1,0:T(8,128)(2,1)S(1)} %pad_maximum_fusion.12), channel_id=1, source_target_pairs={{0,2},{1,3},{2,0},{3,1},{4,6},{5,7},{6,4},{7,5},{8,10},{9,11},{10,... | collective-permute-start | bytes 1179656 | tf_op jit(solution)/shard_map/ppermute | solution.py:367
  173.2 43.7 %collective-permute-start.11 = (bf16[256,768]{1,0:T(8,128)(2,1)S(1)}, bf16[256,768]{1,0:T(8,128)(2,1)S(1)}, u32[]{:S(2)}, u32[]{:S(2)}) collective-permute-start(bf16[256,768]{1,0:T(8,128)(2,1)S(1)} %pad_maximum_fusion.12), channel_id=1, source_target_pairs={{0,1},{1,0},{2,3},{3,2},{4,5},{5,4},{6,7},{7,6},{8,9},{9,8},{10,11... | collective-permute-start | bytes 1179656 | tf_op jit(solution)/shard_map/ppermute | solution.py:367
  249.1 10.9 %collective-permute-start.18 = (bf16[384,256]{1,0:T(8,128)(2,1)S(1)}, bf16[384,256]{1,0:T(8,128)(2,1)S(1)}, u32[]{:S(2)}, u32[]{:S(2)}) collective-permute-start(bf16[384,256]{1,0:T(8,128)(2,1)S(1)} %get-tuple-element.298), channel_id=1, source_target_pairs={{0,1},{1,0},{2,3},{3,2},{4,5},{5,4},{6,7},{7,6},{8,9},{9,8},{10,11... | collective-permute-start | bytes 589832 | tf_op jit(solution)/shard_map/ppermute | solution.py:367
  266.3 20.8 %collective-permute-start.21 = (bf16[192,1024]{1,0:T(8,128)(2,1)}, bf16[192,1024]{1,0:T(8,128)(2,1)S(1)}, u32[]{:S(2)}, u32[]{:S(2)}) collective-permute-start(bf16[192,1024]{1,0:T(8,128)(2,1)} %get-tuple-element.291), channel_id=1, source_target_pairs={{0,4},{1,5},{2,6},{3,7},{4,0},{5,1},{6,2},{7,3},{8,12},{9,13},{10,... | collective-permute-start | bytes 1179656 | tf_op jit(solution)/shard_map/ppermute | solution.py:367
  319.0 13.4 %collective-permute-start.22 = (bf16[16,256,1024]{2,1,0:T(8,128)(2,1)}, bf16[16,256,1024]{2,1,0:T(8,128)(2,1)S(1)}, u32[]{:S(2)}, u32[]{:S(2)}) collective-permute-start(bf16[16,256,1024]{2,1,0:T(8,128)(2,1)} %get-tuple-element.152), channel_id=1, source_target_pairs={{0,1},{1,0},{2,3},{3,2},{4,5},{5,4},{6,7},{7,6},{8,9},{9,8},{10,11... | collective-permute-start | bytes 25165832 | tf_op jit(solution)/shard_map/ppermute | solution.py:367
  341.5 183.4 %reduce-scatter.9.cloned.1.call-start = ((), (), s32[]{:S(2)}) async-start(), calls=%async_computation.6 | async-start | bytes 7864320
  344.5 21.0 %collective-permute-start.23 = (bf16[192,1024]{1,0:T(8,128)(2,1)S(1)}, bf16[192,1024]{1,0:T(8,128)(2,1)S(1)}, u32[]{:S(2)}, u32[]{:S(2)}) collective-permute-start(bf16[192,1024]{1,0:T(8,128)(2,1)S(1)} %get-tuple-element.285), channel_id=1, source_target_pairs={{0,4},{1,5},{2,6},{3,7},{4,0},{5,1},{6,2},{7,3},{8,12},{9,13},{10,... | collective-permute-start | bytes 1179656 | tf_op jit(solution)/shard_map/ppermute | solution.py:367
  383.0 22.0 %collective-permute-start.24 = (bf16[384,256]{1,0:T(8,128)(2,1)S(1)}, bf16[384,256]{1,0:T(8,128)(2,1)S(1)}, u32[]{:S(2)}, u32[]{:S(2)}) collective-permute-start(bf16[384,256]{1,0:T(8,128)(2,1)S(1)} %get-tuple-element.288), channel_id=1, source_target_pairs={{0,1},{1,0},{2,3},{3,2},{4,5},{5,4},{6,7},{7,6},{8,9},{9,8},{10,11... | collective-permute-start | bytes 589832 | tf_op jit(solution)/shard_map/ppermute | solution.py:367
  383.0 21.9 %collective-permute-start.25 = (bf16[384,256]{1,0:T(8,128)(2,1)S(1)}, bf16[384,256]{1,0:T(8,128)(2,1)S(1)}, u32[]{:S(2)}, u32[]{:S(2)}) collective-permute-start(bf16[384,256]{1,0:T(8,128)(2,1)S(1)} %get-tuple-element.287), channel_id=1, source_target_pairs={{0,2},{1,3},{2,0},{3,1},{4,6},{5,7},{6,4},{7,5},{8,10},{9,11},{10,... | collective-permute-start | bytes 589832 | tf_op jit(solution)/shard_map/ppermute | solution.py:367
  385.3 19.7 %collective-permute-start.26 = (bf16[384,256]{1,0:T(8,128)(2,1)S(1)}, bf16[384,256]{1,0:T(8,128)(2,1)S(1)}, u32[]{:S(2)}, u32[]{:S(2)}) collective-permute-start(bf16[384,256]{1,0:T(8,128)(2,1)S(1)} %get-tuple-element.286), channel_id=1, source_target_pairs={{0,3},{1,2},{2,1},{3,0},{4,7},{5,6},{6,5},{7,4},{8,11},{9,10},{10,... | collective-permute-start | bytes 589832 | tf_op jit(solution)/shard_map/ppermute | solution.py:367
  415.6 11.4 %collective-permute-start.28 = (bf16[256,768]{1,0:T(8,128)(2,1)S(1)}, bf16[256,768]{1,0:T(8,128)(2,1)S(1)}, u32[]{:S(2)}, u32[]{:S(2)}) collective-permute-start(bf16[256,768]{1,0:T(8,128)(2,1)S(1)} %get-tuple-element.182), channel_id=1, source_target_pairs={{0,1},{1,0},{2,3},{3,2},{4,5},{5,4},{6,7},{7,6},{8,9},{9,8},{10,11... | collective-permute-start | bytes 1179656 | tf_op jit(solution)/shard_map/ppermute | solution.py:367
  415.7 12.0 %collective-permute-start.29 = (bf16[256,768]{1,0:T(8,128)(2,1)S(1)}, bf16[256,768]{1,0:T(8,128)(2,1)}, u32[]{:S(2)}, u32[]{:S(2)}) collective-permute-start(bf16[256,768]{1,0:T(8,128)(2,1)S(1)} %get-tuple-element.183), channel_id=1, source_target_pairs={{0,1},{1,0},{2,3},{3,2},{4,5},{5,4},{6,7},{7,6},{8,9},{9,8},{10,11... | collective-permute-start | bytes 1179656 | tf_op jit(solution)/shard_map/ppermute | solution.py:367
  432.9 35.9 %collective-permute-start.30 = (bf16[256,768]{1,0:T(8,128)(2,1)}, bf16[256,768]{1,0:T(8,128)(2,1)}, u32[]{:S(2)}, u32[]{:S(2)}) collective-permute-start(bf16[256,768]{1,0:T(8,128)(2,1)} %add_convert_fusion.10), channel_id=1, source_target_pairs={{0,2},{1,3},{2,0},{3,1},{4,6},{5,7},{6,4},{7,5},{8,10},{9,11},{10,... | collective-permute-start | bytes 1179656 | tf_op jit(solution)/shard_map/ppermute | solution.py:367
  434.4 90.5 %all-to-all-start = ((bf16[4,256,1024]{2,1,0:T(8,128)(2,1)}), bf16[4,256,1024]{2,1,0:T(8,128)(2,1)}, u32[]{:S(2)}, u32[]{:S(2)}) async-start(bf16[4,256,1024]{2,1,0:T(8,128)(2,1)} %bitcast.259), calls=%async_computation | async-start | bytes 4194304 | tf_op jit(solution)/shard_map/all_to_all | solution.py:419
  479.5 28.9 %collective-permute-start.34 = (bf16[384,1024]{1,0:T(8,128)(2,1)S(1)}, bf16[384,1024]{1,0:T(8,128)(2,1)S(1)}, u32[]{:S(2)}, u32[]{:S(2)}) collective-permute-start(bf16[384,1024]{1,0:T(8,128)(2,1)S(1)} %add_convert_fusion.5), channel_id=1, source_target_pairs={{0,2},{1,3},{2,0},{3,1},{4,6},{5,7},{6,4},{7,5},{8,10},{9,11},{10,... | collective-permute-start | bytes 2359304 | tf_op jit(solution)/shard_map/ppermute | solution.py:367
  481.7 34.6 %collective-permute-start.33 = (bf16[16,32,768]{2,1,0:T(8,128)(2,1)S(1)}, bf16[16,32,768]{2,1,0:T(8,128)(2,1)}, u32[]{:S(2)}, u32[]{:S(2)}) collective-permute-start(bf16[16,32,768]{2,1,0:T(8,128)(2,1)S(1)} %get-tuple-element.272), channel_id=1, source_target_pairs={{0,16},{1,17},{2,18},{3,19},{4,20},{5,21},{6,22},{7,23},{8,24},{9,... | collective-permute-start | bytes 2359304 | tf_op jit(solution)/shard_map/ppermute | solution.py:367
  485.4 17.4 %collective-permute-start.35 = (bf16[128,768]{1,0:T(8,128)(2,1)S(1)}, bf16[128,768]{1,0:T(8,128)(2,1)S(1)}, u32[]{:S(2)}, u32[]{:S(2)}) collective-permute-start(bf16[128,768]{1,0:T(8,128)(2,1)S(1)} %get-tuple-element.309), channel_id=1, source_target_pairs={{0,4},{1,5},{2,6},{3,7},{4,0},{5,1},{6,2},{7,3},{8,12},{9,13},{10,... | collective-permute-start | bytes 589832 | tf_op jit(solution)/shard_map/ppermute | solution.py:367
  527.1 27.9 %collective-permute-start.38 = (bf16[2,192,1024]{2,1,0:T(8,128)(2,1)}, bf16[2,192,1024]{2,1,0:T(8,128)(2,1)}, u32[]{:S(2)}, u32[]{:S(2)}) collective-permute-start(bf16[2,192,1024]{2,1,0:T(8,128)(2,1)} %dynamic-slice_bitcast_fusion), channel_id=1, source_target_pairs={{0,2},{1,3},{2,0},{3,1},{4,6},{5,7},{6,4},{7,5},{8,10},{9,11},{10,... | collective-permute-start | bytes 2359304 | tf_op jit(solution)/shard_map/ppermute | solution.py:367
  532.7 21.3 %collective-permute-start.37 = (bf16[192,1024]{1,0:T(8,128)(2,1)}, bf16[192,1024]{1,0:T(8,128)(2,1)}, u32[]{:S(2)}, u32[]{:S(2)}) collective-permute-start(bf16[192,1024]{1,0:T(8,128)(2,1)} %get-tuple-element.283), channel_id=1, source_target_pairs={{0,4},{1,5},{2,6},{3,7},{4,0},{5,1},{6,2},{7,3},{8,12},{9,13},{10,... | collective-permute-start | bytes 1179656 | tf_op jit(solution)/shard_map/ppermute | solution.py:367
  556.7 22.5 %collective-permute-start.39 = (bf16[4,32,768]{2,1,0:T(8,128)(2,1)}, bf16[4,32,768]{2,1,0:T(8,128)(2,1)}, u32[]{:S(2)}, u32[]{:S(2)}) collective-permute-start(bf16[4,32,768]{2,1,0:T(8,128)(2,1)} %fusion.21), channel_id=1, source_target_pairs={{0,4},{1,5},{2,6},{3,7},{4,0},{5,1},{6,2},{7,3},{8,12},{9,13},{10,... | collective-permute-start | bytes 589832 | tf_op jit(solution)/shard_map/ppermute | solution.py:367
  562.0 26.0 %collective-permute-start.43 = (bf16[1,192,1024]{2,1,0:T(8,128)(2,1)S(1)}, bf16[1,192,1024]{2,1,0:T(8,128)(2,1)}, u32[]{:S(2)}, u32[]{:S(2)}) collective-permute-start(bf16[1,192,1024]{2,1,0:T(8,128)(2,1)S(1)} %fusion.18), channel_id=1, source_target_pairs={{0,4},{1,5},{2,6},{3,7},{4,0},{5,1},{6,2},{7,3},{8,12},{9,13},{10,... | collective-permute-start | bytes 1179656 | tf_op jit(solution)/shard_map/ppermute | solution.py:367
  563.2 24.1 %all-to-all-start.1 = ((bf16[32,2,768]{2,1,0:T(2,128)(2,1)}), bf16[32,2,768]{2,1,0:T(2,128)(2,1)S(1)}, u32[]{:S(2)}, u32[]{:S(2)}) async-start(bf16[32,2,768]{2,1,0:T(2,128)(2,1)} %reshape.474), calls=%async_computation.1 | async-start | bytes 196608 | tf_op jit(solution)/shard_map/all_to_all | solution.py:773
  (115 other events, 894.0 us)
Sparse Core Ops, SparseCore 0:
  11.1 224.4 all-gather.2
  341.6 86.1 reduce-scatter.6
  431.1 85.1 reduce-scatter.8

commit v7 on v6

--- a/solution.py
+++ b/solution.py
@@ -245,7 +245,7 @@
     rows, width = third.shape
     parts = packed.shape[0]
     hidden = up_bias.shape[1]
-    tile = 512
+    tile = min(hidden, width)
     per = width // tile
     tall = hidden // parts
     spread = tile // tall

time: 609 us -> 609 us (level)
  transfers between devices with their start and end apart: 49 -> 49, of which waited for: 21 -> 22; matrix products, arithmetic and copies ran while one was open for 24% -> 24% of each run, Pallas kernels for 18% -> 18%
where the time goes in v7:
time: 609 us; the launch traced here: 603 us
  waiting for transfers between devices  207 us (34%)
  Pallas kernels  137 us (22%)
  other arithmetic  78.9 us (13%)
  local copies, waits for them, and re-layouts  72 us (12%)
  starting transfers between devices  48.5 us (8%)
  matrix products  43 us (7%)
  between operations  15.9 us (3%)
    ppermute x44, waiting for transfers between devices, swap(): return lax.ppermute(value, BOTH, [(i, i ^ mask) for i in range(self.all)])  204 us
    pallas_call x2, Pallas kernels, attend_back(): pl.pallas_call(partial(attend_back_kernel, masked), grid=(pairs, rows //...  50.6 us
    dot_general x13, matrix products, dot(): return lax.dot_general(left, right, dims, preferred_element_type=f32)  43 us
    ppermute x44, starting transfers between devices, swap(): return lax.ppermute(value, BOTH, [(i, i ^ mask) for i in range(self.all)])  39.4 us
    pallas_call x2, Pallas kernels, attend(): pl.pallas_call(partial(attend_kernel, masked), grid=(pairs, rows // tile)...  35.9 us
    pallas_call x1, Pallas kernels, feed_forward(): pl.pallas_call(block_kernel, grid_spec=pltpu.PrefetchScalarGridSpec(num_s...  31.1 us
    convert_element_type x8, other arithmetic, add(): return sum((t.astype(f32) for t in terms)).astype(bf16)  28 us
    unnamed x220, local copies, waits for them, and re-layouts  23.3 us
  transfers between devices with their start and end apart: 49, of which 22 were waited for; matrix products, arithmetic and copies ran while one was open for 24% of the time, Pallas kernels for 18%

profile of v7, /device:TPU:0, one launch (start us, length us, event | category | flops | bytes accessed | tf_op | source)
XLA Modules:
  0.0 603.0 jit_solution(1847221035788253579)
XLA Ops:
  28.6 31.8 %collective-permute-done.3 = bf16[4,40,768]{2,0,1:T(4,128)(2,1)} collective-permute-done((bf16[4,40,768]{2,0,1:T(4,128)(2,1)}, bf16[4,40,768]{2,0,1:T(4,128)(2,1)}, u32[]{:S(2)}, u32[]{:S(2)}) %collective-permute-start.3) | collective-permute-done | bytes 245792 | tf_op jit(solution)/shard_map/ppermute | solution.py:367
  60.4 3.6 concatenate.123
  63.9 3.4 concatenate.122
  70.4 3.6 collective-permute-done.6
  76.4 12.1 %collective-permute-done.4 = bf16[8,40,768]{2,0,1:T(8,128)(2,1)} collective-permute-done((bf16[8,40,768]{2,0,1:T(8,128)(2,1)}, bf16[8,40,768]{2,0,1:T(8,128)(2,1)}, u32[]{:S(2)}, u32[]{:S(2)}) %collective-permute-start.4) | collective-permute-done | bytes 491552 | tf_op jit(solution)/shard_map/ppermute | solution.py:367
  93.1 38.4 %collective-permute-done.8 = bf16[384,1024]{1,0:T(8,128)(2,1)} collective-permute-done((bf16[384,1024]{1,0:T(8,128)(2,1)}, bf16[384,1024]{1,0:T(8,128)(2,1)}, u32[]{:S(2)}, u32[]{:S(2)}) %collective-permute-start.8) | collective-permute-done | bytes 786464 | tf_op jit(solution)/shard_map/ppermute | solution.py:367
  140.5 3.9 maximum_select_fusion
  149.0 3.4 convert_element_type.324
  154.0 4.4 convolution_convert_fusion.2
  174.1 41.2 %collective-permute-done.12 = bf16[256,768]{1,0:T(8,128)(2,1)S(1)} collective-permute-done((bf16[256,768]{1,0:T(8,128)(2,1)S(1)}, bf16[256,768]{1,0:T(8,128)(2,1)S(1)}, u32[]{:S(2)}, u32[]{:S(2)}) %collective-permute-start.12) | collective-permute-done | bytes 393248 | tf_op jit(solution)/shard_map/ppermute | solution.py:367
  219.4 21.0 %attend.2 = (bf16[1536,256]{1,0:T(8,128)(2,1)}, f32[2,1536,128]{2,1,0:T(8,128)}) custom-call(bf16[1536,256]{1,0:T(8,128)(2,1)} %multiply_convert_fusion.1.refs_0_, bf16[1536,512]{1,0:T(8,128)(2,1)} %slice.254.refs_1_), custom_call_target="tpu_custom_call" | custom-call | flops 9663676416 | bytes 3145728 | tf_op jit(solution)/shard_map/attend/pallas_call | solution.py:74
  241.9 6.5 %fusion.38 = (bf16[32,32,1024]{2,1,0:T(8,128)(2,1)}, bf16[32,32,1024]{2,1,0:T(8,128)(2,1)S(1)}, bf16[32,32,1024]{2,1,0:T(8,128)(2,1)S(1)}, bf16[32,32,1024]{2,1,0:T(8,128)(2,1)S(1)}, bf16[32,32,1024]{2,1,0:T(8,128)(2,1)S(1)}) fusion(bf16[32,448,1024]{2,1,0:T(8,128)(2,1)} %bitcast.242), kind=kLoop, calls=%fused_computation.247 | loop fusion | bytes 20971520 | tf_op jit(solution)/shard_map/slice | solution.py:621
  253.7 6.2 %convolution_convert_fusion.1.refs_1_ = bf16[1024,2048]{1,0:T(8,128)(2,1)} fusion(bf16[1024,1024]{1,0:T(8,128)(2,1)S(1)} %add_convert_fusion.3.refs_6_, bf16[1024,1024]{1,0:T(8,128)(2,1)S(1)} %bitcast.249, bf16[1024,1024]{1,0:T(8,128)(2,1)S(1)} %bitcast.251), kind=kOutput, calls=%fused_computation.17 | convolution fusion | flops 4305453056 | bytes 10485760 | tf_op jit(solution)/shard_map/dot_general | solution.py:26
  267.1 14.9 %attend.3 = (bf16[384,1024]{1,0:T(8,128)(2,1)}, f32[8,384,128]{2,1,0:T(8,128)}) custom-call(bf16[384,1024]{1,0:T(8,128)(2,1)} %multiply_convert_fusion.refs_0_, bf16[1024,2048]{1,0:T(8,128)(2,1)} %convolution_convert_fusion.1.refs_1_, f32[1,1024]{1,0:T(1,128)} %compare_select_fusion.refs_2_.refs_5_), custom_call_target="tpu_custom_call" | custom-call | flops 6442450944 | bytes 5767168 | tf_op jit(solution)/shard_map/attend/pallas_call | solution.py:74
  288.0 31.1 %feed_forward.1 = (bf16[384,1024]{1,0:T(8,128)(2,1)}, f32[384,1024]{1,0:T(8,128)}, bf16[16,256,1024]{2,1,0:T(8,128)(2,1)}, bf16[16,256,1024]{2,1,0:T(8,128)(2,1)}, f32[8,1024]{1,0:T(8,128)}, /*index=5*/f32[1,4096]{1,0:T(1,128)}) custom-call(s32[1]{0:T(128)} %bitcast.8.core_ref, f32[384,1024]{1,0:T(8,128)} %convolution_add_fusion.third_ref, ...), custom_call_target="tpu_custom_call" | custom-call | flops 1 | bytes 1 | tf_op jit(solution)/shard_map/feed_forward/pallas_call | solution.py:254
  322.7 9.8 %collective-permute-done.22 = bf16[16,256,1024]{2,1,0:T(8,128)(2,1)S(1)} collective-permute-done((bf16[16,256,1024]{2,1,0:T(8,128)(2,1)}, bf16[16,256,1024]{2,1,0:T(8,128)(2,1)S(1)}, u32[]{:S(2)}, u32[]{:S(2)}) %collective-permute-start.22) | collective-permute-done | bytes 8388640 | tf_op jit(solution)/shard_map/ppermute | solution.py:367
  332.5 9.1 %add_convert_fusion = bf16[16,256,1024]{2,1,0:T(8,128)(2,1)} fusion(bf16[16,256,1024]{2,1,0:T(8,128)(2,1)S(1)} %collective-permute-done.22, bf16[16,256,1024]{2,1,0:T(8,128)(2,1)} %get-tuple-element.151), kind=kLoop, calls=%fused_computation | loop fusion | flops 16777216 | bytes 25165824 | tf_op jit(solution)/shard_map/convert_element_type | solution.py:450
  345.0 20.6 %attend_back.2 = (bf16[384,1024]{1,0:T(8,128)(2,1)}, bf16[1024,2048]{1,0:T(8,128)(2,1)}) custom-call(bf16[384,1024]{1,0:T(8,128)(2,1)} %multiply_convert_fusion.refs_0_, bf16[1024,2048]{1,0:T(8,128)(2,1)} %convolution_convert_fusion.1.refs_1_, bf16[384,1024]{1,0:T(8,128)(2,1)} %get-tuple-element.163.refs_2_.refs_0_, ...), custom_call_target="tpu_custom_call" | custom-call | flops 16106127360 | bytes 11534336 | tf_op jit(solution)/shard_map/attend_back/pallas_call | solution.py:144
  366.3 4.0 multiply_reduce_fusion.1
  375.9 7.1 %fusion = (f32[1024]{0:T(1024)}, f32[1024]{0:T(1024)}, f32[1024]{0:T(1024)}, f32[1024]{0:T(1024)}, bf16[1024,1024]{1,0:T(8,128)(2,1)}) fusion(f32[1024]{0:T(1024)S(1)} %bitcast.321, f32[1024]{0:T(1024)S(1)} %bitcast.327, f32[1024]{0:T(1024)S(1)} %bitcast.325, f32[1024]{0:T(1024)S(1)} %bitcast.323, bf16[1024,2048]{1,0:T(8,128)(2,1)S(1)} %copy-done.8, ...), kind=kOutput, calls=%fused_computation.9 | convolution fusion | flops 4313837568 | bytes 10518528 | tf_op jit(solution)/shard_map/dot_general | solution.py:26
  385.4 19.6 %weight_grads.1 = (bf16[16,192,1024]{2,1,0:T(8,128)(2,1)}, bf16[16,192,1024]{2,1,0:T(8,128)(2,1)}) custom-call(s32[1]{0:T(128)} %bitcast.8.core_ref, bf16[384,1024]{1,0:T(8,128)(2,1)} %get-tuple-element.163.refs_2_.refs_0_, bf16[384,1024]{1,0:T(8,128)(2,1)} %copy-done.10, bf16[384,1024]{1,0:T(8,128)(2,1)} %copy-done.9, ...), custom_call_target="tpu_custom_call" | custom-call | flops 1 | bytes 1 | tf_op jit(solution)/shard_map/weight_grads/pallas_call | solution.py:342
  410.0 5.6 collective-permute-done.27
  416.2 10.9 %add_convert_fusion.1 = bf16[16,192,1024]{2,1,0:T(8,128)(2,1)} fusion(bf16[16,192,1024]{2,1,0:T(8,128)(2,1)} %collective-permute-done.27, bf16[16,192,1024]{2,1,0:T(8,128)(2,1)} %get-tuple-element.184), kind=kLoop, calls=%fused_computation.1 | loop fusion | flops 12582912 | bytes 18874368 | tf_op jit(solution)/shard_map/convert_element_type | solution.py:450
  434.5 4.5 all-to-all-start
  439.0 30.0 %attend_back.3 = (bf16[1536,256]{1,0:T(8,128)(2,1)}, bf16[1536,512]{1,0:T(8,128)(2,1)}) custom-call(bf16[1536,256]{1,0:T(8,128)(2,1)} %multiply_convert_fusion.1.refs_0_, bf16[1536,512]{1,0:T(8,128)(2,1)} %slice.254.refs_1_, bf16[1536,256]{1,0:T(8,128)(2,1)} %get-tuple-element.135.refs_2_, bf16[1536,256]{1,0:T(8,128)(2,1)} %pad_maximum_fusion.11.refs_3_, ...), custom_call_target="tpu_custom_call" | custom-call | flops 24159191040 | bytes 6291456 | tf_op jit(solution)/shard_map/attend_back/pallas_call | solution.py:144
  476.0 3.3 convolution_convert_fusion.3
  487.9 15.0 %collective-permute-done.35 = bf16[128,768]{1,0:T(8,128)(2,1)S(1)} collective-permute-done((bf16[128,768]{1,0:T(8,128)(2,1)S(1)}, bf16[128,768]{1,0:T(8,128)(2,1)S(1)}, u32[]{:S(2)}, u32[]{:S(2)}) %collective-permute-start.35) | collective-permute-done | bytes 196640 | tf_op jit(solution)/shard_map/ppermute | solution.py:367
  503.0 5.6 collective-permute-done.34
  508.6 7.9 %collective-permute-done.33 = bf16[16,32,768]{2,1,0:T(8,128)(2,1)} collective-permute-done((bf16[16,32,768]{2,1,0:T(8,128)(2,1)S(1)}, bf16[16,32,768]{2,1,0:T(8,128)(2,1)}, u32[]{:S(2)}, u32[]{:S(2)}) %collective-permute-start.33) | collective-permute-done | bytes 786464 | tf_op jit(solution)/shard_map/ppermute | solution.py:367
  541.4 12.8 %collective-permute-done.37 = bf16[192,1024]{1,0:T(8,128)(2,1)} collective-permute-done((bf16[192,1024]{1,0:T(8,128)(2,1)}, bf16[192,1024]{1,0:T(8,128)(2,1)}, u32[]{:S(2)}, u32[]{:S(2)}) %collective-permute-start.37) | collective-permute-done | bytes 393248 | tf_op jit(solution)/shard_map/ppermute | solution.py:367
  563.3 4.6 all-to-all-start.1
  567.9 11.4 %collective-permute-done.39 = bf16[4,32,768]{2,1,0:T(8,128)(2,1)} collective-permute-done((bf16[4,32,768]{2,1,0:T(8,128)(2,1)}, bf16[4,32,768]{2,1,0:T(8,128)(2,1)}, u32[]{:S(2)}, u32[]{:S(2)}) %collective-permute-start.39) | collective-permute-done | bytes 196640 | tf_op jit(solution)/shard_map/ppermute | solution.py:367
  (508 shorter events, 179.7 us)
Async XLA Ops:
  7.2 233.1 %all-gather.3.cloned.1.call-start = ((), (), s32[]{:S(2)}) async-start(), calls=%async_computation.4 | async-start | bytes 30277632 | tf_op jit(solution)/shard_map/all_gather | solution.py:580
  11.0 417.0 %reduce-scatter.7.cloned.1.call-start = ((), (), s32[]{:S(2)}) async-start(), calls=%async_computation.5 | async-start | bytes 10485760
  23.0 37.4 %collective-permute-start.3 = (bf16[4,40,768]{2,0,1:T(4,128)(2,1)}, bf16[4,40,768]{2,0,1:T(4,128)(2,1)}, u32[]{:S(2)}, u32[]{:S(2)}) collective-permute-start(bf16[4,40,768]{2,0,1:T(4,128)(2,1)} %pad_maximum_fusion.15), channel_id=1, source_target_pairs={{0,4},{1,5},{2,6},{3,7},{4,0},{5,1},{6,2},{7,3},{8,12},{9,13},{10,... | collective-permute-start | bytes 737288 | tf_op jit(solution)/shard_map/ppermute | solution.py:367
  26.4 47.6 %collective-permute-start.6 = (bf16[192,1024]{1,0:T(8,128)(2,1)}, bf16[192,1024]{1,0:T(8,128)(2,1)}, u32[]{:S(2)}, u32[]{:S(2)}) collective-permute-start(bf16[192,1024]{1,0:T(8,128)(2,1)} %dynamic-slice_bitcast_fusion.4), channel_id=1, source_target_pairs={{0,4},{1,5},{2,6},{3,7},{4,0},{5,1},{6,2},{7,3},{8,12},{9,13},{10,... | collective-permute-start | bytes 1179656 | tf_op jit(solution)/shard_map/ppermute | solution.py:367
  69.2 19.3 %collective-permute-start.4 = (bf16[8,40,768]{2,0,1:T(8,128)(2,1)}, bf16[8,40,768]{2,0,1:T(8,128)(2,1)}, u32[]{:S(2)}, u32[]{:S(2)}) collective-permute-start(bf16[8,40,768]{2,0,1:T(8,128)(2,1)} %broadcast_select_fusion), channel_id=1, source_target_pairs={{0,8},{1,9},{2,10},{3,11},{4,12},{5,13},{6,14},{7,15},{8,0},{9,1},... | collective-permute-start | bytes 1474568 | tf_op jit(solution)/shard_map/ppermute | solution.py:367
  76.2 55.2 %collective-permute-start.8 = (bf16[384,1024]{1,0:T(8,128)(2,1)}, bf16[384,1024]{1,0:T(8,128)(2,1)}, u32[]{:S(2)}, u32[]{:S(2)}) collective-permute-start(bf16[384,1024]{1,0:T(8,128)(2,1)} %pad_maximum_fusion.5), channel_id=1, source_target_pairs={{0,2},{1,3},{2,0},{3,1},{4,6},{5,7},{6,4},{7,5},{8,10},{9,11},{10,... | collective-permute-start | bytes 2359304 | tf_op jit(solution)/shard_map/ppermute | solution.py:367
  76.3 57.5 %collective-permute-start.7 = (bf16[384,1024]{1,0:T(8,128)(2,1)}, bf16[384,1024]{1,0:T(8,128)(2,1)}, u32[]{:S(2)}, u32[]{:S(2)}) collective-permute-start(bf16[384,1024]{1,0:T(8,128)(2,1)} %pad_maximum_fusion.5), channel_id=1, source_target_pairs={{0,1},{1,0},{2,3},{3,2},{4,5},{5,4},{6,7},{7,6},{8,9},{9,8},{10,11... | collective-permute-start | bytes 2359304 | tf_op jit(solution)/shard_map/ppermute | solution.py:367
  91.2 45.1 %collective-permute-start.5 = (bf16[16,40,768]{2,0,1:T(8,128)(2,1)}, bf16[16,40,768]{2,0,1:T(8,128)(2,1)}, u32[]{:S(2)}, u32[]{:S(2)}) collective-permute-start(bf16[16,40,768]{2,0,1:T(8,128)(2,1)} %maximum_select_fusion.1), channel_id=1, source_target_pairs={{0,16},{1,17},{2,18},{3,19},{4,20},{5,21},{6,22},{7,23},{8,24},{9,... | collective-permute-start | bytes 2949128 | tf_op jit(solution)/shard_map/ppermute | solution.py:367
  136.9 31.6 %collective-permute-start.14 = (s32[128]{0:T(128)}, s32[128]{0:T(128)}, u32[]{:S(2)}, u32[]{:S(2)}) collective-permute-start(s32[128]{0:T(128)} %fusion.32), channel_id=1, source_target_pairs={{0,4},{1,5},{2,6},{3,7},{4,0},{5,1},{6,2},{7,3},{8,12},{9,13},{10,... | collective-permute-start | bytes 1544 | tf_op jit(solution)/shard_map/ppermute | solution.py:367
  137.6 31.6 %collective-permute-start.10 = (bf16[128,768]{1,0:T(8,128)(2,1)}, bf16[128,768]{1,0:T(8,128)(2,1)}, u32[]{:S(2)}, u32[]{:S(2)}) collective-permute-start(bf16[128,768]{1,0:T(8,128)(2,1)} %dynamic-slice_bitcast_fusion.14), channel_id=1, source_target_pairs={{0,4},{1,5},{2,6},{3,7},{4,0},{5,1},{6,2},{7,3},{8,12},{9,13},{10,... | collective-permute-start | bytes 589832 | tf_op jit(solution)/shard_map/ppermute | solution.py:367
  170.1 45.2 %collective-permute-start.12 = (bf16[256,768]{1,0:T(8,128)(2,1)S(1)}, bf16[256,768]{1,0:T(8,128)(2,1)S(1)}, u32[]{:S(2)}, u32[]{:S(2)}) collective-permute-start(bf16[256,768]{1,0:T(8,128)(2,1)S(1)} %pad_maximum_fusion.12), channel_id=1, source_target_pairs={{0,2},{1,3},{2,0},{3,1},{4,6},{5,7},{6,4},{7,5},{8,10},{9,11},{10,... | collective-permute-start | bytes 1179656 | tf_op jit(solution)/shard_map/ppermute | solution.py:367
  173.2 43.7 %collective-permute-start.11 = (bf16[256,768]{1,0:T(8,128)(2,1)S(1)}, bf16[256,768]{1,0:T(8,128)(2,1)S(1)}, u32[]{:S(2)}, u32[]{:S(2)}) collective-permute-start(bf16[256,768]{1,0:T(8,128)(2,1)S(1)} %pad_maximum_fusion.12), channel_id=1, source_target_pairs={{0,1},{1,0},{2,3},{3,2},{4,5},{5,4},{6,7},{7,6},{8,9},{9,8},{10,11... | collective-permute-start | bytes 1179656 | tf_op jit(solution)/shard_map/ppermute | solution.py:367
  249.0 10.9 %collective-permute-start.18 = (bf16[384,256]{1,0:T(8,128)(2,1)S(1)}, bf16[384,256]{1,0:T(8,128)(2,1)S(1)}, u32[]{:S(2)}, u32[]{:S(2)}) collective-permute-start(bf16[384,256]{1,0:T(8,128)(2,1)S(1)} %get-tuple-element.298), channel_id=1, source_target_pairs={{0,1},{1,0},{2,3},{3,2},{4,5},{5,4},{6,7},{7,6},{8,9},{9,8},{10,11... | collective-permute-start | bytes 589832 | tf_op jit(solution)/shard_map/ppermute | solution.py:367
  266.2 20.8 %collective-permute-start.21 = (bf16[192,1024]{1,0:T(8,128)(2,1)}, bf16[192,1024]{1,0:T(8,128)(2,1)S(1)}, u32[]{:S(2)}, u32[]{:S(2)}) collective-permute-start(bf16[192,1024]{1,0:T(8,128)(2,1)} %get-tuple-element.291), channel_id=1, source_target_pairs={{0,4},{1,5},{2,6},{3,7},{4,0},{5,1},{6,2},{7,3},{8,12},{9,13},{10,... | collective-permute-start | bytes 1179656 | tf_op jit(solution)/shard_map/ppermute | solution.py:367
  319.1 13.4 %collective-permute-start.22 = (bf16[16,256,1024]{2,1,0:T(8,128)(2,1)}, bf16[16,256,1024]{2,1,0:T(8,128)(2,1)S(1)}, u32[]{:S(2)}, u32[]{:S(2)}) collective-permute-start(bf16[16,256,1024]{2,1,0:T(8,128)(2,1)} %get-tuple-element.152), channel_id=1, source_target_pairs={{0,1},{1,0},{2,3},{3,2},{4,5},{5,4},{6,7},{7,6},{8,9},{9,8},{10,11... | collective-permute-start | bytes 25165832 | tf_op jit(solution)/shard_map/ppermute | solution.py:367
  341.6 183.4 %reduce-scatter.9.cloned.1.call-start = ((), (), s32[]{:S(2)}) async-start(), calls=%async_computation.6 | async-start | bytes 7864320
  344.6 21.0 %collective-permute-start.23 = (bf16[192,1024]{1,0:T(8,128)(2,1)S(1)}, bf16[192,1024]{1,0:T(8,128)(2,1)S(1)}, u32[]{:S(2)}, u32[]{:S(2)}) collective-permute-start(bf16[192,1024]{1,0:T(8,128)(2,1)S(1)} %get-tuple-element.285), channel_id=1, source_target_pairs={{0,4},{1,5},{2,6},{3,7},{4,0},{5,1},{6,2},{7,3},{8,12},{9,13},{10,... | collective-permute-start | bytes 1179656 | tf_op jit(solution)/shard_map/ppermute | solution.py:367
  383.0 22.0 %collective-permute-start.24 = (bf16[384,256]{1,0:T(8,128)(2,1)S(1)}, bf16[384,256]{1,0:T(8,128)(2,1)S(1)}, u32[]{:S(2)}, u32[]{:S(2)}) collective-permute-start(bf16[384,256]{1,0:T(8,128)(2,1)S(1)} %get-tuple-element.288), channel_id=1, source_target_pairs={{0,1},{1,0},{2,3},{3,2},{4,5},{5,4},{6,7},{7,6},{8,9},{9,8},{10,11... | collective-permute-start | bytes 589832 | tf_op jit(solution)/shard_map/ppermute | solution.py:367
  383.1 21.9 %collective-permute-start.25 = (bf16[384,256]{1,0:T(8,128)(2,1)S(1)}, bf16[384,256]{1,0:T(8,128)(2,1)S(1)}, u32[]{:S(2)}, u32[]{:S(2)}) collective-permute-start(bf16[384,256]{1,0:T(8,128)(2,1)S(1)} %get-tuple-element.287), channel_id=1, source_target_pairs={{0,2},{1,3},{2,0},{3,1},{4,6},{5,7},{6,4},{7,5},{8,10},{9,11},{10,... | collective-permute-start | bytes 589832 | tf_op jit(solution)/shard_map/ppermute | solution.py:367
  385.3 19.7 %collective-permute-start.26 = (bf16[384,256]{1,0:T(8,128)(2,1)S(1)}, bf16[384,256]{1,0:T(8,128)(2,1)S(1)}, u32[]{:S(2)}, u32[]{:S(2)}) collective-permute-start(bf16[384,256]{1,0:T(8,128)(2,1)S(1)} %get-tuple-element.286), channel_id=1, source_target_pairs={{0,3},{1,2},{2,1},{3,0},{4,7},{5,6},{6,5},{7,4},{8,11},{9,10},{10,... | collective-permute-start | bytes 589832 | tf_op jit(solution)/shard_map/ppermute | solution.py:367
  415.7 11.4 %collective-permute-start.28 = (bf16[256,768]{1,0:T(8,128)(2,1)S(1)}, bf16[256,768]{1,0:T(8,128)(2,1)S(1)}, u32[]{:S(2)}, u32[]{:S(2)}) collective-permute-start(bf16[256,768]{1,0:T(8,128)(2,1)S(1)} %get-tuple-element.182), channel_id=1, source_target_pairs={{0,1},{1,0},{2,3},{3,2},{4,5},{5,4},{6,7},{7,6},{8,9},{9,8},{10,11... | collective-permute-start | bytes 1179656 | tf_op jit(solution)/shard_map/ppermute | solution.py:367
  415.8 12.0 %collective-permute-start.29 = (bf16[256,768]{1,0:T(8,128)(2,1)S(1)}, bf16[256,768]{1,0:T(8,128)(2,1)}, u32[]{:S(2)}, u32[]{:S(2)}) collective-permute-start(bf16[256,768]{1,0:T(8,128)(2,1)S(1)} %get-tuple-element.183), channel_id=1, source_target_pairs={{0,1},{1,0},{2,3},{3,2},{4,5},{5,4},{6,7},{7,6},{8,9},{9,8},{10,11... | collective-permute-start | bytes 1179656 | tf_op jit(solution)/shard_map/ppermute | solution.py:367
  433.0 36.0 %collective-permute-start.30 = (bf16[256,768]{1,0:T(8,128)(2,1)}, bf16[256,768]{1,0:T(8,128)(2,1)}, u32[]{:S(2)}, u32[]{:S(2)}) collective-permute-start(bf16[256,768]{1,0:T(8,128)(2,1)} %add_convert_fusion.10), channel_id=1, source_target_pairs={{0,2},{1,3},{2,0},{3,1},{4,6},{5,7},{6,4},{7,5},{8,10},{9,11},{10,... | collective-permute-start | bytes 1179656 | tf_op jit(solution)/shard_map/ppermute | solution.py:367
  434.5 90.5 %all-to-all-start = ((bf16[4,256,1024]{2,1,0:T(8,128)(2,1)}), bf16[4,256,1024]{2,1,0:T(8,128)(2,1)}, u32[]{:S(2)}, u32[]{:S(2)}) async-start(bf16[4,256,1024]{2,1,0:T(8,128)(2,1)} %bitcast.259), calls=%async_computation | async-start | bytes 4194304 | tf_op jit(solution)/shard_map/all_to_all | solution.py:419
  479.7 28.9 %collective-permute-start.34 = (bf16[384,1024]{1,0:T(8,128)(2,1)S(1)}, bf16[384,1024]{1,0:T(8,128)(2,1)S(1)}, u32[]{:S(2)}, u32[]{:S(2)}) collective-permute-start(bf16[384,1024]{1,0:T(8,128)(2,1)S(1)} %add_convert_fusion.5), channel_id=1, source_target_pairs={{0,2},{1,3},{2,0},{3,1},{4,6},{5,7},{6,4},{7,5},{8,10},{9,11},{10,... | collective-permute-start | bytes 2359304 | tf_op jit(solution)/shard_map/ppermute | solution.py:367
  481.9 34.6 %collective-permute-start.33 = (bf16[16,32,768]{2,1,0:T(8,128)(2,1)S(1)}, bf16[16,32,768]{2,1,0:T(8,128)(2,1)}, u32[]{:S(2)}, u32[]{:S(2)}) collective-permute-start(bf16[16,32,768]{2,1,0:T(8,128)(2,1)S(1)} %get-tuple-element.272), channel_id=1, source_target_pairs={{0,16},{1,17},{2,18},{3,19},{4,20},{5,21},{6,22},{7,23},{8,24},{9,... | collective-permute-start | bytes 2359304 | tf_op jit(solution)/shard_map/ppermute | solution.py:367
  485.5 17.5 %collective-permute-start.35 = (bf16[128,768]{1,0:T(8,128)(2,1)S(1)}, bf16[128,768]{1,0:T(8,128)(2,1)S(1)}, u32[]{:S(2)}, u32[]{:S(2)}) collective-permute-start(bf16[128,768]{1,0:T(8,128)(2,1)S(1)} %get-tuple-element.309), channel_id=1, source_target_pairs={{0,4},{1,5},{2,6},{3,7},{4,0},{5,1},{6,2},{7,3},{8,12},{9,13},{10,... | collective-permute-start | bytes 589832 | tf_op jit(solution)/shard_map/ppermute | solution.py:367
  527.3 27.9 %collective-permute-start.38 = (bf16[2,192,1024]{2,1,0:T(8,128)(2,1)}, bf16[2,192,1024]{2,1,0:T(8,128)(2,1)}, u32[]{:S(2)}, u32[]{:S(2)}) collective-permute-start(bf16[2,192,1024]{2,1,0:T(8,128)(2,1)} %dynamic-slice_bitcast_fusion), channel_id=1, source_target_pairs={{0,2},{1,3},{2,0},{3,1},{4,6},{5,7},{6,4},{7,5},{8,10},{9,11},{10,... | collective-permute-start | bytes 2359304 | tf_op jit(solution)/shard_map/ppermute | solution.py:367
  532.9 21.3 %collective-permute-start.37 = (bf16[192,1024]{1,0:T(8,128)(2,1)}, bf16[192,1024]{1,0:T(8,128)(2,1)}, u32[]{:S(2)}, u32[]{:S(2)}) collective-permute-start(bf16[192,1024]{1,0:T(8,128)(2,1)} %get-tuple-element.283), channel_id=1, source_target_pairs={{0,4},{1,5},{2,6},{3,7},{4,0},{5,1},{6,2},{7,3},{8,12},{9,13},{10,... | collective-permute-start | bytes 1179656 | tf_op jit(solution)/shard_map/ppermute | solution.py:367
  556.8 22.5 %collective-permute-start.39 = (bf16[4,32,768]{2,1,0:T(8,128)(2,1)}, bf16[4,32,768]{2,1,0:T(8,128)(2,1)}, u32[]{:S(2)}, u32[]{:S(2)}) collective-permute-start(bf16[4,32,768]{2,1,0:T(8,128)(2,1)} %fusion.21), channel_id=1, source_target_pairs={{0,4},{1,5},{2,6},{3,7},{4,0},{5,1},{6,2},{7,3},{8,12},{9,13},{10,... | collective-permute-start | bytes 589832 | tf_op jit(solution)/shard_map/ppermute | solution.py:367
  562.1 26.0 %collective-permute-start.43 = (bf16[1,192,1024]{2,1,0:T(8,128)(2,1)S(1)}, bf16[1,192,1024]{2,1,0:T(8,128)(2,1)}, u32[]{:S(2)}, u32[]{:S(2)}) collective-permute-start(bf16[1,192,1024]{2,1,0:T(8,128)(2,1)S(1)} %fusion.18), channel_id=1, source_target_pairs={{0,4},{1,5},{2,6},{3,7},{4,0},{5,1},{6,2},{7,3},{8,12},{9,13},{10,... | collective-permute-start | bytes 1179656 | tf_op jit(solution)/shard_map/ppermute | solution.py:367
  563.3 24.1 %all-to-all-start.1 = ((bf16[32,2,768]{2,1,0:T(2,128)(2,1)}), bf16[32,2,768]{2,1,0:T(2,128)(2,1)S(1)}, u32[]{:S(2)}, u32[]{:S(2)}) async-start(bf16[32,2,768]{2,1,0:T(2,128)(2,1)} %reshape.474), calls=%async_computation.1 | async-start | bytes 196608 | tf_op jit(solution)/shard_map/all_to_all | solution.py:773
  (115 other events, 892.6 us)
Sparse Core Ops, SparseCore 0:
  11.1 224.4 all-gather.2
  341.8 86.1 reduce-scatter.6
  431.2 85.1 reduce-scatter.8
